TPU v7x, 32 devices: a whole 2x2x4 slice. The times are simulated.
32 devices in a mesh: space: 16 (over z, y, core), event: 2 (over x).
Axes of the slice: x: 2, y: 2, z: 4, core: 2. Of those that a mesh axis runs over, the one named last changes fastest.
Arguments:
- fwd_now: float32 [4, 64, 16384], P('event', None, 'space'), as said below
- fwd_prev: float32 [4, 64, 16384], P('event', None, 'space'), as said below
- adj_now: float32 [4, 64, 16384], P('event', None, 'space'), as said below
- adj_prev: float32 [4, 64, 16384], P('event', None, 'space'), as said below
- shear_mod: float32 [64, 16384], P(None, 'space'), may hold values from 0.5 to 2
- density: float32 [16384], P('space'), may hold values from 0.5 to 2
- station_owner: int32 [32768, 1], P('space'), may hold values from 0 to 15; in each aligned block of 2048 rows (0 to 2047, 2048 to 4095, ...) at most 256 rows name the same one
- receiver_local: int32 [32768], P('space'), may hold values from 0 to 1023
- station_weights: float32 [64, 32768], P(None, 'space'), may hold values from -6 to 6
- adj_records: float32 [4, 2, 32768], P('event', None, 'space'), may hold values from -6 to 6
Outputs:
- fwd_last: float32 [4, 64, 16384], P('event', None, 'space')
- fwd_before: float32 [4, 64, 16384], P('event', None, 'space')
- adj_last: float32 [4, 64, 16384], P('event', None, 'space')
- adj_before: float32 [4, 64, 16384], P('event', None, 'space')
- kernel: float32 [64, 16384], P(None, ('space', 'event'))
Inputs may be any that keep to these rules, and one draw needn't show every extreme that they name: `station_owner`: the 2048 stations of one index of space name at most 256 with the same owner. `fwd_now`: each displacement is continuous: element-local copies of a shared node hold equal values. `fwd_prev`: continuous like fwd_now. `adj_now`: continuous like fwd_now. `adj_prev`: continuous like fwd_now.
All inputs are finite; a program needn't handle non-finite values.
Results may differ from a plain program's by a relative error of at most 0.0001.
Values sent between devices are 32-bit elements; how exact they have to be, the bound alone decides.
No kernel may reach another device: no remote copies, remote signals or barrier semaphores. Data moves between devices by JAX's collectives and lax.ppermute only.
A program may use at most 64 MiB of HBM per device.

v0:
```python
import jax
import jax.numpy as jnp
import numpy as np
from jax import lax
from jax.sharding import PartitionSpec as P

EX = 16
EY = 16
STEPS = 2
CAP = 256


TIME_STEP = 0.08
STEP_SQUARE = 0.0064


def padded(cells, sides, width):
    for axis, dim in sides:
        count = lax.axis_size(axis)
        ends = count - 1
        head = lax.slice_in_dim(cells, 0, width, axis=dim)
        tail = lax.slice_in_dim(cells, cells.shape[dim] - width, cells.shape[dim], axis=dim)
        cells = jnp.concatenate(
            [
                lax.ppermute(tail, axis, [(i, (i + 1) % count) for i in range(ends)]),
                cells,
                lax.ppermute(head, axis, [((i + 1) % count, i) for i in range(ends)]),
            ],
            axis=dim,
        )
    return cells


def element_tables():
    root = 1.0 / np.sqrt(5.0)
    points = np.array([-1.0, -root, root, 1.0])
    weights = np.array([1.0 / 6.0, 5.0 / 6.0, 5.0 / 6.0, 1.0 / 6.0])
    derivative = np.zeros((4, 4))
    for i in range(4):
        for j in range(4):
            if i == j:
                derivative[i, i] = sum((1.0 / (points[i] - points[k]) for k in range(4) if k != i))
            else:
                upper = 1.0
                for k in range(4):
                    if k != i and k != j:
                        upper = upper * (points[i] - points[k])
                lower = 1.0
                for k in range(4):
                    if k != j:
                        lower = lower * (points[j] - points[k])
                derivative[i, j] = upper / lower
    identity = np.eye(4)
    grad_a = np.kron(np.eye(16), derivative)
    grad_b = np.kron(identity, np.kron(derivative, identity))
    grad_c = np.kron(derivative, np.eye(16))
    weight3 = np.kron(weights, np.kron(weights, weights))
    return (
        jnp.asarray(np.stack([grad_a, grad_b, grad_c]), jnp.float32),
        jnp.asarray(weight3, jnp.float32),
    )


def shifted(values, offset, keep):
    filler = jnp.zeros_like(values[..., : abs(offset)])
    if offset > 0:
        moved = jnp.concatenate([values[..., offset:], filler], axis=-1)
    else:
        moved = jnp.concatenate([filler, values[..., :offset]], axis=-1)
    return jnp.where(keep, moved, jnp.zeros_like(moved))


def assemble_axis(grid, axis, stride, first, last):
    low = jnp.take(grid, 0, axis=axis)
    high = jnp.take(grid, 3, axis=axis)
    new_low = low + shifted(high, -stride, jnp.logical_not(first))
    new_high = high + shifted(low, stride, jnp.logical_not(last))
    middle = lax.slice_in_dim(grid, 1, 3, axis=axis)
    return jnp.concatenate(
        [jnp.expand_dims(new_low, axis), middle, jnp.expand_dims(new_high, axis)], axis=axis
    )


def assemble(field):
    count = field.shape[0]
    elements = field.shape[-1]
    cells = EX * EY
    depth = elements // cells
    element = jnp.arange(elements, dtype=jnp.int32)
    col_x = element % EX
    col_y = element // EX % EY
    col_z = element // cells
    grid = field.reshape(count, 4, 4, 4, elements)
    grid = assemble_axis(grid, 3, 1, col_x == 0, col_x == EX - 1)
    grid = assemble_axis(grid, 2, EX, col_y == 0, col_y == EY - 1)
    low = grid[:, 0]
    high = grid[:, 3]
    new_low = low + shifted(high, -cells, col_z != 0)
    new_high = high + shifted(low, cells, col_z != depth - 1)
    faces = jnp.stack([low[..., :cells], high[..., elements - cells :]], axis=0)
    rim = padded(faces, (("space", 0),), 1)
    filler = jnp.zeros(low.shape[:-1] + (elements - cells,), jnp.float32)
    new_low = new_low + jnp.concatenate([rim[0], filler], axis=-1)
    new_high = new_high + jnp.concatenate([filler, rim[3]], axis=-1)
    grid = jnp.concatenate([new_low[:, None], grid[:, 1:3], new_high[:, None]], axis=1)
    return grid.reshape(count, 64, elements)


def shards(
    fwd_now,
    fwd_prev,
    adj_now,
    adj_prev,
    shear_mod,
    density,
    station_owner,
    receiver_local,
    station_weights,
    adj_records,
):
    grad_ops, weight3 = element_tables()
    high = lax.Precision.HIGHEST
    events = fwd_now.shape[0]
    elements = fwd_now.shape[-1]
    stations = station_owner.shape[0]
    slabs = lax.axis_size("space")
    slots = slabs * CAP
    target = station_owner[:, 0]
    order = jnp.arange(stations, dtype=jnp.int32)
    same_owner = target[:, None] == target[None, :]
    earlier = order[None, :] < order[:, None]
    rank = jnp.sum(jnp.logical_and(same_owner, earlier).astype(jnp.int32), axis=1)
    position = target * CAP + rank
    placing = (position[:, None] == jnp.arange(slots, dtype=jnp.int32)[None, :]).astype(jnp.float32)
    rows_out = jnp.concatenate(
        [
            station_weights,
            adj_records.reshape(events * STEPS, stations),
            receiver_local[None, :].astype(jnp.float32),
        ],
        axis=0,
    )
    placed = jnp.dot(rows_out, placing, precision=high, preferred_element_type=jnp.float32)
    send_weights = placed[:64]
    send_records = placed[64 : 64 + events * STEPS]
    send_ids = placed[64 + events * STEPS :].astype(jnp.int32)
    got_weights, got_records, got_ids = (
        lax.all_to_all(send_weights, "space", split_axis=1, concat_axis=1, tiled=True),
        lax.all_to_all(send_records, "space", split_axis=1, concat_axis=1, tiled=True),
        lax.all_to_all(send_ids, "space", split_axis=1, concat_axis=1, tiled=True),
    )
    contrib = (got_records.reshape(events * STEPS, 1, slots) * got_weights[None]).reshape(
        events * STEPS * 64, slots
    )
    landing = (got_ids[0][:, None] == jnp.arange(elements, dtype=jnp.int32)[None, :]).astype(
        jnp.float32
    )
    source = jnp.dot(contrib, landing, precision=high, preferred_element_type=jnp.float32).reshape(
        events, STEPS, 64, elements
    )
    stiff = weight3[:, None] * shear_mod
    mass = assemble((weight3[:, None] * density[None, :])[None])[0]
    now = jnp.concatenate([fwd_now, adj_now], axis=0)
    before = jnp.concatenate([fwd_prev, adj_prev], axis=0)
    kern = jnp.zeros((64, elements), jnp.float32)
    for step in range(STEPS):
        grads = jnp.einsum("dnm,fme->dfne", grad_ops, now, precision=high)
        kern = kern - TIME_STEP * stiff * jnp.sum(
            grads[:, :events] * grads[:, events:], axis=(0, 1)
        )
        local = jnp.einsum("dnm,dfne->fme", grad_ops, grads * stiff[None, None], precision=high)
        local = local - jnp.concatenate([jnp.zeros_like(source[:, step]), source[:, step]], axis=0)
        after = 2.0 * now - before - STEP_SQUARE * assemble(local) / mass[None]
        before = now
        now = after
    total = lax.psum(kern, "event")
    width = elements // lax.axis_size("event")
    kernel = lax.dynamic_slice_in_dim(total, lax.axis_index("event") * width, width, 1)
    return (now[:events], before[:events], now[events:], before[events:], kernel)


def solution(mesh):
    in_specs = (
        P("event", None, "space"),
        P("event", None, "space"),
        P("event", None, "space"),
        P("event", None, "space"),
        P(None, "space"),
        P("space"),
        P("space", None),
        P("space"),
        P(None, "space"),
        P("event", None, "space"),
    )
    out_specs = (
        P("event", None, "space"),
        P("event", None, "space"),
        P("event", None, "space"),
        P("event", None, "space"),
        P(None, ("space", "event")),
    )
    return jax.shard_map(shards, mesh=mesh, in_specs=in_specs, out_specs=out_specs, check_vma=False)
```

profile of v0, /device:TPU:0, one launch (start us, length us, event | category | flops | bytes accessed | tf_op | source)
XLA Modules:
  0.0 175.4 jit_solution(14018336934634820469)
XLA Ops:
  7.3 0.9 broadcast_multiply_fusion
  9.2 0.7 copy-done.8
  9.9 0.6 copy-done.21
  10.5 0.6 slice_bitcast_fusion.12
  11.1 1.3 collective-permute-start.3
  12.4 4.6 %convert_reduce_fusion = s32[2048]{0:T(1024)S(1)} fusion(s32[2048]{0:T(1024)S(1)} %bitcast.212), kind=kLoop, calls=%fused_computation.4 | loop fusion | flops 20969472 | bytes 16384 | tf_op jit(solution)/shard_map/reduce_sum | solution.py:132
  17.2 12.6 %fusion = f32[69,4096]{1,0:T(8,128)S(1)} fusion(s32[2048]{0:T(1024)S(1)} %bitcast.213, f32[1,2048]{1,0:T(1,128)S(1)} %bitcast.215, f32[4,2048]{1,0:T(4,128)S(1)} %reshape.80, f32[64,2048]{1,0:T(8,128)S(1)} %copy-done.42), kind=kOutput, calls=%fused_computation.1 | convolution fusion | flops 6954438656 | bytes 1703936 | tf_op jit(solution)/shard_map/dot_general | solution.py:143
  29.8 0.7 slice.336
  30.5 8.7 %all-to-all-start = ((f32[4,16,256]{2,0,1:T(4,128)}), f32[4,16,256]{2,0,1:T(4,128)S(1)}, u32[]{:S(2)}, u32[]{:S(2)}) async-start(f32[4,16,256]{2,0,1:T(4,128)} %bitcast.12), calls=%async_computation | async-start | bytes 131072 | tf_op jit(solution)/shard_map/all_to_all | solution.py:149
  39.2 0.6 slice_bitcast_fusion.13
  39.8 3.0 %collective-permute-start.2 = (f32[1,1,4,4,256]{4,3,2,1,0:T(4,128)}, f32[1,1,4,4,256]{4,3,2,1,0:T(4,128)}, u32[]{:S(2)}, u32[]{:S(2)}) collective-permute-start(f32[1,1,4,4,256]{4,3,2,1,0:T(4,128)} %slice_bitcast_fusion.13), channel_id=1, source_target_pairs={{0,2},{2,4},{4,6},{6,8},{8,10},{10,12},{12,14},{14,16},{16,18},{18... | collective-permute-start | bytes 49160 | tf_op jit(solution)/shard_map/ppermute | solution.py:25
  42.9 1.1 copy.246
  44.0 2.1 %all-to-all-done = f32[4,16,256]{2,0,1:T(4,128)S(1)} async-done(((f32[4,16,256]{2,0,1:T(4,128)}), f32[4,16,256]{2,0,1:T(4,128)S(1)}, u32[]{:S(2)}, u32[]{:S(2)}) %all-to-all-start) | async-done | bytes 65568 | tf_op jit(solution)/shard_map/all_to_all | solution.py:149
  46.1 4.8 %all-to-all-start.1 = ((f32[64,16,256]{2,0,1:T(8,128)}), f32[64,16,256]{2,0,1:T(8,128)}, u32[]{:S(2)}, u32[]{:S(2)}) async-start(f32[64,16,256]{2,0,1:T(8,128)} %bitcast.183), calls=%async_computation.1 | async-start | bytes 2097152 | tf_op jit(solution)/shard_map/all_to_all | solution.py:148
  51.0 1.0 copy-done
  52.0 3.5 %convolution_bitcast_fusion.1 = f32[3,4,64,1024]{3,2,0,1:T(8,128)S(1)} fusion(f32[3,64,64,1]{2,1,0,3:T(8,128)S(1)} %copy-done.10, f32[4,64,1024]{2,1,0:T(8,128)S(1)} %constant_dynamic-update-slice_fusion), kind=kOutput, calls=%fused_computation.18 | convolution fusion | flops 603979776 | bytes 4243456 | tf_op jit(solution)/shard_map/dnm,fme->dfne/dot_general | solution.py:167
  55.5 1.0 fusion.15
  56.6 1.5 slice_convert_fusion
  58.1 0.6 fusion.51
  58.7 0.6 slice.366
  59.4 14.4 %all-to-all-done.1 = f32[64,16,256]{2,0,1:T(8,128)} async-done(((f32[64,16,256]{2,0,1:T(8,128)}), f32[64,16,256]{2,0,1:T(8,128)}, u32[]{:S(2)}, u32[]{:S(2)}) %all-to-all-start.1) | async-done | bytes 1048608 | tf_op jit(solution)/shard_map/all_to_all | solution.py:148
  73.7 6.9 %all-to-all-start.2 = ((s32[1,16,256]{2,0,1:T(1,128)}), s32[1,16,256]{2,0,1:T(1,128)}, u32[]{:S(2)}, u32[]{:S(2)}) async-start(s32[1,16,256]{2,0,1:T(1,128)} %bitcast.211), calls=%async_computation.2 | async-start | bytes 32768 | tf_op jit(solution)/shard_map/all_to_all | solution.py:150
  80.7 1.6 add_bitcast_fusion.12
  82.3 1.5 copy.126
  83.8 1.5 mul.114
  85.3 2.4 %copy.209 = f32[16,8,8,256]{3,2,0,1:T(8,128)} copy(f32[16,8,8,256]{3,2,1,0:T(8,128)} %bitcast.89) | data formatting | bytes 2097152 | tf_op jit(solution)/shard_map/mul | solution.py:152
  87.6 9.7 %fusion.4 = f32[2,2,64,1024]{3,2,1,0:T(8,128)S(1)} fusion(s32[4096]{0:T(1024)} %bitcast.14, f32[64,4096]{1,0:T(8,128)} %bitcast.199, f32[2,2,4096]{2,1,0:T(2,128)} %mul.114), kind=kOutput, calls=%fused_computation.8 | convolution fusion | flops 12890144768 | bytes 2179072 | tf_op jit(solution)/shard_map/dot_general | solution.py:158
  97.4 0.9 slice_bitcast_fusion
  98.2 3.4 %fusion.27 = f32[4,64,1024]{2,1,0:T(8,128)} fusion(f32[3,64,64,1]{2,1,0,3:T(8,128)S(1)} %copy-done.10, f32[3,4,64,1024]{3,2,0,1:T(8,128)S(1)} %convolution_bitcast_fusion.1, f32[64,1024]{1,0:T(8,128)S(1)} %broadcast_multiply_fusion.1, f32[2,64,1024]{2,1,0:T(8,128)S(1)} %get-tuple-element.116), kind=kOutput, calls=%fused_computation.30 | convolution fusion | flops 605028352 | bytes 5029888 | tf_op jit(solution)/shard_map/dnm,dfne->fme/dot_general | solution.py:171
  101.6 1.5 reshape.81
  103.2 0.6 fusion.65
  103.7 0.5 copy_bitcast_fusion.3
  105.8 0.3 add_bitcast_fusion.8
  106.4 0.5 fusion.33
  107.0 1.3 collective-permute-start.1
  108.3 3.0 %collective-permute-start = (f32[1,4,4,4,256]{4,3,1,2,0:T(4,128)S(1)}, f32[1,4,4,4,256]{4,3,1,2,0:T(4,128)S(1)}, u32[]{:S(2)}, u32[]{:S(2)}) collective-permute-start(f32[1,4,4,4,256]{4,3,1,2,0:T(4,128)S(1)} %slice_bitcast_fusion.11), channel_id=1, source_target_pairs={{0,2},{2,4},{4,6},{6,8},{8,10},{10,12},{12,14},{14,16},{16,18},{18... | collective-permute-start | bytes 196616 | tf_op jit(solution)/shard_map/ppermute | solution.py:25
  111.4 0.8 div.62
  112.6 0.4 copy_multiply_fusion
  113.0 0.4 mul.120
  113.5 1.6 fusion.34
  115.1 1.0 fusion.61
  116.2 3.5 %convolution_bitcast_fusion = f32[3,4,64,1024]{3,2,0,1:T(8,128)S(1)} fusion(f32[3,64,64,1]{2,1,0,3:T(8,128)S(1)} %copy-done.10, f32[4,64,1024]{2,1,0:T(8,128)S(1)} %fusion.34), kind=kOutput, calls=%fused_computation.17 | convolution fusion | flops 603979776 | bytes 4243456 | tf_op jit(solution)/shard_map/dnm,fme->dfne/dot_general | solution.py:167
  119.7 1.0 fusion.14
  120.7 3.4 %fusion.24 = f32[4,64,1024]{2,1,0:T(8,128)} fusion(f32[3,64,64,1]{2,1,0,3:T(8,128)S(1)} %copy-done.10, f32[3,4,64,1024]{3,2,0,1:T(8,128)S(1)} %convolution_bitcast_fusion, f32[64,1024]{1,0:T(8,128)S(1)} %broadcast_multiply_fusion.1, f32[2,64,1024]{2,1,0:T(8,128)S(1)} %copy-done.7), kind=kOutput, calls=%fused_computation.29 | convolution fusion | flops 605028352 | bytes 5029888 | tf_op jit(solution)/shard_map/dnm,dfne->fme/dot_general | solution.py:171
  124.1 1.5 reshape.82
  125.7 0.6 fusion.64
  128.6 0.5 fusion.31
  129.1 1.0 copy-done.2
  130.2 0.7 copy-done.5
  131.0 3.6 %collective-permute-start.4 = (f32[1,4,4,4,256]{4,3,2,1,0:T(4,128)S(1)}, f32[1,4,4,4,256]{4,3,2,1,0:T(4,128)S(1)}, u32[]{:S(2)}, u32[]{:S(2)}) collective-permute-start(f32[1,4,4,4,256]{4,3,2,1,0:T(4,128)S(1)} %slice_bitcast_fusion.5), channel_id=1, source_target_pairs={{0,2},{2,4},{4,6},{6,8},{8,10},{10,12},{12,14},{14,16},{16,18},{18... | collective-permute-start | bytes 196616 | tf_op jit(solution)/shard_map/ppermute | solution.py:25
  134.6 0.8 multiply_subtract_fusion
  135.5 0.6 slice_bitcast_fusion.4
  136.1 1.6 slice.378
  137.7 1.7 slice.381
  139.5 1.3 collective-permute-start.5
  140.8 1.1 add_bitcast_fusion.1
  141.9 2.8 %collective-permute-done.5 = f32[1,4,4,4,256]{4,3,2,1,0:T(4,128)S(1)} collective-permute-done((f32[1,4,4,4,256]{4,3,2,1,0:T(4,128)}, f32[1,4,4,4,256]{4,3,2,1,0:T(4,128)S(1)}, u32[]{:S(2)}, u32[]{:S(2)}) %collective-permute-start.5) | collective-permute-done | bytes 65568 | tf_op jit(solution)/shard_map/ppermute | solution.py:27
  144.7 1.1 add_bitcast_fusion
  145.8 1.4 maximum_multiply_fusion
  147.2 1.6 mul.128
  148.8 0.3 divide_subtract_fusion
  149.2 1.0 fusion.62
  150.2 16.6 %all-reduce.28.cloned.1.call-done = f32[64,1024]{1,0:T(8,128)} async-done(((f32[64,1024]{1,0:T(8,128)}), f32[64,1024]{1,0:T(8,128)}) %all-reduce.28.cloned.1.call-update) | async-done | bytes 262160 | tf_op jit(solution)/shard_map/psum | solution.py:176
  166.8 1.6 constant_dynamic-slice_fusion
  (144 shorter events, 6.1 us)
Async XLA Ops:
  7.2 5.2 %copy-start.39 = (s32[2048]{0:T(1024)S(1)}, s32[2048]{0:T(1024)}, u32[]{:S(2)}) copy-start(s32[2048]{0:T(1024)} %param.35) | copy-start | bytes 24580
  7.2 5.2 %copy-start.38 = (s32[2048,1]{0,1:T(1,128)S(1)}, s32[2048,1]{0,1:T(1,128)}, u32[]{:S(2)}) copy-start(s32[2048,1]{0,1:T(1,128)} %param.34) | copy-start | bytes 24580
  7.2 9.9 %copy-start.27 = (f32[2,2,2048]{2,1,0:T(2,128)S(1)}, f32[2,2,2048]{2,1,0:T(2,128)}, u32[]{:S(2)}) copy-start(f32[2,2,2048]{2,1,0:T(2,128)} %param.37) | copy-start | bytes 98308
  7.2 10.0 %copy-start.42 = (f32[64,2048]{1,0:T(8,128)S(1)}, f32[64,2048]{1,0:T(8,128)}, u32[]{:S(2)}) copy-start(f32[64,2048]{1,0:T(8,128)} %param.36) | copy-start | bytes 1572868
  7.2 1.8 %copy-start.36 = (pred[1024]{0:T(1024)(128)(4,1)}, pred[1024]{0:T(1024)(128)(4,1)S(1)}, u32[]{:S(2)}) copy-start(pred[1024]{0:T(1024)(128)(4,1)S(1)} %compare_not_fusion.1) | copy-start | bytes 3076
  7.2 1.7 copy-start.34
  7.3 1.7 copy-start.28
  7.3 1.7 copy-start.30
  9.2 0.7 copy-start.8
  9.9 0.6 copy-start.21
  9.9 29.3 %copy-start.23 = (f32[1,4,4,1024]{3,2,1,0:T(4,128)}, f32[1,4,4,1024]{3,2,1,0:T(4,128)S(1)}, u32[]{:S(2)}) copy-start(f32[1,4,4,1024]{3,2,1,0:T(4,128)S(1)} %get-tuple-element.125) | copy-start | bytes 196612
  11.1 69.6 %collective-permute-start.3 = (f32[1,1,4,4,256]{4,3,2,1,0:T(4,128)}, f32[1,1,4,4,256]{4,3,2,1,0:T(4,128)}, u32[]{:S(2)}, u32[]{:S(2)}) collective-permute-start(f32[1,1,4,4,256]{4,3,2,1,0:T(4,128)} %slice_bitcast_fusion.12), channel_id=1, source_target_pairs={{2,0},{4,2},{6,4},{8,6},{10,8},{12,10},{14,12},{16,14},{18,16},{20... | collective-permute-start | bytes 49160 | tf_op jit(solution)/shard_map/ppermute | solution.py:27
  29.8 16.3 %copy-start.11 = (f32[69,4096]{1,0:T(8,128)}, f32[69,4096]{1,0:T(8,128)S(1)}, u32[]{:S(2)}) copy-start(f32[69,4096]{1,0:T(8,128)S(1)} %fusion) | copy-start | bytes 3391492
  30.5 15.6 %all-to-all-start = ((f32[4,16,256]{2,0,1:T(4,128)}), f32[4,16,256]{2,0,1:T(4,128)S(1)}, u32[]{:S(2)}, u32[]{:S(2)}) async-start(f32[4,16,256]{2,0,1:T(4,128)} %bitcast.12), calls=%async_computation | async-start | bytes 131072 | tf_op jit(solution)/shard_map/all_to_all | solution.py:149
  39.8 11.0 %copy-start.18 = (f32[2,64,1024]{2,1,0:T(8,128)S(1)}, f32[2,64,1024]{2,1,0:T(8,128)}, u32[]{:S(2)}) copy-start(f32[2,64,1024]{2,1,0:T(8,128)} %param.28) | copy-start | bytes 1572868
  39.8 40.9 %collective-permute-start.2 = (f32[1,1,4,4,256]{4,3,2,1,0:T(4,128)}, f32[1,1,4,4,256]{4,3,2,1,0:T(4,128)}, u32[]{:S(2)}, u32[]{:S(2)}) collective-permute-start(f32[1,1,4,4,256]{4,3,2,1,0:T(4,128)} %slice_bitcast_fusion.13), channel_id=1, source_target_pairs={{0,2},{2,4},{4,6},{6,8},{8,10},{10,12},{12,14},{14,16},{16,18},{18... | collective-permute-start | bytes 49160 | tf_op jit(solution)/shard_map/ppermute | solution.py:25
  42.9 8.0 %copy-start.19 = (f32[2,64,1024]{2,1,0:T(8,128)S(1)}, f32[2,64,1024]{2,1,0:T(8,128)}, u32[]{:S(2)}) copy-start(f32[2,64,1024]{2,1,0:T(8,128)} %param.30) | copy-start | bytes 1572868
  42.9 9.0 %copy-start.10 = (f32[3,64,64,1]{2,1,0,3:T(8,128)S(1)}, f32[3,64,64,1]{2,1,0,3:T(8,128)}, u32[]{:S(2)}) copy-start(f32[3,64,64,1]{2,1,0,3:T(8,128)} %constant.460) | copy-start | bytes 147460
  46.0 4.8 %copy-start.20 = (f32[4,16,256]{2,0,1:T(4,128)}, f32[4,16,256]{2,0,1:T(4,128)S(1)}, u32[]{:S(2)}) copy-start(f32[4,16,256]{2,0,1:T(4,128)S(1)} %all-to-all-done) | copy-start | bytes 196612
  46.1 27.7 %all-to-all-start.1 = ((f32[64,16,256]{2,0,1:T(8,128)}), f32[64,16,256]{2,0,1:T(8,128)}, u32[]{:S(2)}, u32[]{:S(2)}) async-start(f32[64,16,256]{2,0,1:T(8,128)} %bitcast.183), calls=%async_computation.1 | async-start | bytes 2097152 | tf_op jit(solution)/shard_map/all_to_all | solution.py:148
  50.9 1.0 copy-start
  51.9 4.6 %copy-start.14 = (f32[64,1024]{1,0:T(8,128)S(1)}, f32[64,1024]{1,0:T(8,128)}, u32[]{:S(2)}) copy-start(f32[64,1024]{1,0:T(8,128)} %param.32) | copy-start | bytes 786436
  51.9 4.6 %copy-start.40 = (f32[64]{0:T(128)S(1)}, f32[64]{0:T(128)}, u32[]{:S(2)}) copy-start(f32[64]{0:T(128)} %constant.226.clone) | copy-start | bytes 772
  51.9 6.8 %copy-start.24 = (f32[1,4,4,1024]{3,2,1,0:T(4,128)S(1)}, f32[1,4,4,1024]{3,2,1,0:T(4,128)}, u32[]{:S(2)}) copy-start(f32[1,4,4,1024]{3,2,1,0:T(4,128)} %copy-done.23) | copy-start | bytes 196612
  51.9 6.8 %copy-start.22 = (f32[1,4,4,1024]{3,2,1,0:T(4,128)S(1)}, f32[1,4,4,1024]{3,2,1,0:T(4,128)}, u32[]{:S(2)}) copy-start(f32[1,4,4,1024]{3,2,1,0:T(4,128)} %copy-done.21) | copy-start | bytes 196612
  73.7 13.9 %all-to-all-start.2 = ((s32[1,16,256]{2,0,1:T(1,128)}), s32[1,16,256]{2,0,1:T(1,128)}, u32[]{:S(2)}, u32[]{:S(2)}) async-start(s32[1,16,256]{2,0,1:T(1,128)} %bitcast.211), calls=%async_computation.2 | async-start | bytes 32768 | tf_op jit(solution)/shard_map/all_to_all | solution.py:150
  80.6 86.2 %all-reduce.28.cloned.1.call-start = ((), (), s32[]{:S(2)}) async-start(), calls=%async_computation.3 | async-start | bytes 524288 | tf_op jit(solution)/shard_map/psum | solution.py:176
  101.6 2.6 %copy-start.31 = (pred[1024]{0:T(1024)(128)(4,1)S(1)}, pred[1024]{0:T(1024)(128)(4,1)}, u32[]{:S(2)}) copy-start(pred[1024]{0:T(1024)(128)(4,1)} %copy-done.30) | copy-start | bytes 3076
  101.6 3.4 %copy-start.29 = (pred[1024]{0:T(1024)(128)(4,1)S(1)}, pred[1024]{0:T(1024)(128)(4,1)}, u32[]{:S(2)}) copy-start(pred[1024]{0:T(1024)(128)(4,1)} %copy-done.28) | copy-start | bytes 3076
  103.2 2.6 %copy-start.37 = (pred[1024]{0:T(1024)(128)(4,1)S(1)}, pred[1024]{0:T(1024)(128)(4,1)}, u32[]{:S(2)}) copy-start(pred[1024]{0:T(1024)(128)(4,1)} %copy-done.36) | copy-start | bytes 3076
  104.5 1.8 %copy-start.35 = (pred[1024]{0:T(1024)(128)(4,1)S(1)}, pred[1024]{0:T(1024)(128)(4,1)}, u32[]{:S(2)}) copy-start(pred[1024]{0:T(1024)(128)(4,1)} %copy-done.34) | copy-start | bytes 3076
  105.7 5.6 %copy-start.9 = (f32[1,4,4,4,1024]{4,3,1,2,0:T(4,128)S(1)}, f32[1,4,4,4,1024]{4,3,1,2,0:T(4,128)}, u32[]{:S(2)}) copy-start(f32[1,4,4,4,1024]{4,3,1,2,0:T(4,128)} %copy-done.8) | copy-start | bytes 786436
  105.7 5.6 %copy-start.25 = (f32[1,1,4,4,1024]{4,3,2,1,0:T(4,128)S(1)}, f32[1,1,4,4,1024]{4,3,2,1,0:T(4,128)}, u32[]{:S(2)}) copy-start(f32[1,1,4,4,1024]{4,3,2,1,0:T(4,128)} %get-tuple-element.123) | copy-start | bytes 196612
  105.8 5.6 %copy-start.26 = (f32[1,1,4,4,1024]{4,3,2,1,0:T(4,128)S(1)}, f32[1,1,4,4,1024]{4,3,2,1,0:T(4,128)}, u32[]{:S(2)}) copy-start(f32[1,1,4,4,1024]{4,3,2,1,0:T(4,128)} %get-tuple-element.124) | copy-start | bytes 196612
  106.4 6.0 %copy-start.32 = (pred[1024]{0:T(1024)(128)(4,1)S(1)}, pred[1024]{0:T(1024)(128)(4,1)}, u32[]{:S(2)}) copy-start(pred[1024]{0:T(1024)(128)(4,1)} %get-tuple-element.133) | copy-start | bytes 3076
  106.4 6.0 %copy-start.33 = (pred[1024]{0:T(1024)(128)(4,1)S(1)}, pred[1024]{0:T(1024)(128)(4,1)}, u32[]{:S(2)}) copy-start(pred[1024]{0:T(1024)(128)(4,1)} %get-tuple-element.134) | copy-start | bytes 3076
  107.0 5.4 %collective-permute-start.1 = (f32[1,4,4,4,256]{4,3,1,2,0:T(4,128)S(1)}, f32[1,4,4,4,256]{4,3,1,2,0:T(4,128)S(1)}, u32[]{:S(2)}, u32[]{:S(2)}) collective-permute-start(f32[1,4,4,4,256]{4,3,1,2,0:T(4,128)S(1)} %slice_bitcast_fusion.10), channel_id=1, source_target_pairs={{2,0},{4,2},{6,4},{8,6},{10,8},{12,10},{14,12},{16,14},{18,16},{20... | collective-permute-start | bytes 196616 | tf_op jit(solution)/shard_map/ppermute | solution.py:27
  108.3 4.1 %collective-permute-start = (f32[1,4,4,4,256]{4,3,1,2,0:T(4,128)S(1)}, f32[1,4,4,4,256]{4,3,1,2,0:T(4,128)S(1)}, u32[]{:S(2)}, u32[]{:S(2)}) collective-permute-start(f32[1,4,4,4,256]{4,3,1,2,0:T(4,128)S(1)} %slice_bitcast_fusion.11), channel_id=1, source_target_pairs={{0,2},{2,4},{4,6},{6,8},{8,10},{10,12},{12,14},{14,16},{16,18},{18... | collective-permute-start | bytes 196616 | tf_op jit(solution)/shard_map/ppermute | solution.py:25
  112.3 1.2 copy-start.1
  116.2 4.6 %copy-start.7 = (f32[2,64,1024]{2,1,0:T(8,128)S(1)}, f32[2,64,1024]{2,1,0:T(8,128)}, u32[]{:S(2)}) copy-start(f32[2,64,1024]{2,1,0:T(8,128)} %get-tuple-element.115) | copy-start | bytes 1572868
  128.2 6.4 %copy-start.15 = (f32[64,1024]{1,0:T(8,128)S(1)}, f32[64,1024]{1,0:T(8,128)}, u32[]{:S(2)}) copy-start(f32[64,1024]{1,0:T(8,128)} %param.32) | copy-start | bytes 786436
  128.2 6.3 %copy-start.16 = (f32[64,1024]{1,0:T(8,128)S(1)}, f32[64,1024]{1,0:T(8,128)}, u32[]{:S(2)}) copy-start(f32[64,1024]{1,0:T(8,128)} %fusion.15) | copy-start | bytes 786436
  128.3 6.3 %copy-start.17 = (f32[64,1024]{1,0:T(8,128)S(1)}, f32[64,1024]{1,0:T(8,128)}, u32[]{:S(2)}) copy-start(f32[64,1024]{1,0:T(8,128)} %fusion.14) | copy-start | bytes 786436
  128.3 6.3 %copy-start.41 = (f32[64]{0:T(128)S(1)}, f32[64]{0:T(128)}, u32[]{:S(2)}) copy-start(f32[64]{0:T(128)} %constant.226.clone) | copy-start | bytes 772
  129.1 1.0 copy-start.2
  130.2 0.7 copy-start.5
  130.2 4.4 %copy-start.6 = (f32[4,1,4,4,1024]{4,3,1,0,2:T(4,128)}, f32[4,1,4,4,1024]{4,3,1,0,2:T(4,128)S(1)}, u32[]{:S(2)}) copy-start(f32[4,1,4,4,1024]{4,3,1,0,2:T(4,128)S(1)} %get-tuple-element.112) | copy-start | bytes 786436
  130.2 15.6 %copy-start.3 = (f32[4,4,4,4,1024]{4,3,1,0,2:T(4,128)S(1)}, f32[4,4,4,4,1024]{4,3,1,0,2:T(4,128)}, u32[]{:S(2)}) copy-start(f32[4,4,4,4,1024]{4,3,1,0,2:T(4,128)} %copy-done.2) | copy-start | bytes 3145732
  130.9 3.6 %copy-start.13 = (f32[4,1,4,4,1024]{4,3,2,0,1:T(4,128)}, f32[4,1,4,4,1024]{4,3,2,0,1:T(4,128)S(1)}, u32[]{:S(2)}) copy-start(f32[4,1,4,4,1024]{4,3,2,0,1:T(4,128)S(1)} %copy.249) | copy-start | bytes 786436
  131.0 9.8 %collective-permute-start.4 = (f32[1,4,4,4,256]{4,3,2,1,0:T(4,128)S(1)}, f32[1,4,4,4,256]{4,3,2,1,0:T(4,128)S(1)}, u32[]{:S(2)}, u32[]{:S(2)}) collective-permute-start(f32[1,4,4,4,256]{4,3,2,1,0:T(4,128)S(1)} %slice_bitcast_fusion.5), channel_id=1, source_target_pairs={{0,2},{2,4},{4,6},{6,8},{8,10},{10,12},{12,14},{14,16},{16,18},{18... | collective-permute-start | bytes 196616 | tf_op jit(solution)/shard_map/ppermute | solution.py:25
  134.6 1.5 copy-start.12
  137.7 11.1 %copy-start.4 = (f32[64,1024]{1,0:T(8,128)S(1)}, f32[64,1024]{1,0:T(8,128)}, u32[]{:S(2)}) copy-start(f32[64,1024]{1,0:T(8,128)} %div.62) | copy-start | bytes 786436
  139.5 5.2 %collective-permute-start.5 = (f32[1,4,4,4,256]{4,3,2,1,0:T(4,128)}, f32[1,4,4,4,256]{4,3,2,1,0:T(4,128)S(1)}, u32[]{:S(2)}, u32[]{:S(2)}) collective-permute-start(f32[1,4,4,4,256]{4,3,2,1,0:T(4,128)} %slice_bitcast_fusion.4), channel_id=1, source_target_pairs={{2,0},{4,2},{6,4},{8,6},{10,8},{12,10},{14,12},{16,14},{18,16},{20... | collective-permute-start | bytes 196616 | tf_op jit(solution)/shard_map/ppermute | solution.py:27
Sparse Core Ops, SparseCore 0:
  139.6 27.1 all-reduce.27
where the time goes:
time: 179 us; the launch traced here: 175 us
  matrix products  36.2 us (20%)
  waiting for transfers between devices  35.8 us (20%)
  starting transfers between devices  33.8 us (19%)
  local copies, waits for them, and re-layouts  32.2 us (18%)
  other arithmetic  22 us (12%)
  between operations  15.3 us (9%)
    psum x1, waiting for transfers between devices, shards(): total = lax.psum(kern, 'event')  16.6 us
    all_to_all x1, waiting for transfers between devices, shards(): lax.all_to_all(send_weights, 'space', split_axis=1, concat_axis=1, tiled=...  14.4 us
    dot_general x1, matrix products, shards(): jnp.dot(rows_out, placing, precision=high, preferred_element_type=jnp.flo...  12.6 us
    dot_general x1, matrix products, shards(): jnp.dot(contrib, landing, precision=high, preferred_element_type=jnp.floa...  9.72 us
    ppermute x3, starting transfers between devices, padded(): lax.ppermute(tail, axis, [(i, (i + 1) % count) for i in range(ends)])  9.62 us
    all_to_all x1, starting transfers between devices, shards(): lax.all_to_all(send_records, 'space', split_axis=1, concat_axis=1, tiled=...  8.68 us
    dot_general x2, matrix products, shards(): grads = jnp.einsum('dnm,fme->dfne', grad_ops, now, precision=high)  7.09 us
    all_to_all x1, starting transfers between devices, shards(): lax.all_to_all(send_ids, 'space', split_axis=1, concat_axis=1, tiled=True)  6.86 us
  transfers between devices with their start and end apart: 10, of which 4 were waited for; matrix products, arithmetic and copies ran while one was open for 27% of the time, Pallas kernels for 0%

commit v1 on v0

v1 whole, which is shorter than its diff:
```python
import functools

import jax
import jax.numpy as jnp
import numpy as np
from jax import lax
from jax.experimental import pallas as pl
from jax.experimental.pallas import tpu as pltpu
from jax.sharding import PartitionSpec as P

EX = 16
EY = 16
STEPS = 2
CAP = 256
NODES = 64
SUB = 8
LANE = 128
FIELD = NODES * SUB
FACE = 4 * SUB


TIME_STEP = 0.08
STEP_SQUARE = 0.0064

EDGE = np.array([1.0 / 6.0, 5.0 / 6.0, 5.0 / 6.0, 1.0 / 6.0])
WEIGHT = [float(np.float32(EDGE[n // 16] * EDGE[n // 4 % 4] * EDGE[n % 4])) for n in range(NODES)]
ROOT5 = float(np.sqrt(5.0))

LINES = (
    [[16 * c + 4 * b + i for i in range(4)] for c in range(4) for b in range(4)],
    [[16 * c + 4 * i + a for i in range(4)] for c in range(4) for a in range(4)],
    [[16 * i + 4 * b + a for i in range(4)] for b in range(4) for a in range(4)],
)


def derive(x0, x1, x2, x3):
    o0, o1 = x0 - x3, x1 - x2
    q = (x1 + x2) - (x0 + x3)
    a0, a1 = 1.25 * q, (0.25 * ROOT5) * q
    b0 = -1.75 * o0 + (1.25 * ROOT5) * o1
    b1 = -0.25 * o0 - (0.25 * ROOT5) * o1
    return b0 + a0, b1 + a1, b1 - a1, b0 - a0


def derive_transposed(h0, h1, h2, h3):
    p0, m0, p1, m1 = h0 + h3, h0 - h3, h1 + h2, h1 - h2
    q = 1.25 * m0 + (0.25 * ROOT5) * m1
    o0 = -1.75 * p0 - 0.25 * p1
    o1 = (1.25 * ROOT5) * p0 - (0.25 * ROOT5) * p1
    return o0 - q, o1 + q, q - o1, -o0 - q


def at(ref, base, node):
    if isinstance(base, int):
        return ref.at[pl.ds(base + node * SUB, SUB), :]
    return ref.at[pl.ds(pl.multiple_of(base, SUB) + node * SUB, SUB), :]


def spread(src_ref, index, dst_ref, base):
    for k in range(SUB):
        block = src_ref[:, k * LANE : (k + 1) * LANE] if index is None else src_ref[index, :, k * LANE : (k + 1) * LANE]
        dst_ref[pl.ds(base + k, NODES, stride=SUB), :] = block


def gather_back(src_ref, base, dst_ref, index):
    for k in range(SUB):
        dst_ref[index, :, k * LANE : (k + 1) * LANE] = src_ref[pl.ds(base + k, NODES, stride=SUB), :]


def places():
    lane = lax.broadcasted_iota(jnp.int32, (SUB, LANE), 1)
    sub = lax.broadcasted_iota(jnp.int32, (SUB, LANE), 0)
    return lane, sub


def assemble(ref, base):
    lane, sub = places()
    zero = jnp.zeros((SUB, LANE), jnp.float32)
    not_first = lane % EX != 0
    not_last = lane % EX != EX - 1
    odd = sub % 2 == 1
    for c in range(4):
        for b in range(4):
            n = 16 * c + 4 * b
            low_at, high_at = at(ref, base, n), at(ref, base, n + 3)
            low, high = low_at[...], high_at[...]
            low_at[...] = low + jnp.where(not_first, pltpu.roll(high, 1, 1), zero)
            high_at[...] = high + jnp.where(not_last, pltpu.roll(low, LANE - 1, 1), zero)
    for c in range(4):
        for a in range(4):
            n = 16 * c + a
            low_at, high_at = at(ref, base, n), at(ref, base, n + 12)
            low, high = low_at[...], high_at[...]
            back = pltpu.roll(high, EX, 1)
            ahead = pltpu.roll(low, LANE - EX, 1)
            back = jnp.where(lane >= EX, back, jnp.where(odd, pltpu.roll(back, 1, 0), zero))
            ahead = jnp.where(lane < LANE - EX, ahead, jnp.where(odd, zero, pltpu.roll(ahead, SUB - 1, 0)))
            low_at[...] = low + back
            high_at[...] = high + ahead
    for n in range(16):
        low_at, high_at = at(ref, base, n), at(ref, base, n + 48)
        low, high = low_at[...], high_at[...]
        low_at[...] = low + jnp.where(sub >= 2, pltpu.roll(high, 2, 0), zero)
        high_at[...] = high + jnp.where(sub < SUB - 2, pltpu.roll(low, SUB - 2, 0), zero)


def roll_sub(value, shift):
    shift = shift % SUB
    return value if shift == 0 else pltpu.roll(value, shift, 0)


def pack_faces(ref, base, low_ref, high_ref, out_base):
    _, sub = places()
    for b in range(4):
        for target, first, shift in ((low_ref, 0, 0), (high_ref, 48, 2)):
            pieces = [roll_sub(at(ref, base, first + 4 * b + a)[...], 2 * a + shift) for a in range(4)]
            tile = jnp.where(
                sub < 4,
                jnp.where(sub < 2, pieces[0], pieces[1]),
                jnp.where(sub < 6, pieces[2], pieces[3]),
            )
            at(target, out_base, b)[...] = tile


def with_rim(value, node, low_ref, high_ref, rim_base):
    _, sub = places()
    zero = jnp.zeros((SUB, LANE), jnp.float32)
    c, b, a = node // 16, node // 4 % 4, node % 4
    if c == 0:
        return value + jnp.where(sub < 2, roll_sub(at(low_ref, rim_base, b)[...], -2 * a), zero)
    if c == 3:
        return value + jnp.where(sub >= 6, roll_sub(at(high_ref, rim_base, b)[...], 6 - 2 * a), zero)
    return value


def stiffness(ins, outs, stiff_ref, kern):
    for dim, lines in enumerate(LINES):
        for line in lines:
            stiff = [at(stiff_ref, 0, n)[...] for n in line]
            grads = []
            for (src, sbase), out in zip(ins, outs):
                g = derive(*[at(src, sbase, n)[...] for n in line])
                grads.append(g)
                if out is None:
                    continue
                dst, dbase = out
                back = derive_transposed(*[x * s for x, s in zip(g, stiff)])
                for n, x in zip(line, back):
                    place = at(dst, dbase, n)
                    place[...] = x if dim == 0 else place[...] + x
            if kern is not None:
                for i, n in enumerate(line):
                    place = at(kern, 0, n)
                    place[...] = place[...] + grads[0][i] * grads[1][i]


def place_kernel(owner_ref, local_ref, weights_ref, records_ref, out_ref, rank_ref, data_ref):
    stations = weights_ref.shape[1]
    slabs, rows, _ = out_ref.shape
    blocks = stations // LANE
    owner_id = lax.broadcasted_iota(jnp.int32, (slabs, LANE), 0)
    before = lax.broadcasted_iota(jnp.int32, (LANE, LANE), 0) < lax.broadcasted_iota(jnp.int32, (LANE, LANE), 1)
    counting = jnp.concatenate(
        [jnp.where(before, 1.0, 0.0), jnp.ones((LANE, LANE), jnp.float32)], axis=1
    ).astype(jnp.bfloat16)
    named = [jnp.where(owner_ref[b : b + 1, :] == owner_id, 1.0, 0.0) for b in range(blocks)]
    counts = jnp.dot(
        jnp.concatenate(named, axis=0).astype(jnp.bfloat16), counting, preferred_element_type=jnp.float32
    )
    total = jnp.zeros((slabs, LANE), jnp.float32)
    for b in range(blocks):
        part = counts[b * slabs : (b + 1) * slabs]
        rank_ref[b : b + 1, :] = jnp.sum(named[b] * (part[:, :LANE] + total), axis=0, keepdims=True)
        total = total + part[:, LANE:]
    extra = rows - weights_ref.shape[0] - records_ref.shape[0]
    for b in range(blocks):
        cut = slice(b * LANE, (b + 1) * LANE)
        ids = jnp.broadcast_to(local_ref[b : b + 1, :].astype(jnp.float32), (extra, LANE))
        full = jnp.concatenate([weights_ref[:, cut], records_ref[:, cut], ids], axis=0)
        high = full.astype(jnp.bfloat16)
        data_ref[:rows, cut] = high
        data_ref[rows:, cut] = (full - high.astype(jnp.float32)).astype(jnp.bfloat16)
    slot = lax.broadcasted_iota(jnp.int32, (CAP, LANE), 0).astype(jnp.bfloat16)

    def one(slab, _):
        hot = []
        for b in range(blocks):
            wanted = jnp.where(owner_ref[b : b + 1, :] == slab, rank_ref[b : b + 1, :], -1.0).astype(jnp.bfloat16)
            hot.append(jnp.where(slot == wanted, jnp.bfloat16(1), jnp.bfloat16(0)))
        placed = lax.dot_general(
            data_ref[...],
            jnp.concatenate(hot, axis=1),
            (((1,), (1,)), ((), ())),
            preferred_element_type=jnp.float32,
        )
        out_ref[slab] = placed[:rows] + placed[rows:]
        return 0

    lax.fori_loop(0, slabs, one, 0)


def land(got_ref, step, events, out_ref, acc_ref):
    slabs = got_ref.shape[0]
    group = 4
    half = events * NODES
    slot = lax.broadcasted_iota(jnp.int32, (CAP, LANE), 0).astype(jnp.bfloat16)
    acc_ref[...] = jnp.zeros_like(acc_ref)

    def one(g, _):
        left, hot = [], [[] for _ in range(4)]
        for i in range(group):
            src = g * group + i
            weights = got_ref[src, :NODES, :]
            parts = []
            for event in range(events):
                row = NODES + event * STEPS + step
                parts.append(weights * got_ref[src, row : row + 1, :])
            full = jnp.concatenate(parts, axis=0)
            high = full.astype(jnp.bfloat16)
            low = (full - high.astype(jnp.float32)).astype(jnp.bfloat16)
            left.append(jnp.concatenate([high, low], axis=0))
            ids = got_ref[src, NODES + events * STEPS : NODES + events * STEPS + 1, :].astype(jnp.int32)
            for q in range(4):
                for cut in (slice(0, LANE), slice(LANE, 2 * LANE)):
                    wanted = jnp.where(ids[:, cut] // CAP == q, ids[:, cut] % CAP, -1).astype(jnp.float32).astype(jnp.bfloat16)
                    hot[q].append(jnp.where(slot == wanted, jnp.bfloat16(1), jnp.bfloat16(0)))
        left = jnp.concatenate(left, axis=1)
        for q in range(4):
            landed = lax.dot_general(
                left,
                jnp.concatenate(hot[q], axis=1),
                (((1,), (1,)), ((), ())),
                preferred_element_type=jnp.float32,
            )
            cut = slice(q * CAP, (q + 1) * CAP)
            acc_ref[:, cut] += landed[:half] + landed[half:]
        return 0

    lax.fori_loop(0, slabs // group, one, 0)
    for event in range(events):
        for k in range(SUB):
            out_ref[pl.ds(event * FIELD + k, NODES, stride=SUB), :] = acc_ref[
                event * NODES : (event + 1) * NODES, k * LANE : (k + 1) * LANE
            ]


def land_first_kernel(events, got_ref, out_ref, low_ref, high_ref, acc_ref):
    land(got_ref, 0, events, out_ref, acc_ref)
    for event in range(events):
        assemble(out_ref, event * FIELD)
        pack_faces(out_ref, event * FIELD, low_ref, high_ref, event * FACE)


def land_later_kernel(events, got_ref, out_ref, acc_ref):
    land(got_ref, 1, events, out_ref, acc_ref)


def first_kernel(events, fwd_ref, adj_ref, shear_ref, density_ref, _, fields_ref, stiff_ref, kern_ref, low_ref, high_ref, in_ref):
    spread(shear_ref, None, stiff_ref, 0)
    for n in range(NODES):
        place = at(stiff_ref, 0, n)
        place[...] = place[...] * WEIGHT[n]
        at(kern_ref, 0, n)[...] = jnp.zeros((SUB, LANE), jnp.float32)
        at(fields_ref, 2 * events * FIELD, n)[...] = density_ref[...] * WEIGHT[n]

    def one(event, _):
        u, v = event * FIELD, (events + event) * FIELD
        spread(fwd_ref, event, in_ref, 0)
        spread(adj_ref, event, in_ref, FIELD)
        stiffness([(in_ref, 0), (in_ref, FIELD)], [(fields_ref, u), (fields_ref, v)], stiff_ref, kern_ref)
        return 0

    lax.fori_loop(0, events, one, 0)

    def join(field, _):
        assemble(fields_ref, field * FIELD)
        pack_faces(fields_ref, field * FIELD, low_ref, high_ref, field * FACE)
        return 0

    lax.fori_loop(0, 2 * events + 1, join, 0)


def second_kernel(
    events, fwd_ref, fwd_prev_ref, adj_ref, adj_prev_ref, fields_ref, stiff_ref, rim_low_ref, rim_high_ref,
    fwd_out_ref, now_ref, factor_ref, next_ref, low_ref, high_ref, in_ref, prev_ref,
):
    for n in range(NODES):
        mass = with_rim(at(fields_ref, 2 * events * FIELD, n)[...], n, rim_low_ref, rim_high_ref, 2 * events * FACE)
        at(factor_ref, 0, n)[...] = STEP_SQUARE / mass

    def step(event, now_src, prev_src, field):
        spread(now_src, event, in_ref, 0)
        spread(prev_src, event, prev_ref, 0)
        for n in range(NODES):
            force = with_rim(at(fields_ref, field * FIELD, n)[...], n, rim_low_ref, rim_high_ref, field * FACE)
            at(now_ref, field * FIELD, n)[...] = (
                2.0 * at(in_ref, 0, n)[...] - at(prev_ref, 0, n)[...] - at(factor_ref, 0, n)[...] * force
            )

    def one(event, _):
        step(event, fwd_ref, fwd_prev_ref, event)
        step(event, adj_ref, adj_prev_ref, events + event)
        gather_back(now_ref, event * FIELD, fwd_out_ref, event)
        stiffness([(now_ref, event * FIELD)], [(next_ref, event * FIELD)], stiff_ref, None)
        assemble(next_ref, event * FIELD)
        pack_faces(next_ref, event * FIELD, low_ref, high_ref, event * FACE)
        return 0

    lax.fori_loop(0, events, one, 0)


def last_kernel(events, first, prev_ref, now_ref, factor_ref, next_ref, rim_low_ref, rim_high_ref, *rest):
    if first:
        out_ref, in_ref, done_ref = rest
    else:
        parts, (out_ref, kernel_ref, in_ref, done_ref) = rest[:-4], rest[-4:]
        total = parts[0][0]
        for part in parts[1:]:
            total = total + part[0]
        kernel_ref[...] = total

    def one(event, _):
        spread(prev_ref, event, in_ref, 0)
        for n in range(NODES):
            force = with_rim(at(next_ref, event * FIELD, n)[...], n, rim_low_ref, rim_high_ref, event * FACE)
            at(done_ref, 0, n)[...] = (
                2.0 * at(now_ref, event * FIELD, n)[...] - at(in_ref, 0, n)[...] - at(factor_ref, 0, n)[...] * force
            )
        gather_back(done_ref, 0, out_ref, event)
        return 0

    lax.fori_loop(0, events, one, 0)


def third_kernel(
    events, share, position_ref, now_ref, factor_ref, stiff_ref, kern_in_ref, source_ref, later_ref, rim_low_ref, rim_high_ref,
    adj_out_ref, adj_now_ref, next_ref, parts_ref, low_ref, high_ref, kern_ref,
):
    kern_ref[...] = kern_in_ref[...]

    def one(event, _):
        here = event * FIELD
        for n in range(NODES):
            source = with_rim(at(source_ref, here, n)[...], n, rim_low_ref, rim_high_ref, event * FACE)
            at(adj_now_ref, here, n)[...] = at(now_ref, (events + event) * FIELD, n)[...] + at(factor_ref, 0, n)[...] * source
        gather_back(adj_now_ref, here, adj_out_ref, event)
        stiffness([(now_ref, here), (adj_now_ref, here)], [None, (next_ref, here)], stiff_ref, kern_ref)
        for n in range(NODES):
            place = at(next_ref, here, n)
            place[...] = place[...] - at(later_ref, here, n)[...]
        assemble(next_ref, here)
        pack_faces(next_ref, here, low_ref, high_ref, event * FACE)
        return 0

    lax.fori_loop(0, events, one, 0)
    for n in range(NODES):
        place = at(kern_ref, 0, n)
        place[...] = -TIME_STEP * at(stiff_ref, 0, n)[...] * place[...]
    tiles = SUB // share
    for j in range(share):
        owner = lax.rem(position_ref[0] + j, share)
        for k in range(tiles):
            parts_ref[j, :, k * LANE : (k + 1) * LANE] = kern_ref[pl.ds(owner * tiles + k, NODES, stride=SUB), :]


def call(body, outs, scratch=(), cost=2_000_000, smem=0, count=0):
    in_specs = [pl.BlockSpec(memory_space=pltpu.SMEM)] * smem + [pl.BlockSpec(memory_space=pltpu.VMEM)] * (count - smem)
    return pl.pallas_call(
        body,
        out_shape=[jax.ShapeDtypeStruct(shape, jnp.float32) for shape in outs],
        in_specs=in_specs,
        out_specs=[pl.BlockSpec(memory_space=pltpu.VMEM)] * len(outs),
        scratch_shapes=[pltpu.VMEM(shape, dtype) for shape, dtype in scratch],
        compiler_params=pltpu.CompilerParams(vmem_limit_bytes=24 * 1024 * 1024),
        cost_estimate=pl.CostEstimate(flops=cost, bytes_accessed=cost, transcendentals=0),
    )


def beside(low, high):
    count = lax.axis_size("space")
    from_before = lax.ppermute(high, "space", [(i, i + 1) for i in range(count - 1)])
    from_after = lax.ppermute(low, "space", [(i + 1, i) for i in range(count - 1)])
    return from_before, from_after


def shards(
    fwd_now,
    fwd_prev,
    adj_now,
    adj_prev,
    shear_mod,
    density,
    station_owner,
    receiver_local,
    station_weights,
    adj_records,
):
    events = fwd_now.shape[0]
    stations = station_owner.shape[0]
    elements = fwd_now.shape[-1]
    slabs = lax.axis_size("space")
    share = lax.axis_size("event")
    f32 = jnp.float32
    rows = -(-(NODES + events * STEPS + 1) // SUB) * SUB
    blocks = stations // LANE

    send = call(
        place_kernel,
        [(slabs, rows, CAP)],
        [((blocks, LANE), f32), ((2 * rows, stations), jnp.bfloat16)],
        count=4,
    )(
        station_owner.reshape(blocks, LANE),
        receiver_local.reshape(blocks, LANE),
        station_weights,
        adj_records.reshape(events * STEPS, stations),
    )[0]
    got = lax.all_to_all(send, "space", split_axis=0, concat_axis=0, tiled=True)

    fields, stiff, kern, low, high = call(
        functools.partial(first_kernel, events),
        [
            ((2 * events + 1) * FIELD, LANE),
            (FIELD, LANE),
            (FIELD, LANE),
            ((2 * events + 1) * FACE, LANE),
            ((2 * events + 1) * FACE, LANE),
        ],
        [((2 * FIELD, LANE), f32)],
        count=5,
    )(fwd_now, adj_now, shear_mod, density.reshape(SUB, LANE), send[0, :8, :128])
    rim_low, rim_high = beside(low, high)
    fwd_before, now, factor, fwd_next, low, high = call(
        functools.partial(second_kernel, events),
        [
            fwd_now.shape,
            (2 * events * FIELD, LANE),
            (FIELD, LANE),
            (events * FIELD, LANE),
            (events * FACE, LANE),
            (events * FACE, LANE),
        ],
        [((FIELD, LANE), f32), ((FIELD, LANE), f32)],
        count=8,
    )(fwd_now, fwd_prev, adj_now, adj_prev, fields, stiff, rim_low, rim_high)
    rim_low, rim_high = beside(low, high)
    fwd_last = call(
        functools.partial(last_kernel, events, True),
        [fwd_now.shape],
        [((FIELD, LANE), f32), ((FIELD, LANE), f32)],
        count=6,
    )(fwd_now, now, factor, fwd_next, rim_low, rim_high)[0]

    source, low, high = call(
        functools.partial(land_first_kernel, events),
        [(events * FIELD, LANE), (events * FACE, LANE), (events * FACE, LANE)],
        [((events * NODES, elements), f32)],
        count=1,
    )(got)
    rim_low, rim_high = beside(low, high)
    later = call(
        functools.partial(land_later_kernel, events),
        [(events * FIELD, LANE)],
        [((events * NODES, elements), f32)],
        count=1,
    )(got)[0]
    adj_before, adj_mid, adj_next, parts, low, high = call(
        functools.partial(third_kernel, events, share),
        [
            adj_now.shape,
            (events * FIELD, LANE),
            (events * FIELD, LANE),
            (share, NODES, elements // share),
            (events * FACE, LANE),
            (events * FACE, LANE),
        ],
        [((FIELD, LANE), f32)],
        smem=1,
        count=9,
    )(
        lax.axis_index("event").reshape(1).astype(jnp.int32),
        now, factor, stiff, kern, source, later, rim_low, rim_high,
    )
    rim_low, rim_high = beside(low, high)
    pieces = [parts[0:1]] + [
        lax.ppermute(parts[j : j + 1], "event", [(i, (i + j) % share) for i in range(share)]) for j in range(1, share)
    ]
    adj_last, kernel = call(
        functools.partial(last_kernel, events, False),
        [adj_now.shape, (NODES, elements // share)],
        [((FIELD, LANE), f32), ((FIELD, LANE), f32)],
        count=6 + share,
    )(adj_now, adj_mid, factor, adj_next, rim_low, rim_high, *pieces)
    return fwd_last, fwd_before, adj_last, adj_before, kernel


def solution(mesh):
    in_specs = (
        P("event", None, "space"),
        P("event", None, "space"),
        P("event", None, "space"),
        P("event", None, "space"),
        P(None, "space"),
        P("space"),
        P("space", None),
        P("space"),
        P(None, "space"),
        P("event", None, "space"),
    )
    out_specs = (
        P("event", None, "space"),
        P("event", None, "space"),
        P("event", None, "space"),
        P("event", None, "space"),
        P(None, ("space", "event")),
    )
    return jax.shard_map(shards, mesh=mesh, in_specs=in_specs, out_specs=out_specs, check_vma=False)
```

time: 179 us -> 91.2 us (0.51)
  the two profiles are of different devices: /device:TPU:0 before, /device:TPU:13 now
where the time goes in v1:
time: 91.2 us; the launch traced here: 90.3 us
  starting transfers between devices  32.3 us (35%)
  Pallas kernels  27.6 us (30%)
  waiting for transfers between devices  19.4 us (21%)
  local copies, waits for them, and re-layouts  10.1 us (11%)
    ppermute x4, starting transfers between devices, beside(): lax.ppermute(high, 'space', [(i, i + 1) for i in range(count - 1)])  16.7 us
    all_to_all x1, waiting for transfers between devices, shards(): got = lax.all_to_all(send, 'space', split_axis=0, concat_axis=0, tiled=True)  16.4 us
    pallas_call x1, Pallas kernels, shards(): call(place_kernel, [(slabs, rows, CAP)], [((blocks, LANE), f32), ((2 * ro...  9.1 us
    unnamed x32, local copies, waits for them, and re-layouts  8.62 us
    ppermute x4, starting transfers between devices, beside(): lax.ppermute(low, 'space', [(i + 1, i) for i in range(count - 1)])  7.68 us
    all_to_all x1, starting transfers between devices, shards(): got = lax.all_to_all(send, 'space', split_axis=0, concat_axis=0, tiled=True)  6.69 us
    pallas_call x1, Pallas kernels, shards(): call(functools.partial(land_first_kernel, events), [(events * FIELD, LANE...  4.03 us
    pallas_call x1, Pallas kernels, shards(): call(functools.partial(land_later_kernel, events), [(events * FIELD, LANE...  3.21 us
  transfers between devices with their start and end apart: 10, of which 2 were waited for; matrix products, arithmetic and copies ran while one was open for 1% of the time, Pallas kernels for 16%

profile of v1, /device:TPU:13, one launch (start us, length us, event | category | flops | bytes accessed | tf_op | source)
XLA Modules:
  0.0 90.3 jit_solution(18281068294001261292)
XLA Ops:
  0.6 0.8 reshape.28.records_ref
  1.4 0.0 copy-start.7
  1.4 1.0 %copy-done.7 = f32[64,2048]{1,0:T(8,128)S(1)} copy-done((f32[64,2048]{1,0:T(8,128)S(1)}, f32[64,2048]{1,0:T(8,128)}, u32[]{:S(2)}) %copy-start.7) | copy-done | bytes 524312
  2.5 0.0 copy-start.13
  2.5 0.7 copy-done.13
  3.2 0.0 copy-start.14
  3.2 0.7 copy-done.14
  3.9 9.1 %shard_map.137 = f32[16,72,256]{2,1,0:T(8,128)} custom-call(s32[16,128]{1,0:T(8,128)S(1)} %bitcast.6, s32[16,128]{1,0:T(8,128)S(1)} %bitcast.7, f32[64,2048]{1,0:T(8,128)S(1)} %copy-done.7, f32[4,2048]{1,0:T(4,128)S(1)} %reshape.28.records_ref), custom_call_target="tpu_custom_call" | custom-call | flops 2000000 | bytes 2000000 | tf_op jit(solution)/shard_map/pallas_call | solution.py:407
  13.0 0.0 copy-start
  13.0 0.0 copy-start.1
  13.0 0.0 copy-start.15
  13.0 6.7 %all-to-all-start = ((f32[16,72,256]{2,1,0:T(8,128)}), f32[16,72,256]{2,1,0:T(8,128)S(1)}, u32[]{:S(2)}, u32[]{:S(2)}) async-start(f32[16,72,256]{2,1,0:T(8,128)} %shard_map.137), calls=%async_computation | async-start | bytes 2359296 | tf_op jit(solution)/shard_map/all_to_all | solution.py:418
  19.7 0.7 slice_bitcast_fusion._
  20.4 0.0 copy-done
  20.4 0.0 copy-done.1
  20.4 0.0 copy-done.15
  20.4 0.0 copy-start.10
  20.4 0.9 %copy-done.10 = f32[64,1024]{1,0:T(8,128)S(1)} copy-done((f32[64,1024]{1,0:T(8,128)S(1)}, f32[64,1024]{1,0:T(8,128)}, u32[]{:S(2)}) %copy-start.10) | copy-done | bytes 262168
  21.3 3.1 %shard_map.138 = (f32[2560,128]{1,0:T(8,128)S(1)}, f32[512,128]{1,0:T(8,128)S(1)}, f32[512,128]{1,0:T(8,128)S(1)}, f32[160,128]{1,0:T(8,128)}, f32[160,128]{1,0:T(8,128)}) custom-call(f32[2,64,1024]{2,1,0:T(8,128)S(1)} %copy-done, f32[2,64,1024]{2,1,0:T(8,128)S(1)} %copy-done.1, f32[64,1024]{1,0:T(8,128)S(1)} %copy-done.10, f32[8,128]{1,0:T(8,128)S(1)} %bitcast.8, ...), custom_call_target="tpu_custom_call" | custom-call | flops 2000000 | bytes 2000000 | tf_op jit(solution)/shard_map/pallas_call | solution.py:420
  24.4 0.0 copy-start.2
  24.4 0.7 copy-done.2
  25.1 0.0 copy-start.11
  25.1 0.7 copy-done.11
  25.8 3.3 %collective-permute-start = (f32[160,128]{1,0:T(8,128)}, f32[160,128]{1,0:T(8,128)}, u32[]{:S(2)}, u32[]{:S(2)}) collective-permute-start(f32[160,128]{1,0:T(8,128)} %get-tuple-element.29), channel_id=1, source_target_pairs={{0,2},{2,4},{4,6},{6,8},{8,10},{10,12},{12,14},{14,16},{16,18},{18... | collective-permute-start | bytes 245768 | tf_op jit(solution)/shard_map/ppermute | solution.py:381
  29.1 1.9 %collective-permute-start.1 = (f32[160,128]{1,0:T(8,128)}, f32[160,128]{1,0:T(8,128)}, u32[]{:S(2)}, u32[]{:S(2)}) collective-permute-start(f32[160,128]{1,0:T(8,128)} %get-tuple-element.30), channel_id=1, source_target_pairs={{2,0},{4,2},{6,4},{8,6},{10,8},{12,10},{14,12},{16,14},{18,16},{20... | collective-permute-start | bytes 245768 | tf_op jit(solution)/shard_map/ppermute | solution.py:382
  31.1 16.4 %all-to-all-done.got_ref = f32[16,72,256]{2,1,0:T(8,128)S(1)} async-done(((f32[16,72,256]{2,1,0:T(8,128)}), f32[16,72,256]{2,1,0:T(8,128)S(1)}, u32[]{:S(2)}, u32[]{:S(2)}) %all-to-all-start) | async-done | bytes 1179680 | tf_op jit(solution)/shard_map/all_to_all | solution.py:418
  47.4 4.0 %shard_map.141 = (f32[1024,128]{1,0:T(8,128)S(1)}, f32[64,128]{1,0:T(8,128)}, f32[64,128]{1,0:T(8,128)}) custom-call(f32[16,72,256]{2,1,0:T(8,128)S(1)} %all-to-all-done.got_ref), custom_call_target="tpu_custom_call" | custom-call | flops 2000000 | bytes 2000000 | tf_op jit(solution)/shard_map/pallas_call | solution.py:454
  51.4 0.0 copy-start.5
  51.4 0.8 copy-done.5
  52.2 4.0 %collective-permute-start.4 = (f32[64,128]{1,0:T(8,128)}, f32[64,128]{1,0:T(8,128)}, u32[]{:S(2)}, u32[]{:S(2)}) collective-permute-start(f32[64,128]{1,0:T(8,128)} %get-tuple-element.39), channel_id=1, source_target_pairs={{0,2},{2,4},{4,6},{6,8},{8,10},{10,12},{12,14},{14,16},{16,18},{18... | collective-permute-start | bytes 98312 | tf_op jit(solution)/shard_map/ppermute | solution.py:381
  56.3 1.9 %collective-permute-start.5 = (f32[64,128]{1,0:T(8,128)}, f32[64,128]{1,0:T(8,128)}, u32[]{:S(2)}, u32[]{:S(2)}) collective-permute-start(f32[64,128]{1,0:T(8,128)} %get-tuple-element.40), channel_id=1, source_target_pairs={{2,0},{4,2},{6,4},{8,6},{10,8},{12,10},{14,12},{16,14},{18,16},{20... | collective-permute-start | bytes 98312 | tf_op jit(solution)/shard_map/ppermute | solution.py:382
  58.2 0.0 collective-permute-done.rim_low_ref
  58.2 0.0 collective-permute-done.1.rim_high_ref
  58.2 0.0 copy-start.3
  58.2 0.9 %copy-done.3 = f32[512,128]{1,0:T(8,128)S(1)} copy-done((f32[512,128]{1,0:T(8,128)S(1)}, f32[512,128]{1,0:T(8,128)}, u32[]{:S(2)}) %copy-start.3) | copy-done | bytes 262168
  59.2 0.0 copy-start.8
  59.2 1.0 %copy-done.8 = f32[2,64,1024]{2,1,0:T(8,128)S(1)} copy-done((f32[2,64,1024]{2,1,0:T(8,128)S(1)}, f32[2,64,1024]{2,1,0:T(8,128)}, u32[]{:S(2)}) %copy-start.8) | copy-done | bytes 524312
  60.2 0.0 copy-start.9
  60.2 1.0 %copy-done.9 = f32[2,64,1024]{2,1,0:T(8,128)S(1)} copy-done((f32[2,64,1024]{2,1,0:T(8,128)S(1)}, f32[2,64,1024]{2,1,0:T(8,128)}, u32[]{:S(2)}) %copy-start.9) | copy-done | bytes 524312
  61.2 3.0 %shard_map.139 = (f32[2,64,1024]{2,1,0:T(8,128)}, f32[2048,128]{1,0:T(8,128)S(1)}, f32[512,128]{1,0:T(8,128)S(1)}, f32[1024,128]{1,0:T(8,128)S(1)}, f32[64,128]{1,0:T(8,128)S(1)}, /*index=5*/f32[64,128]{1,0:T(8,128)S(1)}) custom-call(f32[2,64,1024]{2,1,0:T(8,128)S(1)} %copy-done, f32[2,64,1024]{2,1,0:T(8,128)S(1)} %copy-done.8, ...), custom_call_target="tpu_custom_call" | custom-call | flops 2000000 | bytes 2000000 | tf_op jit(solution)/shard_map/pallas_call | solution.py:433
  64.3 0.0 copy-start.4
  64.3 0.0 copy-start.6
  64.3 0.0 copy-start.12
  64.3 3.2 %shard_map.142.later_ref = f32[1024,128]{1,0:T(8,128)S(1)} custom-call(f32[16,72,256]{2,1,0:T(8,128)S(1)} %all-to-all-done.got_ref), custom_call_target="tpu_custom_call" | custom-call | flops 2000000 | bytes 2000000 | tf_op jit(solution)/shard_map/pallas_call | solution.py:461
  67.5 0.0 collective-permute-done.4.rim_low_ref
  67.5 0.0 collective-permute-done.5.rim_high_ref
  67.5 0.0 copy-done.4
  67.5 0.0 copy-done.6
  67.5 0.0 copy-done.12
  67.5 2.9 %shard_map.143 = (f32[2,64,1024]{2,1,0:T(8,128)}, f32[1024,128]{1,0:T(8,128)S(1)}, f32[1024,128]{1,0:T(8,128)S(1)}, f32[2,64,512]{2,1,0:T(8,128)S(1)}, f32[64,128]{1,0:T(8,128)S(1)}, /*index=5*/f32[64,128]{1,0:T(8,128)S(1)}) custom-call(s32[1]{0:T(128)} %bitcast.4.position_ref, f32[2048,128]{1,0:T(8,128)S(1)} %get-tuple-element.31.now_ref, ...), custom_call_target="tpu_custom_call" | custom-call | flops 2000000 | bytes 2000000 | tf_op jit(solution)/shard_map/pallas_call | solution.py:467
  70.4 1.3 %collective-permute-start.8 = (f32[1,64,512]{2,1,0:T(8,128)S(1)}, f32[1,64,512]{2,1,0:T(8,128)S(1)}, u32[]{:S(2)}, u32[]{:S(2)}) collective-permute-start(f32[1,64,512]{2,1,0:T(8,128)S(1)} %get-tuple-element.49), channel_id=1, source_target_pairs={{0,1},{1,0},{2,3},{3,2},{4,5},{5,4},{6,7},{7,6},{8,9},{9,8},{10,11... | collective-permute-start | bytes 393224 | tf_op jit(solution)/shard_map/ppermute | solution.py:486
  71.7 4.8 %collective-permute-start.2 = (f32[64,128]{1,0:T(8,128)S(1)}, f32[64,128]{1,0:T(8,128)S(1)}, u32[]{:S(2)}, u32[]{:S(2)}) collective-permute-start(f32[64,128]{1,0:T(8,128)S(1)} %get-tuple-element.34), channel_id=1, source_target_pairs={{0,2},{2,4},{4,6},{6,8},{8,10},{10,12},{12,14},{14,16},{16,18},{18... | collective-permute-start | bytes 98312 | tf_op jit(solution)/shard_map/ppermute | solution.py:381
  76.5 1.9 %collective-permute-start.3 = (f32[64,128]{1,0:T(8,128)S(1)}, f32[64,128]{1,0:T(8,128)S(1)}, u32[]{:S(2)}, u32[]{:S(2)}) collective-permute-start(f32[64,128]{1,0:T(8,128)S(1)} %get-tuple-element.35), channel_id=1, source_target_pairs={{2,0},{4,2},{6,4},{8,6},{10,8},{12,10},{14,12},{16,14},{18,16},{20... | collective-permute-start | bytes 98312 | tf_op jit(solution)/shard_map/ppermute | solution.py:382
  78.5 4.5 %collective-permute-start.6 = (f32[64,128]{1,0:T(8,128)S(1)}, f32[64,128]{1,0:T(8,128)S(1)}, u32[]{:S(2)}, u32[]{:S(2)}) collective-permute-start(f32[64,128]{1,0:T(8,128)S(1)} %get-tuple-element.43), channel_id=1, source_target_pairs={{0,2},{2,4},{4,6},{6,8},{8,10},{10,12},{12,14},{14,16},{16,18},{18... | collective-permute-start | bytes 98312 | tf_op jit(solution)/shard_map/ppermute | solution.py:381
  83.0 1.9 %collective-permute-start.7 = (f32[64,128]{1,0:T(8,128)S(1)}, f32[64,128]{1,0:T(8,128)S(1)}, u32[]{:S(2)}, u32[]{:S(2)}) collective-permute-start(f32[64,128]{1,0:T(8,128)S(1)} %get-tuple-element.44), channel_id=1, source_target_pairs={{2,0},{4,2},{6,4},{8,6},{10,8},{12,10},{14,12},{16,14},{18,16},{20... | collective-permute-start | bytes 98312 | tf_op jit(solution)/shard_map/ppermute | solution.py:382
  84.9 0.0 collective-permute-done.2.rim_low_ref
  84.9 0.0 collective-permute-done.3.rim_high_ref
  84.9 1.2 %shard_map.140 = f32[2,64,1024]{2,1,0:T(8,128)} custom-call(f32[2,64,1024]{2,1,0:T(8,128)S(1)} %copy-done, f32[2048,128]{1,0:T(8,128)S(1)} %get-tuple-element.31.now_ref, f32[512,128]{1,0:T(8,128)S(1)} %get-tuple-element.32.factor_ref, f32[1024,128]{1,0:T(8,128)S(1)} %get-tuple-element.33.next_ref, f32[64,128]{1,0:T(8,128)S(1)} %collective-permute-done.2.rim_low_ref, ...), custom_call_target="tpu_custom_call" | custom-call | flops 2000000 | bytes 2000000 | tf_op jit(solution)/shard_map/pallas_call | solution.py:447
  86.1 0.0 collective-permute-done.6.rim_low_ref
  86.1 3.0 %collective-permute-done.7.rim_high_ref = f32[64,128]{1,0:T(8,128)S(1)} collective-permute-done((f32[64,128]{1,0:T(8,128)S(1)}, f32[64,128]{1,0:T(8,128)S(1)}, u32[]{:S(2)}, u32[]{:S(2)}) %collective-permute-start.7) | collective-permute-done | bytes 32800 | tf_op jit(solution)/shard_map/ppermute | solution.py:382
  89.1 0.0 collective-permute-done.8.rest_1_
  89.1 1.2 %shard_map.144 = (f32[2,64,1024]{2,1,0:T(8,128)}, f32[64,512]{1,0:T(8,128)}) custom-call(f32[2,64,1024]{2,1,0:T(8,128)S(1)} %copy-done.1, f32[1024,128]{1,0:T(8,128)S(1)} %get-tuple-element.41.now_ref, f32[512,128]{1,0:T(8,128)S(1)} %get-tuple-element.32.factor_ref, f32[1024,128]{1,0:T(8,128)S(1)} %get-tuple-element.42.next_ref, ...), custom_call_target="tpu_custom_call" | custom-call | flops 2000000 | bytes 2000000 | tf_op jit(solution)/shard_map/pallas_call | solution.py:488
  (1 shorter events, 0.0 us)
Async XLA Ops:
  1.4 1.0 %copy-start.7 = (f32[64,2048]{1,0:T(8,128)S(1)}, f32[64,2048]{1,0:T(8,128)}, u32[]{:S(2)}) copy-start(f32[64,2048]{1,0:T(8,128)} %weights_ref.1) | copy-start | bytes 1572868
  2.5 0.7 copy-start.13
  3.2 0.7 copy-start.14
  13.0 7.4 %copy-start = (f32[2,64,1024]{2,1,0:T(8,128)S(1)}, f32[2,64,1024]{2,1,0:T(8,128)}, u32[]{:S(2)}) copy-start(f32[2,64,1024]{2,1,0:T(8,128)} %prev_ref.2) | copy-start | bytes 1572868
  13.0 7.4 %copy-start.1 = (f32[2,64,1024]{2,1,0:T(8,128)S(1)}, f32[2,64,1024]{2,1,0:T(8,128)}, u32[]{:S(2)}) copy-start(f32[2,64,1024]{2,1,0:T(8,128)} %prev_ref.3) | copy-start | bytes 1572868
  13.0 7.4 %copy-start.15 = (f32[1024]{0:T(1024)S(1)}, f32[1024]{0:T(1024)}, u32[]{:S(2)}) copy-start(f32[1024]{0:T(1024)} %param.15) | copy-start | bytes 12292
  13.0 34.4 %all-to-all-start = ((f32[16,72,256]{2,1,0:T(8,128)}), f32[16,72,256]{2,1,0:T(8,128)S(1)}, u32[]{:S(2)}, u32[]{:S(2)}) async-start(f32[16,72,256]{2,1,0:T(8,128)} %shard_map.137), calls=%async_computation | async-start | bytes 2359296 | tf_op jit(solution)/shard_map/all_to_all | solution.py:418
  20.4 1.0 %copy-start.10 = (f32[64,1024]{1,0:T(8,128)S(1)}, f32[64,1024]{1,0:T(8,128)}, u32[]{:S(2)}) copy-start(f32[64,1024]{1,0:T(8,128)} %shear_ref.1) | copy-start | bytes 786436
  24.4 0.7 copy-start.2
  25.1 0.7 copy-start.11
  25.8 32.4 %collective-permute-start = (f32[160,128]{1,0:T(8,128)}, f32[160,128]{1,0:T(8,128)}, u32[]{:S(2)}, u32[]{:S(2)}) collective-permute-start(f32[160,128]{1,0:T(8,128)} %get-tuple-element.29), channel_id=1, source_target_pairs={{0,2},{2,4},{4,6},{6,8},{8,10},{10,12},{12,14},{14,16},{16,18},{18... | collective-permute-start | bytes 245768 | tf_op jit(solution)/shard_map/ppermute | solution.py:381
  29.1 29.1 %collective-permute-start.1 = (f32[160,128]{1,0:T(8,128)}, f32[160,128]{1,0:T(8,128)}, u32[]{:S(2)}, u32[]{:S(2)}) collective-permute-start(f32[160,128]{1,0:T(8,128)} %get-tuple-element.30), channel_id=1, source_target_pairs={{2,0},{4,2},{6,4},{8,6},{10,8},{12,10},{14,12},{16,14},{18,16},{20... | collective-permute-start | bytes 245768 | tf_op jit(solution)/shard_map/ppermute | solution.py:382
  51.4 0.8 copy-start.5
  52.2 15.3 %collective-permute-start.4 = (f32[64,128]{1,0:T(8,128)}, f32[64,128]{1,0:T(8,128)}, u32[]{:S(2)}, u32[]{:S(2)}) collective-permute-start(f32[64,128]{1,0:T(8,128)} %get-tuple-element.39), channel_id=1, source_target_pairs={{0,2},{2,4},{4,6},{6,8},{8,10},{10,12},{12,14},{14,16},{16,18},{18... | collective-permute-start | bytes 98312 | tf_op jit(solution)/shard_map/ppermute | solution.py:381
  56.3 11.2 %collective-permute-start.5 = (f32[64,128]{1,0:T(8,128)}, f32[64,128]{1,0:T(8,128)}, u32[]{:S(2)}, u32[]{:S(2)}) collective-permute-start(f32[64,128]{1,0:T(8,128)} %get-tuple-element.40), channel_id=1, source_target_pairs={{2,0},{4,2},{6,4},{8,6},{10,8},{12,10},{14,12},{16,14},{18,16},{20... | collective-permute-start | bytes 98312 | tf_op jit(solution)/shard_map/ppermute | solution.py:382
  58.2 1.0 %copy-start.3 = (f32[512,128]{1,0:T(8,128)S(1)}, f32[512,128]{1,0:T(8,128)}, u32[]{:S(2)}) copy-start(f32[512,128]{1,0:T(8,128)} %copy-done.2) | copy-start | bytes 786436
  59.2 1.0 %copy-start.8 = (f32[2,64,1024]{2,1,0:T(8,128)S(1)}, f32[2,64,1024]{2,1,0:T(8,128)}, u32[]{:S(2)}) copy-start(f32[2,64,1024]{2,1,0:T(8,128)} %fwd_prev_ref.1) | copy-start | bytes 1572868
  60.2 1.0 %copy-start.9 = (f32[2,64,1024]{2,1,0:T(8,128)S(1)}, f32[2,64,1024]{2,1,0:T(8,128)}, u32[]{:S(2)}) copy-start(f32[2,64,1024]{2,1,0:T(8,128)} %adj_prev_ref.1) | copy-start | bytes 1572868
  64.3 3.2 %copy-start.4 = (f32[512,128]{1,0:T(8,128)S(1)}, f32[512,128]{1,0:T(8,128)}, u32[]{:S(2)}) copy-start(f32[512,128]{1,0:T(8,128)} %copy-done.2) | copy-start | bytes 786436
  64.3 3.3 %copy-start.6 = (f32[1024,128]{1,0:T(8,128)S(1)}, f32[1024,128]{1,0:T(8,128)}, u32[]{:S(2)}) copy-start(f32[1024,128]{1,0:T(8,128)} %copy-done.5) | copy-start | bytes 1572868
  64.3 3.3 %copy-start.12 = (f32[512,128]{1,0:T(8,128)S(1)}, f32[512,128]{1,0:T(8,128)}, u32[]{:S(2)}) copy-start(f32[512,128]{1,0:T(8,128)} %copy-done.11) | copy-start | bytes 786436
  70.4 18.7 %collective-permute-start.8 = (f32[1,64,512]{2,1,0:T(8,128)S(1)}, f32[1,64,512]{2,1,0:T(8,128)S(1)}, u32[]{:S(2)}, u32[]{:S(2)}) collective-permute-start(f32[1,64,512]{2,1,0:T(8,128)S(1)} %get-tuple-element.49), channel_id=1, source_target_pairs={{0,1},{1,0},{2,3},{3,2},{4,5},{5,4},{6,7},{7,6},{8,9},{9,8},{10,11... | collective-permute-start | bytes 393224 | tf_op jit(solution)/shard_map/ppermute | solution.py:486
  71.7 13.2 %collective-permute-start.2 = (f32[64,128]{1,0:T(8,128)S(1)}, f32[64,128]{1,0:T(8,128)S(1)}, u32[]{:S(2)}, u32[]{:S(2)}) collective-permute-start(f32[64,128]{1,0:T(8,128)S(1)} %get-tuple-element.34), channel_id=1, source_target_pairs={{0,2},{2,4},{4,6},{6,8},{8,10},{10,12},{12,14},{14,16},{16,18},{18... | collective-permute-start | bytes 98312 | tf_op jit(solution)/shard_map/ppermute | solution.py:381
  76.5 8.4 %collective-permute-start.3 = (f32[64,128]{1,0:T(8,128)S(1)}, f32[64,128]{1,0:T(8,128)S(1)}, u32[]{:S(2)}, u32[]{:S(2)}) collective-permute-start(f32[64,128]{1,0:T(8,128)S(1)} %get-tuple-element.35), channel_id=1, source_target_pairs={{2,0},{4,2},{6,4},{8,6},{10,8},{12,10},{14,12},{16,14},{18,16},{20... | collective-permute-start | bytes 98312 | tf_op jit(solution)/shard_map/ppermute | solution.py:382
  78.5 7.7 %collective-permute-start.6 = (f32[64,128]{1,0:T(8,128)S(1)}, f32[64,128]{1,0:T(8,128)S(1)}, u32[]{:S(2)}, u32[]{:S(2)}) collective-permute-start(f32[64,128]{1,0:T(8,128)S(1)} %get-tuple-element.43), channel_id=1, source_target_pairs={{0,2},{2,4},{4,6},{6,8},{8,10},{10,12},{12,14},{14,16},{16,18},{18... | collective-permute-start | bytes 98312 | tf_op jit(solution)/shard_map/ppermute | solution.py:381
  83.0 6.1 %collective-permute-start.7 = (f32[64,128]{1,0:T(8,128)S(1)}, f32[64,128]{1,0:T(8,128)S(1)}, u32[]{:S(2)}, u32[]{:S(2)}) collective-permute-start(f32[64,128]{1,0:T(8,128)S(1)} %get-tuple-element.44), channel_id=1, source_target_pairs={{2,0},{4,2},{6,4},{8,6},{10,8},{12,10},{14,12},{16,14},{18,16},{20... | collective-permute-start | bytes 98312 | tf_op jit(solution)/shard_map/ppermute | solution.py:382

commit v2 on v1

v2 whole, which is shorter than its diff:
```python
import functools

import jax
import jax.numpy as jnp
import numpy as np
from jax import lax
from jax.experimental import pallas as pl
from jax.experimental.pallas import tpu as pltpu
from jax.sharding import PartitionSpec as P

EX = 16
EY = 16
STEPS = 2
CAP = 256
NODES = 64
SUB = 8
LANE = 128
FIELD = NODES * SUB
FACE = 4 * SUB
LAND_LIMIT = 24


TIME_STEP = 0.08
STEP_SQUARE = 0.0064

EDGE = np.array([1.0 / 6.0, 5.0 / 6.0, 5.0 / 6.0, 1.0 / 6.0])
WEIGHT = [float(np.float32(EDGE[n // 16] * EDGE[n // 4 % 4] * EDGE[n % 4])) for n in range(NODES)]
ROOT5 = float(np.sqrt(5.0))

LINES = (
    [[16 * c + 4 * b + i for i in range(4)] for c in range(4) for b in range(4)],
    [[16 * c + 4 * i + a for i in range(4)] for c in range(4) for a in range(4)],
    [[16 * i + 4 * b + a for i in range(4)] for b in range(4) for a in range(4)],
)


def derive(x0, x1, x2, x3):
    o0, o1 = x0 - x3, x1 - x2
    q = (x1 + x2) - (x0 + x3)
    a0, a1 = 1.25 * q, (0.25 * ROOT5) * q
    b0 = -1.75 * o0 + (1.25 * ROOT5) * o1
    b1 = -0.25 * o0 - (0.25 * ROOT5) * o1
    return b0 + a0, b1 + a1, b1 - a1, b0 - a0


def derive_transposed(h0, h1, h2, h3):
    p0, m0, p1, m1 = h0 + h3, h0 - h3, h1 + h2, h1 - h2
    q = 1.25 * m0 + (0.25 * ROOT5) * m1
    o0 = -1.75 * p0 - 0.25 * p1
    o1 = (1.25 * ROOT5) * p0 - (0.25 * ROOT5) * p1
    return o0 - q, o1 + q, q - o1, -o0 - q


def at(ref, base, node):
    if isinstance(base, int):
        return ref.at[pl.ds(base + node * SUB, SUB), :]
    return ref.at[pl.ds(pl.multiple_of(base, SUB) + node * SUB, SUB), :]


def spread(src_ref, index, dst_ref, base):
    for k in range(SUB):
        block = src_ref[:, k * LANE : (k + 1) * LANE] if index is None else src_ref[index, :, k * LANE : (k + 1) * LANE]
        dst_ref[pl.ds(base + k, NODES, stride=SUB), :] = block


def gather_back(src_ref, base, dst_ref, index):
    for k in range(SUB):
        dst_ref[index, :, k * LANE : (k + 1) * LANE] = src_ref[pl.ds(base + k, NODES, stride=SUB), :]


def places():
    lane = lax.broadcasted_iota(jnp.int32, (SUB, LANE), 1)
    sub = lax.broadcasted_iota(jnp.int32, (SUB, LANE), 0)
    return lane, sub


def assemble(ref, base):
    lane, sub = places()
    zero = jnp.zeros((SUB, LANE), jnp.float32)
    not_first = lane % EX != 0
    not_last = lane % EX != EX - 1
    odd = sub % 2 == 1
    for c in range(4):
        for b in range(4):
            n = 16 * c + 4 * b
            low_at, high_at = at(ref, base, n), at(ref, base, n + 3)
            low, high = low_at[...], high_at[...]
            low_at[...] = low + jnp.where(not_first, pltpu.roll(high, 1, 1), zero)
            high_at[...] = high + jnp.where(not_last, pltpu.roll(low, LANE - 1, 1), zero)
    for c in range(4):
        for a in range(4):
            n = 16 * c + a
            low_at, high_at = at(ref, base, n), at(ref, base, n + 12)
            low, high = low_at[...], high_at[...]
            back = pltpu.roll(high, EX, 1)
            ahead = pltpu.roll(low, LANE - EX, 1)
            back = jnp.where(lane >= EX, back, jnp.where(odd, pltpu.roll(back, 1, 0), zero))
            ahead = jnp.where(lane < LANE - EX, ahead, jnp.where(odd, zero, pltpu.roll(ahead, SUB - 1, 0)))
            low_at[...] = low + back
            high_at[...] = high + ahead
    for n in range(16):
        low_at, high_at = at(ref, base, n), at(ref, base, n + 48)
        low, high = low_at[...], high_at[...]
        low_at[...] = low + jnp.where(sub >= 2, pltpu.roll(high, 2, 0), zero)
        high_at[...] = high + jnp.where(sub < SUB - 2, pltpu.roll(low, SUB - 2, 0), zero)


def roll_sub(value, shift):
    shift = shift % SUB
    return value if shift == 0 else pltpu.roll(value, shift, 0)


def is_even():
    return lax.rem(lax.axis_index("space"), 2) == 0


def pack_faces(ref, base, near_ref, far_ref, out_base):
    _, sub = places()
    even = is_even()
    for b in range(4):
        tiles = []
        for first, shift in ((0, 0), (48, 2)):
            pieces = [roll_sub(at(ref, base, first + 4 * b + a)[...], 2 * a + shift) for a in range(4)]
            tiles.append(
                jnp.where(
                    sub < 4,
                    jnp.where(sub < 2, pieces[0], pieces[1]),
                    jnp.where(sub < 6, pieces[2], pieces[3]),
                )
            )
        low, high = tiles
        at(near_ref, out_base, b)[...] = jnp.where(even, high, low)
        at(far_ref, out_base, b)[...] = jnp.where(even, low, high)


def with_rim(value, node, near_ref, far_ref, rim_base):
    _, sub = places()
    zero = jnp.zeros((SUB, LANE), jnp.float32)
    c, b, a = node // 16, node // 4 % 4, node % 4
    if c not in (0, 3):
        return value
    near, far = at(near_ref, rim_base, b)[...], at(far_ref, rim_base, b)[...]
    if c == 0:
        return value + jnp.where(sub < 2, roll_sub(jnp.where(is_even(), far, near), -2 * a), zero)
    return value + jnp.where(sub >= 6, roll_sub(jnp.where(is_even(), near, far), 6 - 2 * a), zero)


def stiffness(ins, outs, stiff_ref, kern):
    for dim, lines in enumerate(LINES):
        for line in lines:
            stiff = [at(stiff_ref, 0, n)[...] for n in line]
            grads = []
            for (src, sbase), out in zip(ins, outs):
                g = derive(*[at(src, sbase, n)[...] for n in line])
                grads.append(g)
                if out is None:
                    continue
                dst, dbase = out
                back = derive_transposed(*[x * s for x, s in zip(g, stiff)])
                for n, x in zip(line, back):
                    place = at(dst, dbase, n)
                    place[...] = x if dim == 0 else place[...] + x
            if kern is not None:
                for i, n in enumerate(line):
                    place = at(kern, 0, n)
                    place[...] = place[...] + grads[0][i] * grads[1][i]


def place_kernel(
    owner_hbm, local_hbm, weights_hbm, records_hbm, out_ref, token_ref,
    owner_ref, local_ref, weights_ref, records_ref, spot_ref, data_ref, sorted_ref, sems,
):
    copies = [
        pltpu.make_async_copy(src, dst, sems.at[i])
        for i, (src, dst) in enumerate(
            (
                (owner_hbm, owner_ref),
                (local_hbm, local_ref),
                (weights_hbm, weights_ref),
                (records_hbm, records_ref),
            )
        )
    ]
    for copy in copies:
        copy.start()
    token_ref[...] = jnp.zeros_like(token_ref)
    stations = weights_ref.shape[1]
    slabs, rows, _ = out_ref.shape
    events = records_ref.shape[0]
    blocks = stations // LANE
    chunks = stations // CAP
    owner_id = lax.broadcasted_iota(jnp.int32, (slabs, LANE), 0)
    before = lax.broadcasted_iota(jnp.int32, (LANE, LANE), 0) < lax.broadcasted_iota(jnp.int32, (LANE, LANE), 1)
    counting = jnp.concatenate(
        [jnp.where(before, 1.0, 0.0), jnp.ones((LANE, LANE), jnp.float32)], axis=1
    ).astype(jnp.bfloat16)
    copies[0].wait()
    named = [jnp.where(owner_ref[b : b + 1, :] == owner_id, 1.0, 0.0) for b in range(blocks)]
    counts = jnp.dot(
        jnp.concatenate(named, axis=0).astype(jnp.bfloat16), counting, preferred_element_type=jnp.float32
    )
    total = jnp.zeros((slabs, LANE), jnp.float32)
    earlier = []
    for b in range(blocks):
        part = counts[b * slabs : (b + 1) * slabs]
        earlier.append(part[:, :LANE] + total)
        total = total + part[:, LANE:]
    start = jnp.zeros((1, LANE), jnp.float32)
    starts = []
    for slab in range(slabs):
        starts.append(start)
        start = start + total[slab : slab + 1]
    starts = jnp.concatenate(starts, axis=0)
    for b in range(blocks):
        spot_ref[b : b + 1, :] = jnp.sum(named[b] * (earlier[b] + starts), axis=0, keepdims=True)
    first, count = starts.astype(jnp.int32), total.astype(jnp.int32)
    begins = [first[slab, 0] for slab in range(slabs)]
    sizes = [count[slab, 0] for slab in range(slabs)]
    for copy in copies[1:]:
        copy.wait()
    extra = rows - NODES - events * STEPS
    for b in range(blocks):
        cut = slice(b * LANE, (b + 1) * LANE)
        ids = jnp.broadcast_to(local_ref[b : b + 1, :].astype(jnp.float32), (extra, LANE))
        full = jnp.concatenate(
            [weights_ref[:, cut]] + [records_ref[event, :, cut] for event in range(events)] + [ids], axis=0
        )
        high = full.astype(jnp.bfloat16)
        data_ref[:rows, cut] = high
        data_ref[rows:, cut] = (full - high.astype(jnp.float32)).astype(jnp.bfloat16)
    slot = lax.broadcasted_iota(jnp.int32, (CAP, LANE), 0).astype(jnp.bfloat16)
    lane = lax.broadcasted_iota(jnp.int32, (rows, LANE), 1)

    def cut_block(slab):
        begin, size = begins[slab], sizes[slab]
        shift = lax.rem(begin, LANE)
        base = begin - shift
        turn = lax.rem(LANE - shift, LANE)
        turned = [
            pltpu.roll(sorted_ref[:, pl.ds(pl.multiple_of(base + j * LANE, LANE), LANE)], turn, 1) for j in range(3)
        ]
        for j in range(2):
            piece = jnp.where(lane < LANE - shift, turned[j], turned[j + 1])
            out_ref[slab, :, j * LANE : (j + 1) * LANE] = jnp.where(lane + j * LANE < size, piece, 0.0)

    for chunk in range(chunks):
        spots = spot_ref[...] - float(chunk * CAP)
        wanted = jnp.where((spots >= 0.0) & (spots < CAP), spots, -1.0)
        hot = [
            jnp.where(slot == wanted[b : b + 1, :].astype(jnp.bfloat16), jnp.bfloat16(1), jnp.bfloat16(0))
            for b in range(blocks)
        ]
        placed = lax.dot_general(
            data_ref[...],
            jnp.concatenate(hot, axis=1),
            (((1,), (1,)), ((), ())),
            preferred_element_type=jnp.float32,
        )
        sorted_ref[:, chunk * CAP : (chunk + 1) * CAP] = placed[:rows] + placed[rows:]
        cut_block(chunk)
    for slab in range(chunks, slabs):
        cut_block(slab)


def land(got_ref, step, events, out_ref, acc_ref):
    slabs = got_ref.shape[0]
    group = 4
    half = events * NODES
    slot = lax.broadcasted_iota(jnp.int32, (CAP, LANE), 0).astype(jnp.bfloat16)
    acc_ref[...] = jnp.zeros_like(acc_ref)

    def one(g, _):
        left, hot = [], [[] for _ in range(4)]
        for i in range(group):
            src = g * group + i
            weights = got_ref[src, :NODES, :]
            parts = []
            for event in range(events):
                row = NODES + event * STEPS + step
                parts.append(weights * got_ref[src, row : row + 1, :])
            full = jnp.concatenate(parts, axis=0)
            high = full.astype(jnp.bfloat16)
            low = (full - high.astype(jnp.float32)).astype(jnp.bfloat16)
            left.append(jnp.concatenate([high, low], axis=0))
            ids = got_ref[src, NODES + events * STEPS : NODES + events * STEPS + 1, :].astype(jnp.int32)
            for q in range(4):
                for cut in (slice(0, LANE), slice(LANE, 2 * LANE)):
                    wanted = jnp.where(ids[:, cut] // CAP == q, ids[:, cut] % CAP, -1).astype(jnp.float32).astype(jnp.bfloat16)
                    hot[q].append(jnp.where(slot == wanted, jnp.bfloat16(1), jnp.bfloat16(0)))
        left = jnp.concatenate(left, axis=1)
        for q in range(4):
            landed = lax.dot_general(
                left,
                jnp.concatenate(hot[q], axis=1),
                (((1,), (1,)), ((), ())),
                preferred_element_type=jnp.float32,
            )
            cut = slice(q * CAP, (q + 1) * CAP)
            acc_ref[:, cut] += landed[:half] + landed[half:]
        return 0

    lax.fori_loop(0, slabs // group, one, 0)
    for event in range(events):
        for k in range(SUB):
            out_ref[pl.ds(event * FIELD + k, NODES, stride=SUB), :] = acc_ref[
                event * NODES : (event + 1) * NODES, k * LANE : (k + 1) * LANE
            ]


def land_first_kernel(
    events, got_ref, fields_hbm, force_ref, near_ref, far_ref, acc_ref, fields_ref, sem
):
    copy = pltpu.make_async_copy(fields_hbm, fields_ref, sem)
    copy.start()
    land(got_ref, 0, events, force_ref, acc_ref)
    copy.wait()
    for event in range(events):
        for n in range(NODES):
            place = at(force_ref, event * FIELD, n)
            place[...] = at(fields_ref, (events + event) * FIELD, n)[...] - place[...]
        assemble(force_ref, event * FIELD)
        pack_faces(force_ref, event * FIELD, near_ref, far_ref, (events + event) * FACE)
        pack_faces(fields_ref, event * FIELD, near_ref, far_ref, event * FACE)
    pack_faces(fields_ref, 2 * events * FIELD, near_ref, far_ref, 2 * events * FACE)


def land_later_kernel(events, got_ref, out_ref, acc_ref):
    land(got_ref, 1, events, out_ref, acc_ref)


def first_kernel(
    events, fwd_ref, fwd_prev_ref, adj_ref, adj_prev_ref, shear_ref, density_ref, _,
    fields_ref, now_ref, base_ref, stiff_ref, kern_ref, prev_ref,
):
    spread(shear_ref, None, stiff_ref, 0)
    mass = 2 * events * FIELD
    for n in range(NODES):
        place = at(stiff_ref, 0, n)
        place[...] = place[...] * WEIGHT[n]
        at(kern_ref, 0, n)[...] = jnp.zeros((SUB, LANE), jnp.float32)
        at(fields_ref, mass, n)[...] = density_ref[...] * WEIGHT[n]
    assemble(fields_ref, mass)

    def one(event, _):
        u, v = event * FIELD, (events + event) * FIELD
        for now_src, prev_src, base in ((fwd_ref, fwd_prev_ref, u), (adj_ref, adj_prev_ref, v)):
            spread(now_src, event, now_ref, base)
            spread(prev_src, event, prev_ref, 0)
            for n in range(NODES):
                at(base_ref, base, n)[...] = 2.0 * at(now_ref, base, n)[...] - at(prev_ref, 0, n)[...]
        stiffness([(now_ref, u), (now_ref, v)], [(fields_ref, u), (fields_ref, v)], stiff_ref, kern_ref)
        assemble(fields_ref, u)
        return 0

    lax.fori_loop(0, events, one, 0)


def second_kernel(
    events, share, position_ref, fields_ref, force_ref, base_ref, stiff_ref, kern_in_ref, later_ref, near_rim_ref, far_rim_ref,
    new_ref, factor_ref, next_ref, parts_ref, near_ref, far_ref, kern_ref,
):
    kern_ref[...] = kern_in_ref[...]
    mass = 2 * events
    for n in range(NODES):
        at(factor_ref, 0, n)[...] = STEP_SQUARE / with_rim(
            at(fields_ref, mass * FIELD, n)[...], n, near_rim_ref, far_rim_ref, mass * FACE
        )

    def one(event, _):
        u, v = event * FIELD, (events + event) * FIELD
        for base, src_ref, src, rim in ((u, fields_ref, u, event), (v, force_ref, u, events + event)):
            for n in range(NODES):
                force = with_rim(at(src_ref, src, n)[...], n, near_rim_ref, far_rim_ref, rim * FACE)
                at(new_ref, base, n)[...] = at(base_ref, base, n)[...] - at(factor_ref, 0, n)[...] * force
        stiffness([(new_ref, u), (new_ref, v)], [(next_ref, u), (next_ref, v)], stiff_ref, kern_ref)
        for n in range(NODES):
            place = at(next_ref, v, n)
            place[...] = place[...] - at(later_ref, u, n)[...]
        assemble(next_ref, u)
        assemble(next_ref, v)
        pack_faces(next_ref, u, near_ref, far_ref, event * FACE)
        pack_faces(next_ref, v, near_ref, far_ref, (events + event) * FACE)
        return 0

    lax.fori_loop(0, events, one, 0)
    for n in range(NODES):
        place = at(kern_ref, 0, n)
        place[...] = -TIME_STEP * at(stiff_ref, 0, n)[...] * place[...]
    tiles = SUB // share
    for j in range(share):
        owner = lax.rem(position_ref[0] + j, share)
        for k in range(tiles):
            parts_ref[j, :, k * LANE : (k + 1) * LANE] = kern_ref[pl.ds(owner * tiles + k, NODES, stride=SUB), :]


def emit_kernel(events, new_ref, now_ref, fwd_out_ref, adj_out_ref, base_ref):
    def one(event, _):
        u, v = event * FIELD, (events + event) * FIELD
        gather_back(new_ref, u, fwd_out_ref, event)
        gather_back(new_ref, v, adj_out_ref, event)
        for base in (u, v):
            for n in range(NODES):
                at(base_ref, base, n)[...] = 2.0 * at(new_ref, base, n)[...] - at(now_ref, base, n)[...]
        return 0

    lax.fori_loop(0, events, one, 0)


def last_kernel(events, share, base_ref, factor_ref, next_ref, near_rim_ref, far_rim_ref, *rest):
    fwd_out_ref, adj_out_ref, kernel_ref, done_ref = rest[share:]
    total = rest[0][0]
    for part in rest[1:share]:
        total = total + part[0]
    kernel_ref[...] = total

    def one(event, _):
        for field, out_ref in ((event, fwd_out_ref), (events + event, adj_out_ref)):
            for n in range(NODES):
                force = with_rim(at(next_ref, field * FIELD, n)[...], n, near_rim_ref, far_rim_ref, field * FACE)
                at(done_ref, 0, n)[...] = at(base_ref, field * FIELD, n)[...] - at(factor_ref, 0, n)[...] * force
            gather_back(done_ref, 0, out_ref, event)
        return 0

    lax.fori_loop(0, events, one, 0)


def call(body, outs, scratch=(), cost=2_000_000, smem=0, count=0, outside=0, limit=24):
    in_specs = [pl.BlockSpec(memory_space=pltpu.SMEM)] * smem
    in_specs += [pl.BlockSpec(memory_space=pltpu.VMEM)] * (count - smem - outside)
    in_specs += [pl.BlockSpec(memory_space=pl.ANY)] * outside
    return pl.pallas_call(
        body,
        out_shape=[jax.ShapeDtypeStruct(shape, jnp.float32) for shape in outs],
        in_specs=in_specs,
        out_specs=[pl.BlockSpec(memory_space=pltpu.VMEM)] * len(outs),
        scratch_shapes=[x if isinstance(x, pltpu.SemaphoreType) or not isinstance(x, tuple) else pltpu.VMEM(*x) for x in scratch],
        compiler_params=pltpu.CompilerParams(vmem_limit_bytes=limit * 1024 * 1024),
        cost_estimate=pl.CostEstimate(flops=cost, bytes_accessed=cost, transcendentals=0),
    )


def beside(near, far):
    count = lax.axis_size("space")
    inner = [pair for i in range(1, count - 1, 2) for pair in ((i, i + 1), (i + 1, i))]
    from_far = lax.ppermute(far, "space", inner)
    from_near = lax.ppermute(near, "space", [(i, i + 1 - 2 * (i % 2)) for i in range(count)])
    return from_near, from_far


def shards(
    fwd_now,
    fwd_prev,
    adj_now,
    adj_prev,
    shear_mod,
    density,
    station_owner,
    receiver_local,
    station_weights,
    adj_records,
):
    events = fwd_now.shape[0]
    stations = station_owner.shape[0]
    elements = fwd_now.shape[-1]
    slabs = lax.axis_size("space")
    share = lax.axis_size("event")
    f32 = jnp.float32
    rows = -(-(NODES + events * STEPS + 1) // SUB) * SUB
    blocks = stations // LANE

    send, token = call(
        place_kernel,
        [(slabs, rows, CAP), (SUB, LANE)],
        [
            ((blocks, LANE), jnp.int32),
            ((blocks, LANE), jnp.int32),
            ((NODES, stations), f32),
            ((events, STEPS, stations), f32),
            ((blocks, LANE), f32),
            ((2 * rows, stations), jnp.bfloat16),
            ((rows, stations + 3 * LANE), f32),
            pltpu.SemaphoreType.DMA((4,)),
        ],
        count=4,
        outside=4,
        limit=63,
    )(
        station_owner.reshape(blocks, LANE),
        receiver_local.reshape(blocks, LANE),
        station_weights,
        adj_records,
    )
    got = lax.all_to_all(send, "space", split_axis=0, concat_axis=0, tiled=True)

    fields, now, base, stiff, kern = call(
        functools.partial(first_kernel, events),
        [
            ((2 * events + 1) * FIELD, LANE),
            (2 * events * FIELD, LANE),
            (2 * events * FIELD, LANE),
            (FIELD, LANE),
            (FIELD, LANE),
        ],
        [((FIELD, LANE), f32)],
        count=7,
    )(fwd_now, fwd_prev, adj_now, adj_prev, shear_mod, density.reshape(SUB, LANE), token)
    force, near, far = call(
        functools.partial(land_first_kernel, events),
        [(events * FIELD, LANE), ((2 * events + 1) * FACE, LANE), ((2 * events + 1) * FACE, LANE)],
        [
            ((events * NODES, elements), f32),
            (((2 * events + 1) * FIELD, LANE), f32),
            pltpu.SemaphoreType.DMA(()),
        ],
        count=2,
        outside=1,
        limit=LAND_LIMIT,
    )(got, fields)
    near_rim, far_rim = beside(near, far)
    later = call(
        functools.partial(land_later_kernel, events),
        [(events * FIELD, LANE)],
        [((events * NODES, elements), f32)],
        count=1,
    )(got)[0]
    new, factor, after, parts, near, far = call(
        functools.partial(second_kernel, events, share),
        [
            (2 * events * FIELD, LANE),
            (FIELD, LANE),
            (2 * events * FIELD, LANE),
            (share, NODES, elements // share),
            (2 * events * FACE, LANE),
            (2 * events * FACE, LANE),
        ],
        [((FIELD, LANE), f32)],
        smem=1,
        count=9,
    )(
        lax.axis_index("event").reshape(1).astype(jnp.int32),
        fields, force, base, stiff, kern, later, near_rim, far_rim,
    )
    near_rim, far_rim = beside(near, far)
    pieces = [parts[0:1]] + [
        lax.ppermute(parts[j : j + 1], "event", [(i, (i + j) % share) for i in range(share)]) for j in range(1, share)
    ]
    fwd_before, adj_before, base = call(
        functools.partial(emit_kernel, events),
        [fwd_now.shape, adj_now.shape, (2 * events * FIELD, LANE)],
        count=2,
    )(new, now)
    fwd_last, adj_last, kernel = call(
        functools.partial(last_kernel, events, share),
        [fwd_now.shape, adj_now.shape, (NODES, elements // share)],
        [((FIELD, LANE), f32)],
        count=5 + share,
    )(base, factor, after, near_rim, far_rim, *pieces)
    return fwd_last, fwd_before, adj_last, adj_before, kernel


def solution(mesh):
    in_specs = (
        P("event", None, "space"),
        P("event", None, "space"),
        P("event", None, "space"),
        P("event", None, "space"),
        P(None, "space"),
        P("space"),
        P("space", None),
        P("space"),
        P(None, "space"),
        P("event", None, "space"),
    )
    out_specs = (
        P("event", None, "space"),
        P("event", None, "space"),
        P("event", None, "space"),
        P("event", None, "space"),
        P(None, ("space", "event")),
    )
    return jax.shard_map(shards, mesh=mesh, in_specs=in_specs, out_specs=out_specs, check_vma=False)
```

time: 91.2 us -> 67.5 us (0.74)
  starting transfers between devices: 32.3 us -> 15.2 us
  Pallas kernels: 27.6 us -> 20.3 us
    ppermute x8 -> x4, starting transfers between devices: 24.4 us -> 7.38 us  [the longest x2 7.18 us: beside(): from_far = lax.ppermute(far, 'space', inner)]
    pallas_call x5 -> x4, Pallas kernels: 17.3 us -> 10.8 us  [the longest x1 5.44 us: shards(): call(place_kernel, [(slabs, rows, CAP), (SUB, LANE)], [((blocks, LANE), j...]
    all_to_all x1, waiting for transfers between devices: 16.4 us -> 18.2 us  [shards(): got = lax.all_to_all(send, 'space', split_axis=0, concat_axis=0, tiled=True)]
    unnamed x32 -> x30, local copies, waits for them, and re-layouts: 8.62 us -> 10.2 us
    ppermute x8 -> x4, waiting for transfers between devices: 3.02 us -> 1.73 us  [the longest x2 1.72 us: beside(): from_far = lax.ppermute(far, 'space', inner)]
    pallas_call x1, Pallas kernels: 3.06 us -> 2.02 us  [shards(): call(functools.partial(first_kernel, events), [((2 * events + 1) * FIELD,...]
  transfers between devices with their start and end apart: 10 -> 6, of which waited for: 2 -> 3; matrix products, arithmetic and copies ran while one was open for 1% -> 0% of each run, Pallas kernels for 16% -> 10%
where the time goes in v2:
time: 67.5 us; the launch traced here: 66.4 us
  Pallas kernels  20.3 us (30%)
  waiting for transfers between devices  20 us (30%)
  starting transfers between devices  15.2 us (23%)
  local copies, waits for them, and re-layouts  10.2 us (15%)
  between operations  0.77 us (1%)
    all_to_all x1, waiting for transfers between devices, shards(): got = lax.all_to_all(send, 'space', split_axis=0, concat_axis=0, tiled=True)  18.2 us
    unnamed x30, local copies, waits for them, and re-layouts  10.2 us
    ppermute x2, starting transfers between devices, beside(): from_far = lax.ppermute(far, 'space', inner)  7.18 us
    all_to_all x1, starting transfers between devices, shards(): got = lax.all_to_all(send, 'space', split_axis=0, concat_axis=0, tiled=True)  6.57 us
    pallas_call x1, Pallas kernels, shards(): call(place_kernel, [(slabs, rows, CAP), (SUB, LANE)], [((blocks, LANE), j...  5.44 us
    pallas_call x1, Pallas kernels, shards(): call(functools.partial(land_first_kernel, events), [(events * FIELD, LANE...  4.23 us
    pallas_call x1, Pallas kernels, shards(): call(functools.partial(land_later_kernel, events), [(events * FIELD, LANE...  3.21 us
    pallas_call x1, Pallas kernels, shards(): call(functools.partial(second_kernel, events, share), [(2 * events * FIEL...  2.74 us
  transfers between devices with their start and end apart: 6, of which 3 were waited for; matrix products, arithmetic and copies ran while one was open for 0% of the time, Pallas kernels for 10%

profile of v2, /device:TPU:13, one launch (start us, length us, event | category | flops | bytes accessed | tf_op | source)
XLA Modules:
  0.0 66.4 jit_solution(6082732247515407276)
XLA Ops:
  0.6 5.4 %shard_map.137 = (f32[16,72,256]{2,1,0:T(8,128)}, f32[8,128]{1,0:T(8,128)}) custom-call(s32[16,128]{1,0:T(8,128)} %bitcast.5, s32[16,128]{1,0:T(8,128)} %bitcast.6, f32[64,2048]{1,0:T(8,128)} %weights_hbm.1, f32[2,2,2048]{2,1,0:T(2,128)} %records_hbm.1), custom_call_target="tpu_custom_call" | custom-call | flops 2000000 | bytes 2000000 | tf_op jit(solution)/shard_map/pallas_call | solution.py:471
  6.1 0.0 copy-start.13
  6.1 0.0 copy-start.14
  6.1 6.6 %all-to-all-start = ((f32[16,72,256]{2,1,0:T(8,128)}), f32[16,72,256]{2,1,0:T(8,128)S(1)}, u32[]{:S(2)}, u32[]{:S(2)}) async-start(f32[16,72,256]{2,1,0:T(8,128)} %get-tuple-element.29), calls=%async_computation | async-start | bytes 2359296 | tf_op jit(solution)/shard_map/all_to_all | solution.py:493
  12.7 0.0 copy-done.13
  12.7 0.0 copy-done.14
  12.7 0.0 copy-start.4
  12.7 1.0 %copy-done.4 = f32[2,64,1024]{2,1,0:T(8,128)S(1)} copy-done((f32[2,64,1024]{2,1,0:T(8,128)S(1)}, f32[2,64,1024]{2,1,0:T(8,128)}, u32[]{:S(2)}) %copy-start.4) | copy-done | bytes 524312
  13.7 0.0 copy-start.5
  13.7 1.0 %copy-done.5 = f32[2,64,1024]{2,1,0:T(8,128)S(1)} copy-done((f32[2,64,1024]{2,1,0:T(8,128)S(1)}, f32[2,64,1024]{2,1,0:T(8,128)}, u32[]{:S(2)}) %copy-start.5) | copy-done | bytes 524312
  14.8 0.0 copy-start.6
  14.8 1.0 %copy-done.6 = f32[2,64,1024]{2,1,0:T(8,128)S(1)} copy-done((f32[2,64,1024]{2,1,0:T(8,128)S(1)}, f32[2,64,1024]{2,1,0:T(8,128)}, u32[]{:S(2)}) %copy-start.6) | copy-done | bytes 524312
  15.8 0.0 copy-start.7
  15.8 1.0 %copy-done.7 = f32[2,64,1024]{2,1,0:T(8,128)S(1)} copy-done((f32[2,64,1024]{2,1,0:T(8,128)S(1)}, f32[2,64,1024]{2,1,0:T(8,128)}, u32[]{:S(2)}) %copy-start.7) | copy-done | bytes 524312
  16.9 0.0 copy-start.8
  16.9 0.9 %copy-done.8 = f32[64,1024]{1,0:T(8,128)S(1)} copy-done((f32[64,1024]{1,0:T(8,128)S(1)}, f32[64,1024]{1,0:T(8,128)}, u32[]{:S(2)}) %copy-start.8) | copy-done | bytes 262168
  17.8 2.0 %shard_map.138 = (f32[2560,128]{1,0:T(8,128)S(1)}, f32[2048,128]{1,0:T(8,128)S(1)}, f32[2048,128]{1,0:T(8,128)S(1)}, f32[512,128]{1,0:T(8,128)S(1)}, f32[512,128]{1,0:T(8,128)S(1)}) custom-call(f32[2,64,1024]{2,1,0:T(8,128)S(1)} %copy-done.4, f32[2,64,1024]{2,1,0:T(8,128)S(1)} %copy-done.5, f32[2,64,1024]{2,1,0:T(8,128)S(1)} %copy-done.6, ...), custom_call_target="tpu_custom_call" | custom-call | flops 2000000 | bytes 2000000 | tf_op jit(solution)/shard_map/pallas_call | solution.py:495
  19.8 0.0 copy-start
  19.8 1.0 %copy-done = f32[2048,128]{1,0:T(8,128)} copy-done((f32[2048,128]{1,0:T(8,128)}, f32[2048,128]{1,0:T(8,128)S(1)}, u32[]{:S(2)}) %copy-start) | copy-done | bytes 1048600
  20.8 0.0 copy-start.9
  20.8 0.7 %copy-done.9 = f32[512,128]{1,0:T(8,128)} copy-done((f32[512,128]{1,0:T(8,128)}, f32[512,128]{1,0:T(8,128)S(1)}, u32[]{:S(2)}) %copy-start.9) | copy-done | bytes 262168
  21.5 0.0 copy-start.11
  21.5 0.7 %copy-done.11 = f32[512,128]{1,0:T(8,128)} copy-done((f32[512,128]{1,0:T(8,128)}, f32[512,128]{1,0:T(8,128)S(1)}, u32[]{:S(2)}) %copy-start.11) | copy-done | bytes 262168
  22.2 18.2 %all-to-all-done.got_ref = f32[16,72,256]{2,1,0:T(8,128)S(1)} async-done(((f32[16,72,256]{2,1,0:T(8,128)}), f32[16,72,256]{2,1,0:T(8,128)S(1)}, u32[]{:S(2)}, u32[]{:S(2)}) %all-to-all-start) | async-done | bytes 1179680 | tf_op jit(solution)/shard_map/all_to_all | solution.py:493
  40.4 4.2 %shard_map.139 = (f32[1024,128]{1,0:T(8,128)S(1)}, f32[160,128]{1,0:T(8,128)}, f32[160,128]{1,0:T(8,128)}) custom-call(f32[16,72,256]{2,1,0:T(8,128)S(1)} %all-to-all-done.got_ref, f32[2560,128]{1,0:T(8,128)S(1)} %get-tuple-element.28.fields_hbm.fields_ref), custom_call_target="tpu_custom_call" | custom-call | flops 2000000 | bytes 2000000 | tf_op jit(solution)/shard_map/pallas_call | solution.py:507
  44.7 0.0 copy-start.2
  44.7 0.8 %copy-done.2 = f32[1024,128]{1,0:T(8,128)} copy-done((f32[1024,128]{1,0:T(8,128)}, f32[1024,128]{1,0:T(8,128)S(1)}, u32[]{:S(2)}) %copy-start.2) | copy-done | bytes 524312
  45.5 0.2 collective-permute-start
  45.7 3.3 %collective-permute-start.1 = (f32[160,128]{1,0:T(8,128)}, f32[160,128]{1,0:T(8,128)}, u32[]{:S(2)}, u32[]{:S(2)}) collective-permute-start(f32[160,128]{1,0:T(8,128)} %get-tuple-element.35), channel_id=1, source_target_pairs={{2,4},{4,2},{6,8},{8,6},{10,12},{12,10},{14,16},{16,14},{18,20},{2... | collective-permute-start | bytes 245768 | tf_op jit(solution)/shard_map/ppermute | solution.py:445
  49.0 0.0 copy-start.1
  49.0 0.0 copy-start.3
  49.0 3.2 %shard_map.140.later_ref = f32[1024,128]{1,0:T(8,128)S(1)} custom-call(f32[16,72,256]{2,1,0:T(8,128)S(1)} %all-to-all-done.got_ref), custom_call_target="tpu_custom_call" | custom-call | flops 2000000 | bytes 2000000 | tf_op jit(solution)/shard_map/pallas_call | solution.py:520
  52.3 0.0 collective-permute-done.near_rim_ref
  52.3 0.4 collective-permute-done.1.far_rim_ref
  52.6 0.0 copy-done.1
  52.6 0.0 copy-done.3
  52.6 0.0 copy-start.10
  52.6 0.9 %copy-done.10 = f32[512,128]{1,0:T(8,128)S(1)} copy-done((f32[512,128]{1,0:T(8,128)S(1)}, f32[512,128]{1,0:T(8,128)}, u32[]{:S(2)}) %copy-start.10) | copy-done | bytes 262168
  53.6 0.0 copy-start.12
  53.6 0.9 %copy-done.12 = f32[512,128]{1,0:T(8,128)S(1)} copy-done((f32[512,128]{1,0:T(8,128)S(1)}, f32[512,128]{1,0:T(8,128)}, u32[]{:S(2)}) %copy-start.12) | copy-done | bytes 262168
  54.5 2.7 %shard_map.141 = (f32[2048,128]{1,0:T(8,128)S(1)}, f32[512,128]{1,0:T(8,128)S(1)}, f32[2048,128]{1,0:T(8,128)S(1)}, f32[2,64,512]{2,1,0:T(8,128)S(1)}, f32[128,128]{1,0:T(8,128)S(1)}, /*index=5*/f32[128,128]{1,0:T(8,128)S(1)}) custom-call(s32[1]{0:T(128)} %bitcast.position_ref, f32[2560,128]{1,0:T(8,128)S(1)} %get-tuple-element.28.fields_hbm.fields_ref, ...), custom_call_target="tpu_custom_call" | custom-call | flops 2000000 | bytes 2000000 | tf_op jit(solution)/shard_map/pallas_call | solution.py:526
  57.3 1.3 %collective-permute-start.4 = (f32[1,64,512]{2,1,0:T(8,128)S(1)}, f32[1,64,512]{2,1,0:T(8,128)S(1)}, u32[]{:S(2)}, u32[]{:S(2)}) collective-permute-start(f32[1,64,512]{2,1,0:T(8,128)S(1)} %get-tuple-element.49), channel_id=1, source_target_pairs={{0,1},{1,0},{2,3},{3,2},{4,5},{5,4},{6,7},{7,6},{8,9},{9,8},{10,11... | collective-permute-start | bytes 393224 | tf_op jit(solution)/shard_map/ppermute | solution.py:545
  58.6 0.0 collective-permute-start.2
  58.6 3.8 %collective-permute-start.3 = (f32[128,128]{1,0:T(8,128)S(1)}, f32[128,128]{1,0:T(8,128)S(1)}, u32[]{:S(2)}, u32[]{:S(2)}) collective-permute-start(f32[128,128]{1,0:T(8,128)S(1)} %get-tuple-element.42), channel_id=1, source_target_pairs={{2,4},{4,2},{6,8},{8,6},{10,12},{12,10},{14,16},{16,14},{18,20},{2... | collective-permute-start | bytes 196616 | tf_op jit(solution)/shard_map/ppermute | solution.py:445
  62.4 1.3 %shard_map.142 = (f32[2,64,1024]{2,1,0:T(8,128)}, f32[2,64,1024]{2,1,0:T(8,128)}, f32[2048,128]{1,0:T(8,128)S(1)}) custom-call(f32[2048,128]{1,0:T(8,128)S(1)} %get-tuple-element.36.new_ref, f32[2048,128]{1,0:T(8,128)S(1)} %get-tuple-element.37.now_ref), custom_call_target="tpu_custom_call" | custom-call | flops 2000000 | bytes 2000000 | tf_op jit(solution)/shard_map/pallas_call | solution.py:547
  63.7 0.0 collective-permute-done.2.near_rim_ref
  63.7 1.4 %collective-permute-done.3.far_rim_ref = f32[128,128]{1,0:T(8,128)S(1)} collective-permute-done((f32[128,128]{1,0:T(8,128)S(1)}, f32[128,128]{1,0:T(8,128)S(1)}, u32[]{:S(2)}, u32[]{:S(2)}) %collective-permute-start.3) | collective-permute-done | bytes 65568 | tf_op jit(solution)/shard_map/ppermute | solution.py:445
  65.0 0.0 collective-permute-done.4.rest_1_
  65.1 1.4 %shard_map.143 = (f32[2,64,1024]{2,1,0:T(8,128)}, f32[2,64,1024]{2,1,0:T(8,128)}, f32[64,512]{1,0:T(8,128)}) custom-call(f32[2048,128]{1,0:T(8,128)S(1)} %get-tuple-element.38.base_ref, f32[512,128]{1,0:T(8,128)S(1)} %get-tuple-element.39.factor_ref, f32[2048,128]{1,0:T(8,128)S(1)} %get-tuple-element.40.next_ref, ...), custom_call_target="tpu_custom_call" | custom-call | flops 2000000 | bytes 2000000 | tf_op jit(solution)/shard_map/pallas_call | solution.py:552
  (1 shorter events, 0.0 us)
Async XLA Ops:
  6.1 6.6 %copy-start.13 = (f32[1024]{0:T(1024)S(1)}, f32[1024]{0:T(1024)}, u32[]{:S(2)}) copy-start(f32[1024]{0:T(1024)} %param.15) | copy-start | bytes 12292
  6.1 6.6 %copy-start.14 = (f32[8,128]{1,0:T(8,128)S(1)}, f32[8,128]{1,0:T(8,128)}, u32[]{:S(2)}) copy-start(f32[8,128]{1,0:T(8,128)} %get-tuple-element.27._) | copy-start | bytes 12292
  6.1 34.3 %all-to-all-start = ((f32[16,72,256]{2,1,0:T(8,128)}), f32[16,72,256]{2,1,0:T(8,128)S(1)}, u32[]{:S(2)}, u32[]{:S(2)}) async-start(f32[16,72,256]{2,1,0:T(8,128)} %get-tuple-element.29), calls=%async_computation | async-start | bytes 2359296 | tf_op jit(solution)/shard_map/all_to_all | solution.py:493
  12.7 1.0 %copy-start.4 = (f32[2,64,1024]{2,1,0:T(8,128)S(1)}, f32[2,64,1024]{2,1,0:T(8,128)}, u32[]{:S(2)}) copy-start(f32[2,64,1024]{2,1,0:T(8,128)} %fwd_ref.1) | copy-start | bytes 1572868
  13.7 1.0 %copy-start.5 = (f32[2,64,1024]{2,1,0:T(8,128)S(1)}, f32[2,64,1024]{2,1,0:T(8,128)}, u32[]{:S(2)}) copy-start(f32[2,64,1024]{2,1,0:T(8,128)} %fwd_prev_ref.1) | copy-start | bytes 1572868
  14.8 1.0 %copy-start.6 = (f32[2,64,1024]{2,1,0:T(8,128)S(1)}, f32[2,64,1024]{2,1,0:T(8,128)}, u32[]{:S(2)}) copy-start(f32[2,64,1024]{2,1,0:T(8,128)} %adj_ref.1) | copy-start | bytes 1572868
  15.8 1.0 %copy-start.7 = (f32[2,64,1024]{2,1,0:T(8,128)S(1)}, f32[2,64,1024]{2,1,0:T(8,128)}, u32[]{:S(2)}) copy-start(f32[2,64,1024]{2,1,0:T(8,128)} %adj_prev_ref.1) | copy-start | bytes 1572868
  16.9 0.9 %copy-start.8 = (f32[64,1024]{1,0:T(8,128)S(1)}, f32[64,1024]{1,0:T(8,128)}, u32[]{:S(2)}) copy-start(f32[64,1024]{1,0:T(8,128)} %shear_ref.1) | copy-start | bytes 786436
  19.8 1.0 %copy-start = (f32[2048,128]{1,0:T(8,128)}, f32[2048,128]{1,0:T(8,128)S(1)}, u32[]{:S(2)}) copy-start(f32[2048,128]{1,0:T(8,128)S(1)} %get-tuple-element.31.base_ref) | copy-start | bytes 3145732
  20.8 0.7 %copy-start.9 = (f32[512,128]{1,0:T(8,128)}, f32[512,128]{1,0:T(8,128)S(1)}, u32[]{:S(2)}) copy-start(f32[512,128]{1,0:T(8,128)S(1)} %get-tuple-element.32.stiff_ref) | copy-start | bytes 786436
  21.5 0.7 %copy-start.11 = (f32[512,128]{1,0:T(8,128)}, f32[512,128]{1,0:T(8,128)S(1)}, u32[]{:S(2)}) copy-start(f32[512,128]{1,0:T(8,128)S(1)} %get-tuple-element.33.kern_in_ref) | copy-start | bytes 786436
  44.7 0.8 %copy-start.2 = (f32[1024,128]{1,0:T(8,128)}, f32[1024,128]{1,0:T(8,128)S(1)}, u32[]{:S(2)}) copy-start(f32[1024,128]{1,0:T(8,128)S(1)} %get-tuple-element.30.force_ref) | copy-start | bytes 1572868
  45.5 6.8 %collective-permute-start = (f32[160,128]{1,0:T(8,128)}, f32[160,128]{1,0:T(8,128)}, u32[]{:S(2)}, u32[]{:S(2)}) collective-permute-start(f32[160,128]{1,0:T(8,128)} %get-tuple-element.34), channel_id=1, source_target_pairs={{0,2},{2,0},{4,6},{6,4},{8,10},{10,8},{12,14},{14,12},{16,18},{18,... | collective-permute-start | bytes 245768 | tf_op jit(solution)/shard_map/ppermute | solution.py:446
  45.7 7.0 %collective-permute-start.1 = (f32[160,128]{1,0:T(8,128)}, f32[160,128]{1,0:T(8,128)}, u32[]{:S(2)}, u32[]{:S(2)}) collective-permute-start(f32[160,128]{1,0:T(8,128)} %get-tuple-element.35), channel_id=1, source_target_pairs={{2,4},{4,2},{6,8},{8,6},{10,12},{12,10},{14,16},{16,14},{18,20},{2... | collective-permute-start | bytes 245768 | tf_op jit(solution)/shard_map/ppermute | solution.py:445
  49.0 3.6 %copy-start.1 = (f32[2048,128]{1,0:T(8,128)S(1)}, f32[2048,128]{1,0:T(8,128)}, u32[]{:S(2)}) copy-start(f32[2048,128]{1,0:T(8,128)} %copy-done) | copy-start | bytes 3145732
  49.0 3.6 %copy-start.3 = (f32[1024,128]{1,0:T(8,128)S(1)}, f32[1024,128]{1,0:T(8,128)}, u32[]{:S(2)}) copy-start(f32[1024,128]{1,0:T(8,128)} %copy-done.2) | copy-start | bytes 1572868
  52.6 1.0 %copy-start.10 = (f32[512,128]{1,0:T(8,128)S(1)}, f32[512,128]{1,0:T(8,128)}, u32[]{:S(2)}) copy-start(f32[512,128]{1,0:T(8,128)} %copy-done.9) | copy-start | bytes 786436
  53.6 0.9 %copy-start.12 = (f32[512,128]{1,0:T(8,128)S(1)}, f32[512,128]{1,0:T(8,128)}, u32[]{:S(2)}) copy-start(f32[512,128]{1,0:T(8,128)} %copy-done.11) | copy-start | bytes 786436
  57.3 7.8 %collective-permute-start.4 = (f32[1,64,512]{2,1,0:T(8,128)S(1)}, f32[1,64,512]{2,1,0:T(8,128)S(1)}, u32[]{:S(2)}, u32[]{:S(2)}) collective-permute-start(f32[1,64,512]{2,1,0:T(8,128)S(1)} %get-tuple-element.49), channel_id=1, source_target_pairs={{0,1},{1,0},{2,3},{3,2},{4,5},{5,4},{6,7},{7,6},{8,9},{9,8},{10,11... | collective-permute-start | bytes 393224 | tf_op jit(solution)/shard_map/ppermute | solution.py:545
  58.6 5.1 %collective-permute-start.2 = (f32[128,128]{1,0:T(8,128)S(1)}, f32[128,128]{1,0:T(8,128)S(1)}, u32[]{:S(2)}, u32[]{:S(2)}) collective-permute-start(f32[128,128]{1,0:T(8,128)S(1)} %get-tuple-element.41), channel_id=1, source_target_pairs={{0,2},{2,0},{4,6},{6,4},{8,10},{10,8},{12,14},{14,12},{16,18},{18,... | collective-permute-start | bytes 196616 | tf_op jit(solution)/shard_map/ppermute | solution.py:446
  58.6 6.5 %collective-permute-start.3 = (f32[128,128]{1,0:T(8,128)S(1)}, f32[128,128]{1,0:T(8,128)S(1)}, u32[]{:S(2)}, u32[]{:S(2)}) collective-permute-start(f32[128,128]{1,0:T(8,128)S(1)} %get-tuple-element.42), channel_id=1, source_target_pairs={{2,4},{4,2},{6,8},{8,6},{10,12},{12,10},{14,16},{16,14},{18,20},{2... | collective-permute-start | bytes 196616 | tf_op jit(solution)/shard_map/ppermute | solution.py:445

commit v3 on v2

--- a/solution.py
+++ b/solution.py
@@ -17,7 +17,6 @@
 LANE = 128
 FIELD = NODES * SUB
 FACE = 4 * SUB
-LAND_LIMIT = 24
 
 
 TIME_STEP = 0.08
@@ -74,20 +73,20 @@
     return lane, sub
 
 
-def assemble(ref, base):
+def assemble_layers(ref, base, planes):
     lane, sub = places()
     zero = jnp.zeros((SUB, LANE), jnp.float32)
     not_first = lane % EX != 0
     not_last = lane % EX != EX - 1
     odd = sub % 2 == 1
-    for c in range(4):
+    for c in range(planes):
         for b in range(4):
             n = 16 * c + 4 * b
             low_at, high_at = at(ref, base, n), at(ref, base, n + 3)
             low, high = low_at[...], high_at[...]
             low_at[...] = low + jnp.where(not_first, pltpu.roll(high, 1, 1), zero)
             high_at[...] = high + jnp.where(not_last, pltpu.roll(low, LANE - 1, 1), zero)
-    for c in range(4):
+    for c in range(planes):
         for a in range(4):
             n = 16 * c + a
             low_at, high_at = at(ref, base, n), at(ref, base, n + 12)
@@ -98,6 +97,12 @@
             ahead = jnp.where(lane < LANE - EX, ahead, jnp.where(odd, zero, pltpu.roll(ahead, SUB - 1, 0)))
             low_at[...] = low + back
             high_at[...] = high + ahead
+
+
+def assemble(ref, base):
+    _, sub = places()
+    zero = jnp.zeros((SUB, LANE), jnp.float32)
+    assemble_layers(ref, base, 4)
     for n in range(16):
         low_at, high_at = at(ref, base, n), at(ref, base, n + 48)
         low, high = low_at[...], high_at[...]
@@ -114,23 +119,17 @@
     return lax.rem(lax.axis_index("space"), 2) == 0
 
 
-def pack_faces(ref, base, near_ref, far_ref, out_base):
+def face_tiles(ref, base, b, low_first, high_first):
     _, sub = places()
-    even = is_even()
-    for b in range(4):
-        tiles = []
-        for first, shift in ((0, 0), (48, 2)):
-            pieces = [roll_sub(at(ref, base, first + 4 * b + a)[...], 2 * a + shift) for a in range(4)]
-            tiles.append(
-                jnp.where(
-                    sub < 4,
-                    jnp.where(sub < 2, pieces[0], pieces[1]),
-                    jnp.where(sub < 6, pieces[2], pieces[3]),
-                )
+    tiles = []
+    for first, shift in ((low_first, 0), (high_first, 2)):
+        pieces = [roll_sub(at(ref, base, first + 4 * b + a)[...], 2 * a + shift) for a in range(4)]
+        tiles.append(
+            jnp.where(
+                sub < 4, jnp.where(sub < 2, pieces[0], pieces[1]), jnp.where(sub < 6, pieces[2], pieces[3])
             )
-        low, high = tiles
-        at(near_ref, out_base, b)[...] = jnp.where(even, high, low)
-        at(far_ref, out_base, b)[...] = jnp.where(even, low, high)
+        )
+    return tiles
 
 
 def with_rim(value, node, near_ref, far_ref, rim_base):
@@ -262,124 +261,232 @@
         cut_block(slab)
 
 
-def land(got_ref, step, events, out_ref, acc_ref):
+def split(full):
+    high = full.astype(jnp.bfloat16)
+    return jnp.concatenate([high, (full - high.astype(jnp.float32)).astype(jnp.bfloat16)], axis=0)
+
+
+def land(got_ref, events, wants, acc_refs):
     slabs = got_ref.shape[0]
-    group = 4
-    half = events * NODES
+    group = min(slabs, 16)
     slot = lax.broadcasted_iota(jnp.int32, (CAP, LANE), 0).astype(jnp.bfloat16)
-    acc_ref[...] = jnp.zeros_like(acc_ref)
+    if slabs > group:
+        for acc_ref in acc_refs:
+            acc_ref[...] = jnp.zeros_like(acc_ref)
 
     def one(g, _):
-        left, hot = [], [[] for _ in range(4)]
+        items = {item: [] for _, chosen in wants for item in chosen}
+        hot = [[] for _ in wants]
         for i in range(group):
             src = g * group + i
-            weights = got_ref[src, :NODES, :]
-            parts = []
-            for event in range(events):
-                row = NODES + event * STEPS + step
-                parts.append(weights * got_ref[src, row : row + 1, :])
-            full = jnp.concatenate(parts, axis=0)
-            high = full.astype(jnp.bfloat16)
-            low = (full - high.astype(jnp.float32)).astype(jnp.bfloat16)
-            left.append(jnp.concatenate([high, low], axis=0))
+            for (first, last, step), found in items.items():
+                weights = got_ref[src, first:last, :]
+                rows = [NODES + event * STEPS + step for event in range(events)]
+                found.append(
+                    split(jnp.concatenate([weights * got_ref[src, row : row + 1, :] for row in rows], axis=0))
+                )
             ids = got_ref[src, NODES + events * STEPS : NODES + events * STEPS + 1, :].astype(jnp.int32)
-            for q in range(4):
+            for at_hot, (quarter, _) in zip(hot, wants):
+                wanted = jnp.where(ids // CAP == quarter, ids % CAP, -1).astype(jnp.float32).astype(jnp.bfloat16)
                 for cut in (slice(0, LANE), slice(LANE, 2 * LANE)):
-                    wanted = jnp.where(ids[:, cut] // CAP == q, ids[:, cut] % CAP, -1).astype(jnp.float32).astype(jnp.bfloat16)
-                    hot[q].append(jnp.where(slot == wanted, jnp.bfloat16(1), jnp.bfloat16(0)))
-        left = jnp.concatenate(left, axis=1)
-        for q in range(4):
+                    at_hot.append(jnp.where(slot == wanted[:, cut], jnp.bfloat16(1), jnp.bfloat16(0)))
+        left = {item: jnp.concatenate(found, axis=1) for item, found in items.items()}
+        for at_hot, (_, chosen), acc_ref in zip(hot, wants, acc_refs):
             landed = lax.dot_general(
-                left,
-                jnp.concatenate(hot[q], axis=1),
+                jnp.concatenate([left[item] for item in chosen], axis=0),
+                jnp.concatenate(at_hot, axis=1),
                 (((1,), (1,)), ((), ())),
                 preferred_element_type=jnp.float32,
             )
-            cut = slice(q * CAP, (q + 1) * CAP)
-            acc_ref[:, cut] += landed[:half] + landed[half:]
+            at_in, at_out = 0, 0
+            for first, last, _ in chosen:
+                count = events * (last - first)
+                rows = slice(at_out, at_out + count)
+                both = landed[at_in : at_in + count] + landed[at_in + count : at_in + 2 * count]
+                acc_ref[rows, :] = acc_ref[rows, :] + both if slabs > group else both
+                at_in, at_out = at_in + 2 * count, at_out + count
         return 0
 
-    lax.fori_loop(0, slabs // group, one, 0)
+    if slabs > group:
+        lax.fori_loop(0, slabs // group, one, 0)
+    else:
+        one(0, 0)
+
+
+FACE_WANTS = ((0, ((0, 16, 0),)), (3, ((48, 64, 0),)))
+FIRST_WANTS = (
+    (0, ((0, NODES, 0), (0, 16, 1))),
+    (1, ((0, NODES, 0),)),
+    (2, ((0, NODES, 0),)),
+    (3, ((0, NODES, 0), (48, 64, 1))),
+)
+LATER_WANTS = tuple((q, ((0, NODES, 1),)) for q in range(4))
+
+
+def sums(events, wants):
+    return [
+        ((sum(events * (last - first) for first, last, _ in chosen), CAP), jnp.float32) for _, chosen in wants
+    ]
+
+
+def spread_source(events, acc_refs, out_ref):
     for event in range(events):
         for k in range(SUB):
-            out_ref[pl.ds(event * FIELD + k, NODES, stride=SUB), :] = acc_ref[
-                event * NODES : (event + 1) * NODES, k * LANE : (k + 1) * LANE
-            ]
+            cut = slice(k % 2 * LANE, (k % 2 + 1) * LANE)
+            out_ref[pl.ds(event * FIELD + k, NODES, stride=SUB), :] = acc_refs[k // 2][event * NODES : (event + 1) * NODES, cut]
+        assemble(out_ref, event * FIELD)
+
+
+def spread_faces(events, low_ref, high_ref, skip, out_ref):
+    out_ref[...] = jnp.zeros_like(out_ref)
+    for event in range(events):
+        rows = slice(skip + event * 16, skip + (event + 1) * 16)
+        for j in range(2):
+            cut = slice(j * LANE, (j + 1) * LANE)
+            out_ref[pl.ds(event * 16 * SUB + j, 16, stride=SUB), :] = low_ref[rows, cut]
+            out_ref[pl.ds(event * 16 * SUB + SUB - 2 + j, 16, stride=SUB), :] = high_ref[rows, cut]
+        assemble_layers(out_ref, event * 16 * SUB, 1)
+
+
+def land_faces_kernel(events, got_ref, faces_hbm, near_ref, far_ref, faces_ref, source_ref, low_ref, high_ref, sem):
+    copy = pltpu.make_async_copy(faces_hbm, faces_ref, sem)
+    copy.start()
+    land(got_ref, events, FACE_WANTS, (low_ref, high_ref))
+    spread_faces(events, low_ref, high_ref, 0, source_ref)
+    copy.wait()
+    even = is_even()
+    fields = 2 * events + 1
+    for field in range(fields):
+        for b in range(4):
+            low = at(faces_ref, field * FACE, b)[...]
+            high = at(faces_ref, (fields + field) * FACE, b)[...]
+            if events <= field < 2 * events:
+                source_low, source_high = face_tiles(source_ref, (field - events) * 16 * SUB, b, 0, 0)
+                low, high = low - source_low, high - source_high
+            at(near_ref, field * FACE, b)[...] = jnp.where(even, high, low)
+            at(far_ref, field * FACE, b)[...] = jnp.where(even, low, high)
+
+
+def state_rows(events):
+    counts = {"force": 2 * events, "mass": 1, "base": 2 * events, "stiff": 1, "kern": 1}
+    rows, total = {}, 0
+    for name, count in counts.items():
+        rows[name] = total * FIELD
+        total += count
+    return rows, total * FIELD
 
 
 def land_first_kernel(
-    events, got_ref, fields_hbm, force_ref, near_ref, far_ref, acc_ref, fields_ref, sem
+    events, got_ref, state_hbm, now_hbm, state_ref, now_ref, later_ref, source_ref, acc0, acc1, acc2, acc3, sems
 ):
-    copy = pltpu.make_async_copy(fields_hbm, fields_ref, sem)
-    copy.start()
-    land(got_ref, 0, events, force_ref, acc_ref)
-    copy.wait()
+    copies = [
+        pltpu.make_async_copy(state_hbm, state_ref, sems.at[0]),
+        pltpu.make_async_copy(now_hbm, now_ref, sems.at[1]),
+    ]
+    for copy in copies:
+        copy.start()
+    land(got_ref, events, FIRST_WANTS, (acc0, acc1, acc2, acc3))
+    spread_source(events, (acc0, acc1, acc2, acc3), source_ref)
+    spread_faces(events, acc0, acc3, events * NODES, later_ref)
+    for copy in copies:
+        copy.wait()
+    rows, _ = state_rows(events)
     for event in range(events):
         for n in range(NODES):
-            place = at(force_ref, event * FIELD, n)
-            place[...] = at(fields_ref, (events + event) * FIELD, n)[...] - place[...]
-        assemble(force_ref, event * FIELD)
-        pack_faces(force_ref, event * FIELD, near_ref, far_ref, (events + event) * FACE)
-        pack_faces(fields_ref, event * FIELD, near_ref, far_ref, event * FACE)
-    pack_faces(fields_ref, 2 * events * FIELD, near_ref, far_ref, 2 * events * FACE)
-
-
-def land_later_kernel(events, got_ref, out_ref, acc_ref):
-    land(got_ref, 1, events, out_ref, acc_ref)
+            place = at(state_ref, rows["force"] + (events + event) * FIELD, n)
+            place[...] = place[...] - at(source_ref, event * FIELD, n)[...]
+
+
+def land_later_kernel(
+    events, got_ref, new_ref, fwd_hbm, adj_hbm, source_ref, out_ref, acc0, acc1, acc2, acc3, sems
+):
+    copies = []
+    for event in range(events):
+        for field, out_hbm in ((event, fwd_hbm), (events + event, adj_hbm)):
+            gather_back(new_ref, field * FIELD, out_ref, field)
+            copies.append(pltpu.make_async_copy(out_ref.at[field], out_hbm.at[event], sems.at[field]))
+            copies[-1].start()
+    land(got_ref, events, LATER_WANTS, (acc0, acc1, acc2, acc3))
+    spread_source(events, (acc0, acc1, acc2, acc3), source_ref)
+    for copy in copies:
+        copy.wait()
 
 
 def first_kernel(
-    events, fwd_ref, fwd_prev_ref, adj_ref, adj_prev_ref, shear_ref, density_ref, _,
-    fields_ref, now_ref, base_ref, stiff_ref, kern_ref, prev_ref,
+    events, fwd_ref, fwd_prev_ref, adj_ref, adj_prev_ref, shear_ref, density_ref, _, state_ref, now_ref, faces_ref, prev_ref
 ):
-    spread(shear_ref, None, stiff_ref, 0)
-    mass = 2 * events * FIELD
+    rows, _ = state_rows(events)
+    stiff_ref, kern_ref = (state_ref.at[pl.ds(rows[name], FIELD), :] for name in ("stiff", "kern"))
+    spread(shear_ref, None, state_ref, rows["stiff"])
     for n in range(NODES):
         place = at(stiff_ref, 0, n)
         place[...] = place[...] * WEIGHT[n]
         at(kern_ref, 0, n)[...] = jnp.zeros((SUB, LANE), jnp.float32)
-        at(fields_ref, mass, n)[...] = density_ref[...] * WEIGHT[n]
-    assemble(fields_ref, mass)
+        at(state_ref, rows["mass"], n)[...] = density_ref[...] * WEIGHT[n]
 
     def one(event, _):
         u, v = event * FIELD, (events + event) * FIELD
-        for now_src, prev_src, base in ((fwd_ref, fwd_prev_ref, u), (adj_ref, adj_prev_ref, v)):
-            spread(now_src, event, now_ref, base)
+        for now_src, prev_src, field in ((fwd_ref, fwd_prev_ref, u), (adj_ref, adj_prev_ref, v)):
+            spread(now_src, event, now_ref, field)
             spread(prev_src, event, prev_ref, 0)
             for n in range(NODES):
-                at(base_ref, base, n)[...] = 2.0 * at(now_ref, base, n)[...] - at(prev_ref, 0, n)[...]
-        stiffness([(now_ref, u), (now_ref, v)], [(fields_ref, u), (fields_ref, v)], stiff_ref, kern_ref)
-        assemble(fields_ref, u)
+                at(state_ref, rows["base"] + field, n)[...] = 2.0 * at(now_ref, field, n)[...] - at(prev_ref, 0, n)[...]
+        stiffness(
+            [(now_ref, u), (now_ref, v)],
+            [(state_ref, rows["force"] + u), (state_ref, rows["force"] + v)],
+            stiff_ref,
+            kern_ref,
+        )
         return 0
 
     lax.fori_loop(0, events, one, 0)
+    fields = 2 * events + 1
+
+    def join(field, _):
+        assemble(state_ref, rows["force"] + field * FIELD)
+        for b in range(4):
+            low, high = face_tiles(state_ref, rows["force"] + field * FIELD, b, 0, 48)
+            at(faces_ref, field * FACE, b)[...] = low
+            at(faces_ref, (fields + field) * FACE, b)[...] = high
+        return 0
+
+    lax.fori_loop(0, fields, join, 0)
 
 
 def second_kernel(
-    events, share, position_ref, fields_ref, force_ref, base_ref, stiff_ref, kern_in_ref, later_ref, near_rim_ref, far_rim_ref,
-    new_ref, factor_ref, next_ref, parts_ref, near_ref, far_ref, kern_ref,
+    events, share, position_ref, state_ref, now_ref, later_ref, near_rim_ref, far_rim_ref,
+    new_ref, base_ref, factor_ref, next_ref, parts_ref, near_ref, far_ref, kern_ref,
 ):
-    kern_ref[...] = kern_in_ref[...]
+    rows, _ = state_rows(events)
+    stiff_ref = state_ref.at[pl.ds(rows["stiff"], FIELD), :]
+    kern_ref[...] = state_ref[pl.ds(rows["kern"], FIELD), :]
     mass = 2 * events
+    even = is_even()
     for n in range(NODES):
         at(factor_ref, 0, n)[...] = STEP_SQUARE / with_rim(
-            at(fields_ref, mass * FIELD, n)[...], n, near_rim_ref, far_rim_ref, mass * FACE
+            at(state_ref, rows["mass"], n)[...], n, near_rim_ref, far_rim_ref, mass * FACE
         )
 
     def one(event, _):
         u, v = event * FIELD, (events + event) * FIELD
-        for base, src_ref, src, rim in ((u, fields_ref, u, event), (v, force_ref, u, events + event)):
+        for field, rim in ((u, event), (v, events + event)):
             for n in range(NODES):
-                force = with_rim(at(src_ref, src, n)[...], n, near_rim_ref, far_rim_ref, rim * FACE)
-                at(new_ref, base, n)[...] = at(base_ref, base, n)[...] - at(factor_ref, 0, n)[...] * force
+                force = with_rim(at(state_ref, rows["force"] + field, n)[...], n, near_rim_ref, far_rim_ref, rim * FACE)
+                new = at(state_ref, rows["base"] + field, n)[...] - at(factor_ref, 0, n)[...] * force
+                at(new_ref, field, n)[...] = new
+                at(base_ref, field, n)[...] = 2.0 * new - at(now_ref, field, n)[...]
         stiffness([(new_ref, u), (new_ref, v)], [(next_ref, u), (next_ref, v)], stiff_ref, kern_ref)
-        for n in range(NODES):
-            place = at(next_ref, v, n)
-            place[...] = place[...] - at(later_ref, u, n)[...]
         assemble(next_ref, u)
         assemble(next_ref, v)
-        pack_faces(next_ref, u, near_ref, far_ref, event * FACE)
-        pack_faces(next_ref, v, near_ref, far_ref, (events + event) * FACE)
+        for b in range(4):
+            low, high = face_tiles(next_ref, u, b, 0, 48)
+            at(near_ref, event * FACE, b)[...] = jnp.where(even, high, low)
+            at(far_ref, event * FACE, b)[...] = jnp.where(even, low, high)
+            low, high = face_tiles(next_ref, v, b, 0, 48)
+            source_low, source_high = face_tiles(later_ref, event * 16 * SUB, b, 0, 0)
+            low, high = low - source_low, high - source_high
+            at(near_ref, (events + event) * FACE, b)[...] = jnp.where(even, high, low)
+            at(far_ref, (events + event) * FACE, b)[...] = jnp.where(even, low, high)
         return 0
 
     lax.fori_loop(0, events, one, 0)
@@ -393,50 +500,57 @@
             parts_ref[j, :, k * LANE : (k + 1) * LANE] = kern_ref[pl.ds(owner * tiles + k, NODES, stride=SUB), :]
 
 
-def emit_kernel(events, new_ref, now_ref, fwd_out_ref, adj_out_ref, base_ref):
-    def one(event, _):
-        u, v = event * FIELD, (events + event) * FIELD
-        gather_back(new_ref, u, fwd_out_ref, event)
-        gather_back(new_ref, v, adj_out_ref, event)
-        for base in (u, v):
+def last_kernel(events, share, base_ref, factor_ref, next_ref, source_ref, near_rim_ref, far_rim_ref, *rest):
+    fwd_hbm, adj_hbm, kernel_ref, done_ref, out_ref, sems = rest[share:]
+    copies = []
+    for event in range(events):
+        for field, out_hbm in ((event, fwd_hbm), (events + event, adj_hbm)):
             for n in range(NODES):
-                at(base_ref, base, n)[...] = 2.0 * at(new_ref, base, n)[...] - at(now_ref, base, n)[...]
-        return 0
-
-    lax.fori_loop(0, events, one, 0)
-
-
-def last_kernel(events, share, base_ref, factor_ref, next_ref, near_rim_ref, far_rim_ref, *rest):
-    fwd_out_ref, adj_out_ref, kernel_ref, done_ref = rest[share:]
+                force = with_rim(at(next_ref, field * FIELD, n)[...], n, near_rim_ref, far_rim_ref, field * FACE)
+                if field >= events:
+                    force = force - at(source_ref, event * FIELD, n)[...]
+                at(done_ref, 0, n)[...] = at(base_ref, field * FIELD, n)[...] - at(factor_ref, 0, n)[...] * force
+            gather_back(done_ref, 0, out_ref, field)
+            copies.append(pltpu.make_async_copy(out_ref.at[field], out_hbm.at[event], sems.at[field]))
+            copies[-1].start()
     total = rest[0][0]
     for part in rest[1:share]:
         total = total + part[0]
     kernel_ref[...] = total
-
-    def one(event, _):
-        for field, out_ref in ((event, fwd_out_ref), (events + event, adj_out_ref)):
-            for n in range(NODES):
-                force = with_rim(at(next_ref, field * FIELD, n)[...], n, near_rim_ref, far_rim_ref, field * FACE)
-                at(done_ref, 0, n)[...] = at(base_ref, field * FIELD, n)[...] - at(factor_ref, 0, n)[...] * force
-            gather_back(done_ref, 0, out_ref, event)
-        return 0
-
-    lax.fori_loop(0, events, one, 0)
-
-
-def call(body, outs, scratch=(), cost=2_000_000, smem=0, count=0, outside=0, limit=24):
+    for copy in copies:
+        copy.wait()
+
+
+def call(body, outs, scratch=(), cost=2_000_000, smem=0, count=0, outside=0, limit=24, written=0):
     in_specs = [pl.BlockSpec(memory_space=pltpu.SMEM)] * smem
     in_specs += [pl.BlockSpec(memory_space=pltpu.VMEM)] * (count - smem - outside)
     in_specs += [pl.BlockSpec(memory_space=pl.ANY)] * outside
     return pl.pallas_call(
         body,
-        out_shape=[jax.ShapeDtypeStruct(shape, jnp.float32) for shape in outs],
+        out_shape=[out if not isinstance(out, tuple) else jax.ShapeDtypeStruct(out, jnp.float32) for out in outs],
         in_specs=in_specs,
-        out_specs=[pl.BlockSpec(memory_space=pltpu.VMEM)] * len(outs),
-        scratch_shapes=[x if isinstance(x, pltpu.SemaphoreType) or not isinstance(x, tuple) else pltpu.VMEM(*x) for x in scratch],
+        out_specs=[pl.BlockSpec(memory_space=pl.ANY)] * written
+        + [pl.BlockSpec(memory_space=pltpu.VMEM)] * (len(outs) - written),
+        scratch_shapes=[pltpu.VMEM(*x) if isinstance(x, tuple) else x for x in scratch],
         compiler_params=pltpu.CompilerParams(vmem_limit_bytes=limit * 1024 * 1024),
         cost_estimate=pl.CostEstimate(flops=cost, bytes_accessed=cost, transcendentals=0),
     )
+
+
+def near_core(shape):
+    return pltpu.VMEM(shape, jnp.float32)
+
+
+def off_core(shape):
+    return pltpu.HBM(shape, jnp.float32)
+
+
+def kept(*arrays):
+    return [pltpu.with_memory_space_constraint(x, pltpu.VMEM) for x in arrays]
+
+
+def far_off(*arrays):
+    return [pltpu.with_memory_space_constraint(x, pltpu.HBM) for x in arrays]
 
 
 def beside(near, far):
@@ -470,7 +584,7 @@
 
     send, token = call(
         place_kernel,
-        [(slabs, rows, CAP), (SUB, LANE)],
+        [(slabs, rows, CAP), near_core((SUB, LANE))],
         [
             ((blocks, LANE), jnp.int32),
             ((blocks, LANE), jnp.int32),
@@ -483,78 +597,79 @@
         ],
         count=4,
         outside=4,
-        limit=63,
+        limit=48,
     )(
-        station_owner.reshape(blocks, LANE),
-        receiver_local.reshape(blocks, LANE),
-        station_weights,
-        adj_records,
+        *far_off(
+            station_owner.reshape(blocks, LANE), receiver_local.reshape(blocks, LANE), station_weights, adj_records
+        )
     )
     got = lax.all_to_all(send, "space", split_axis=0, concat_axis=0, tiled=True)
 
-    fields, now, base, stiff, kern = call(
+    fields = 2 * events + 1
+    state, now, faces = call(
         functools.partial(first_kernel, events),
         [
-            ((2 * events + 1) * FIELD, LANE),
-            (2 * events * FIELD, LANE),
-            (2 * events * FIELD, LANE),
-            (FIELD, LANE),
-            (FIELD, LANE),
+            off_core((state_rows(events)[1], LANE)),
+            off_core((2 * events * FIELD, LANE)),
+            off_core((2 * fields * FACE, LANE)),
         ],
         [((FIELD, LANE), f32)],
         count=7,
-    )(fwd_now, fwd_prev, adj_now, adj_prev, shear_mod, density.reshape(SUB, LANE), token)
-    force, near, far = call(
-        functools.partial(land_first_kernel, events),
-        [(events * FIELD, LANE), ((2 * events + 1) * FACE, LANE), ((2 * events + 1) * FACE, LANE)],
-        [
-            ((events * NODES, elements), f32),
-            (((2 * events + 1) * FIELD, LANE), f32),
-            pltpu.SemaphoreType.DMA(()),
-        ],
+    )(*far_off(fwd_now, fwd_prev, adj_now, adj_prev, shear_mod, density.reshape(SUB, LANE)), *kept(token))
+    near, far = call(
+        functools.partial(land_faces_kernel, events),
+        [(fields * FACE, LANE), (fields * FACE, LANE)],
+        [((2 * fields * FACE, LANE), f32), ((events * 16 * SUB, LANE), f32)]
+        + sums(events, FACE_WANTS)
+        + [pltpu.SemaphoreType.DMA(())],
         count=2,
         outside=1,
-        limit=LAND_LIMIT,
-    )(got, fields)
+    )(got, *far_off(faces))
     near_rim, far_rim = beside(near, far)
-    later = call(
-        functools.partial(land_later_kernel, events),
-        [(events * FIELD, LANE)],
-        [((events * NODES, elements), f32)],
-        count=1,
-    )(got)[0]
-    new, factor, after, parts, near, far = call(
+    state, now, later = call(
+        functools.partial(land_first_kernel, events),
+        [near_core(state.shape), near_core(now.shape), near_core((events * 16 * SUB, LANE))],
+        [((events * FIELD, LANE), f32)] + sums(events, FIRST_WANTS) + [pltpu.SemaphoreType.DMA((2,))],
+        count=3,
+        outside=2,
+        limit=40,
+    )(got, *far_off(state, now))
+    new, base, factor, after, parts, near, far = call(
         functools.partial(second_kernel, events, share),
         [
-            (2 * events * FIELD, LANE),
-            (FIELD, LANE),
-            (2 * events * FIELD, LANE),
+            near_core((2 * events * FIELD, LANE)),
+            near_core((2 * events * FIELD, LANE)),
+            near_core((FIELD, LANE)),
+            near_core((2 * events * FIELD, LANE)),
             (share, NODES, elements // share),
             (2 * events * FACE, LANE),
             (2 * events * FACE, LANE),
         ],
         [((FIELD, LANE), f32)],
         smem=1,
-        count=9,
-    )(
-        lax.axis_index("event").reshape(1).astype(jnp.int32),
-        fields, force, base, stiff, kern, later, near_rim, far_rim,
-    )
+        count=6,
+    )(lax.axis_index("event").reshape(1).astype(jnp.int32), *kept(state, now, later), near_rim, far_rim)
     near_rim, far_rim = beside(near, far)
     pieces = [parts[0:1]] + [
         lax.ppermute(parts[j : j + 1], "event", [(i, (i + j) % share) for i in range(share)]) for j in range(1, share)
     ]
-    fwd_before, adj_before, base = call(
-        functools.partial(emit_kernel, events),
-        [fwd_now.shape, adj_now.shape, (2 * events * FIELD, LANE)],
+    fwd_before, adj_before, source = call(
+        functools.partial(land_later_kernel, events),
+        [fwd_now.shape, adj_now.shape, near_core((events * FIELD, LANE))],
+        [((2 * events, NODES, elements), f32)]
+        + sums(events, LATER_WANTS)
+        + [pltpu.SemaphoreType.DMA((2 * events,))],
         count=2,
-    )(new, now)
+        limit=40,
+        written=2,
+    )(got, *kept(new))
     fwd_last, adj_last, kernel = call(
         functools.partial(last_kernel, events, share),
         [fwd_now.shape, adj_now.shape, (NODES, elements // share)],
-        [((FIELD, LANE), f32)],
-        count=5 + share,
-    )(base, factor, after, near_rim, far_rim, *pieces)
+        [((FIELD, LANE), f32), ((2 * events, NODES, elements), f32), pltpu.SemaphoreType.DMA((2 * events,))],
+        count=6 + share,
+        written=2,
+    )(*kept(base, factor, after, source), near_rim, far_rim, *pieces)
     return fwd_last, fwd_before, adj_last, adj_before, kernel
 
 

time: 67.5 us -> 61.6 us (0.913); the launches traced: 66.4 us -> 61.3 us
  local copies, waits for them, and re-layouts: 10.2 us -> 0.02 us
  Pallas kernels: 20.3 us -> 23.4 us
  waiting for transfers between devices: 20 us -> 21.8 us
    unnamed x30 -> x0, local copies, waits for them, and re-layouts: 10.2 us -> none
    all_to_all x1, waiting for transfers between devices: 18.2 us -> 21.5 us  [shards(): got = lax.all_to_all(send, 'space', split_axis=0, concat_axis=0, tiled=True)]
    pallas_call x6, Pallas kernels: 18.9 us -> 21.6 us  [the longest x1 6.24 us: shards(): call(functools.partial(first_kernel, events), [off_core((state_rows(event...]
    ppermute x2, waiting for transfers between devices: 1.72 us -> 0.29 us  [beside(): from_far = lax.ppermute(far, 'space', inner)]
  transfers between devices with their start and end apart: 6 -> 6, of which waited for: 3 -> 2; matrix products, arithmetic and copies ran while one was open for 0% -> 0% of each run, Pallas kernels for 10% -> 21%
where the time goes in v3:
time: 61.6 us; the launch traced here: 61.3 us
  Pallas kernels  23.4 us (38%)
  waiting for transfers between devices  21.8 us (35%)
  starting transfers between devices  15.3 us (25%)
  between operations  0.73 us (1%)
    all_to_all x1, waiting for transfers between devices, shards(): got = lax.all_to_all(send, 'space', split_axis=0, concat_axis=0, tiled=True)  21.5 us
    ppermute x2, starting transfers between devices, beside(): from_far = lax.ppermute(far, 'space', inner)  7.2 us
    all_to_all x1, starting transfers between devices, shards(): got = lax.all_to_all(send, 'space', split_axis=0, concat_axis=0, tiled=True)  6.57 us
    pallas_call x1, Pallas kernels, shards(): call(functools.partial(first_kernel, events), [off_core((state_rows(event...  6.24 us
    pallas_call x1, Pallas kernels, shards(): call(place_kernel, [(slabs, rows, CAP), near_core((SUB, LANE))], [((block...  5.41 us
    pallas_call x1, Pallas kernels, shards(): call(functools.partial(land_later_kernel, events), [fwd_now.shape, adj_no...  3.61 us
    pallas_call x1, Pallas kernels, shards(): call(functools.partial(land_first_kernel, events), [near_core(state.shape...  2.96 us
    pallas_call x1, Pallas kernels, shards(): call(functools.partial(second_kernel, events, share), [near_core((2 * eve...  1.82 us
  transfers between devices with their start and end apart: 6, of which 2 were waited for; matrix products, arithmetic and copies ran while one was open for 0% of the time, Pallas kernels for 21%

profile of v3, /device:TPU:13, one launch (start us, length us, event | category | flops | bytes accessed | tf_op | source)
XLA Modules:
  0.0 61.3 jit_solution(17063533407455640495)
XLA Ops:
  0.6 5.4 %shard_map.137 = (f32[16,72,256]{2,1,0:T(8,128)}, f32[8,128]{1,0:T(8,128)S(1)}) custom-call(s32[16,128]{1,0:T(8,128)} %bitcast.4, s32[16,128]{1,0:T(8,128)} %bitcast.5, f32[64,2048]{1,0:T(8,128)} %weights_hbm.1, f32[2,2,2048]{2,1,0:T(2,128)} %records_hbm.1), custom_call_target="tpu_custom_call" | custom-call | flops 2000000 | bytes 2000000 | tf_op jit(solution)/shard_map/pallas_call | solution.py:585
  6.0 6.6 %all-to-all-start = ((f32[16,72,256]{2,1,0:T(8,128)}), f32[16,72,256]{2,1,0:T(8,128)S(1)}, u32[]{:S(2)}, u32[]{:S(2)}) async-start(f32[16,72,256]{2,1,0:T(8,128)} %get-tuple-element.28), calls=%async_computation | async-start | bytes 2359296 | tf_op jit(solution)/shard_map/all_to_all | solution.py:606
  12.6 6.2 %shard_map.138 = (f32[5632,128]{1,0:T(8,128)}, f32[2048,128]{1,0:T(8,128)}, f32[320,128]{1,0:T(8,128)}) custom-call(f32[2,64,1024]{2,1,0:T(8,128)} %fwd_ref.1, f32[2,64,1024]{2,1,0:T(8,128)} %fwd_prev_ref.1, f32[2,64,1024]{2,1,0:T(8,128)} %adj_ref.1, f32[2,64,1024]{2,1,0:T(8,128)} %adj_prev_ref.1, f32[64,1024]{1,0:T(8,128)} %shear_ref.1, f32[8,128]{1,0:T(8,128)} %bitcast.6, ...), custom_call_target="tpu_custom_call" | custom-call | flops 2000000 | bytes 2000000 | tf_op jit(solution)/shard_map/pallas_call | solution.py:609
  18.9 21.5 %all-to-all-done.got_ref = f32[16,72,256]{2,1,0:T(8,128)S(1)} async-done(((f32[16,72,256]{2,1,0:T(8,128)}), f32[16,72,256]{2,1,0:T(8,128)S(1)}, u32[]{:S(2)}, u32[]{:S(2)}) %all-to-all-start) | async-done | bytes 1179680 | tf_op jit(solution)/shard_map/all_to_all | solution.py:606
  40.4 1.6 %shard_map.140 = (f32[160,128]{1,0:T(8,128)S(1)}, f32[160,128]{1,0:T(8,128)S(1)}) custom-call(f32[16,72,256]{2,1,0:T(8,128)S(1)} %all-to-all-done.got_ref, f32[320,128]{1,0:T(8,128)} %get-tuple-element.35.faces_hbm), custom_call_target="tpu_custom_call" | custom-call | flops 2000000 | bytes 2000000 | tf_op jit(solution)/shard_map/pallas_call | solution.py:619
  42.0 0.3 collective-permute-start
  42.2 3.4 %collective-permute-start.1 = (f32[160,128]{1,0:T(8,128)S(1)}, f32[160,128]{1,0:T(8,128)S(1)}, u32[]{:S(2)}, u32[]{:S(2)}) collective-permute-start(f32[160,128]{1,0:T(8,128)S(1)} %get-tuple-element.37), channel_id=1, source_target_pairs={{2,4},{4,2},{6,8},{8,6},{10,12},{12,10},{14,16},{16,14},{18,20},{2... | collective-permute-start | bytes 245768 | tf_op jit(solution)/shard_map/ppermute | solution.py:559
  45.6 3.0 %shard_map.139 = (f32[5632,128]{1,0:T(8,128)S(1)}, f32[2048,128]{1,0:T(8,128)S(1)}, f32[256,128]{1,0:T(8,128)S(1)}) custom-call(f32[16,72,256]{2,1,0:T(8,128)S(1)} %all-to-all-done.got_ref, f32[5632,128]{1,0:T(8,128)} %get-tuple-element.30.state_hbm, f32[2048,128]{1,0:T(8,128)} %get-tuple-element.31.now_hbm), custom_call_target="tpu_custom_call" | custom-call | flops 2000000 | bytes 2000000 | tf_op jit(solution)/shard_map/pallas_call | solution.py:629
  48.6 0.0 collective-permute-done.near_rim_ref
  48.6 0.3 collective-permute-done.1.far_rim_ref
  48.9 1.8 %shard_map.141 = (f32[2048,128]{1,0:T(8,128)S(1)}, f32[2048,128]{1,0:T(8,128)S(1)}, f32[512,128]{1,0:T(8,128)S(1)}, f32[2048,128]{1,0:T(8,128)S(1)}, f32[2,64,51...) custom-call(s32[1]{0:T(128)} %bitcast.position_ref, f32[5632,128]{1,0:T(8,128)S(1)} %get-tuple-element.32.state_ref, ...), custom_call_target="tpu_custom_call" | custom-call | flops 2000000 | bytes 2000000 | tf_op jit(solution)/shard_map/pallas_call | solution.py:637
  50.7 1.3 %collective-permute-start.4 = (f32[1,64,512]{2,1,0:T(8,128)S(1)}, f32[1,64,512]{2,1,0:T(8,128)S(1)}, u32[]{:S(2)}, u32[]{:S(2)}) collective-permute-start(f32[1,64,512]{2,1,0:T(8,128)S(1)} %get-tuple-element.51), channel_id=1, source_target_pairs={{0,1},{1,0},{2,3},{3,2},{4,5},{5,4},{6,7},{7,6},{8,9},{9,8},{10,11... | collective-permute-start | bytes 393224 | tf_op jit(solution)/shard_map/ppermute | solution.py:654
  52.0 0.0 collective-permute-start.2
  52.0 3.8 %collective-permute-start.3 = (f32[128,128]{1,0:T(8,128)S(1)}, f32[128,128]{1,0:T(8,128)S(1)}, u32[]{:S(2)}, u32[]{:S(2)}) collective-permute-start(f32[128,128]{1,0:T(8,128)S(1)} %get-tuple-element.44), channel_id=1, source_target_pairs={{2,4},{4,2},{6,8},{8,6},{10,12},{12,10},{14,16},{16,14},{18,20},{2... | collective-permute-start | bytes 196616 | tf_op jit(solution)/shard_map/ppermute | solution.py:559
  55.9 3.6 %shard_map.142 = (f32[2,64,1024]{2,1,0:T(8,128)}, f32[2,64,1024]{2,1,0:T(8,128)}, f32[1024,128]{1,0:T(8,128)S(1)}) custom-call(f32[16,72,256]{2,1,0:T(8,128)S(1)} %all-to-all-done.got_ref, f32[2048,128]{1,0:T(8,128)S(1)} %get-tuple-element.41.new_ref), custom_call_target="tpu_custom_call" | custom-call | flops 2000000 | bytes 2000000 | tf_op jit(solution)/shard_map/pallas_call | solution.py:656
  59.5 0.0 collective-permute-done.2.near_rim_ref
  59.5 0.0 collective-permute-done.3.far_rim_ref
  59.5 0.0 collective-permute-done.4.rest_1_
  59.5 1.8 %shard_map.143 = (f32[2,64,1024]{2,1,0:T(8,128)}, f32[2,64,1024]{2,1,0:T(8,128)}, f32[64,512]{1,0:T(8,128)}) custom-call(f32[2048,128]{1,0:T(8,128)S(1)} %get-tuple-element.38.base_ref, f32[512,128]{1,0:T(8,128)S(1)} %get-tuple-element.39.factor_ref, f32[2048,128]{1,0:T(8,128)S(1)} %get-tuple-element.40.next_ref, ...), custom_call_target="tpu_custom_call" | custom-call | flops 2000000 | bytes 2000000 | tf_op jit(solution)/shard_map/pallas_call | solution.py:666
  (1 shorter events, 0.0 us)
Async XLA Ops:
  6.0 34.3 %all-to-all-start = ((f32[16,72,256]{2,1,0:T(8,128)}), f32[16,72,256]{2,1,0:T(8,128)S(1)}, u32[]{:S(2)}, u32[]{:S(2)}) async-start(f32[16,72,256]{2,1,0:T(8,128)} %get-tuple-element.28), calls=%async_computation | async-start | bytes 2359296 | tf_op jit(solution)/shard_map/all_to_all | solution.py:606
  42.0 6.6 %collective-permute-start = (f32[160,128]{1,0:T(8,128)S(1)}, f32[160,128]{1,0:T(8,128)S(1)}, u32[]{:S(2)}, u32[]{:S(2)}) collective-permute-start(f32[160,128]{1,0:T(8,128)S(1)} %get-tuple-element.36), channel_id=1, source_target_pairs={{0,2},{2,0},{4,6},{6,4},{8,10},{10,8},{12,14},{14,12},{16,18},{18,... | collective-permute-start | bytes 245768 | tf_op jit(solution)/shard_map/ppermute | solution.py:560
  42.2 6.6 %collective-permute-start.1 = (f32[160,128]{1,0:T(8,128)S(1)}, f32[160,128]{1,0:T(8,128)S(1)}, u32[]{:S(2)}, u32[]{:S(2)}) collective-permute-start(f32[160,128]{1,0:T(8,128)S(1)} %get-tuple-element.37), channel_id=1, source_target_pairs={{2,4},{4,2},{6,8},{8,6},{10,12},{12,10},{14,16},{16,14},{18,20},{2... | collective-permute-start | bytes 245768 | tf_op jit(solution)/shard_map/ppermute | solution.py:559
  50.7 8.8 %collective-permute-start.4 = (f32[1,64,512]{2,1,0:T(8,128)S(1)}, f32[1,64,512]{2,1,0:T(8,128)S(1)}, u32[]{:S(2)}, u32[]{:S(2)}) collective-permute-start(f32[1,64,512]{2,1,0:T(8,128)S(1)} %get-tuple-element.51), channel_id=1, source_target_pairs={{0,1},{1,0},{2,3},{3,2},{4,5},{5,4},{6,7},{7,6},{8,9},{9,8},{10,11... | collective-permute-start | bytes 393224 | tf_op jit(solution)/shard_map/ppermute | solution.py:654
  52.0 7.5 %collective-permute-start.2 = (f32[128,128]{1,0:T(8,128)S(1)}, f32[128,128]{1,0:T(8,128)S(1)}, u32[]{:S(2)}, u32[]{:S(2)}) collective-permute-start(f32[128,128]{1,0:T(8,128)S(1)} %get-tuple-element.43), channel_id=1, source_target_pairs={{0,2},{2,0},{4,6},{6,4},{8,10},{10,8},{12,14},{14,12},{16,18},{18,... | collective-permute-start | bytes 196616 | tf_op jit(solution)/shard_map/ppermute | solution.py:560
  52.0 7.5 %collective-permute-start.3 = (f32[128,128]{1,0:T(8,128)S(1)}, f32[128,128]{1,0:T(8,128)S(1)}, u32[]{:S(2)}, u32[]{:S(2)}) collective-permute-start(f32[128,128]{1,0:T(8,128)S(1)} %get-tuple-element.44), channel_id=1, source_target_pairs={{2,4},{4,2},{6,8},{8,6},{10,12},{12,10},{14,16},{16,14},{18,20},{2... | collective-permute-start | bytes 196616 | tf_op jit(solution)/shard_map/ppermute | solution.py:559

commit v4 on v3

--- a/solution.py
+++ b/solution.py
@@ -184,8 +184,11 @@
         copy.start()
     token_ref[...] = jnp.zeros_like(token_ref)
     stations = weights_ref.shape[1]
-    slabs, rows, _ = out_ref.shape
+    rows = sorted_ref.shape[0]
     events = records_ref.shape[0]
+    few = events * STEPS + 1
+    packed = 2 * (NODES + few)
+    slabs = out_ref.shape[0] // packed
     blocks = stations // LANE
     chunks = stations // CAP
     owner_id = lax.broadcasted_iota(jnp.int32, (slabs, LANE), 0)
@@ -228,19 +231,26 @@
         data_ref[:rows, cut] = high
         data_ref[rows:, cut] = (full - high.astype(jnp.float32)).astype(jnp.bfloat16)
     slot = lax.broadcasted_iota(jnp.int32, (CAP, LANE), 0).astype(jnp.bfloat16)
-    lane = lax.broadcasted_iota(jnp.int32, (rows, LANE), 1)
+    lane = lax.broadcasted_iota(jnp.int32, (SUB, LANE), 1)
+    sorted_ref[:, stations:] = jnp.zeros((rows, 3 * LANE), jnp.float32)
 
     def cut_block(slab):
         begin, size = begins[slab], sizes[slab]
         shift = lax.rem(begin, LANE)
         base = begin - shift
         turn = lax.rem(LANE - shift, LANE)
-        turned = [
-            pltpu.roll(sorted_ref[:, pl.ds(pl.multiple_of(base + j * LANE, LANE), LANE)], turn, 1) for j in range(3)
-        ]
-        for j in range(2):
-            piece = jnp.where(lane < LANE - shift, turned[j], turned[j + 1])
-            out_ref[slab, :, j * LANE : (j + 1) * LANE] = jnp.where(lane + j * LANE < size, piece, 0.0)
+        kept_lanes = lane >= shift
+        for first in range(0, rows, SUB):
+            tiles = [
+                sorted_ref[first : first + SUB, pl.ds(pl.multiple_of(base + j * LANE, LANE), LANE)] for j in range(3)
+            ]
+            for j in range(2):
+                piece = pltpu.roll(jnp.where(kept_lanes, tiles[j], tiles[j + 1]), turn, 1)
+                if first < NODES:
+                    out_ref[pl.ds(slab * packed + j * NODES + first, SUB), :] = piece
+                else:
+                    piece = jnp.where(lane + j * LANE < size, piece, 0.0)
+                    out_ref[pl.ds(slab * packed + 2 * NODES + j * few, few), :] = piece[:few]
 
     for chunk in range(chunks):
         spots = spot_ref[...] - float(chunk * CAP)
@@ -267,7 +277,9 @@
 
 
 def land(got_ref, events, wants, acc_refs):
-    slabs = got_ref.shape[0]
+    few = events * STEPS + 1
+    packed = 2 * (NODES + few)
+    slabs = got_ref.shape[0] // packed
     group = min(slabs, 16)
     slot = lax.broadcasted_iota(jnp.int32, (CAP, LANE), 0).astype(jnp.bfloat16)
     if slabs > group:
@@ -280,16 +292,20 @@
         for i in range(group):
             src = g * group + i
             for (first, last, step), found in items.items():
-                weights = got_ref[src, first:last, :]
-                rows = [NODES + event * STEPS + step for event in range(events)]
-                found.append(
-                    split(jnp.concatenate([weights * got_ref[src, row : row + 1, :] for row in rows], axis=0))
-                )
-            ids = got_ref[src, NODES + events * STEPS : NODES + events * STEPS + 1, :].astype(jnp.int32)
+                for j in range(2):
+                    weights = got_ref[pl.ds(src * packed + j * NODES + first, last - first), :]
+                    samples = [
+                        got_ref[pl.ds(src * packed + 2 * NODES + j * few + event * STEPS + step, 1), :]
+                        for event in range(events)
+                    ]
+                    found.append(split(jnp.concatenate([weights * sample for sample in samples], axis=0)))
+            ids = [
+                got_ref[pl.ds(src * packed + 2 * NODES + (j + 1) * few - 1, 1), :].astype(jnp.int32) for j in range(2)
+            ]
             for at_hot, (quarter, _) in zip(hot, wants):
-                wanted = jnp.where(ids // CAP == quarter, ids % CAP, -1).astype(jnp.float32).astype(jnp.bfloat16)
-                for cut in (slice(0, LANE), slice(LANE, 2 * LANE)):
-                    at_hot.append(jnp.where(slot == wanted[:, cut], jnp.bfloat16(1), jnp.bfloat16(0)))
+                for half in ids:
+                    wanted = jnp.where(half // CAP == quarter, half % CAP, -1).astype(jnp.float32).astype(jnp.bfloat16)
+                    at_hot.append(jnp.where(slot == wanted, jnp.bfloat16(1), jnp.bfloat16(0)))
         left = {item: jnp.concatenate(found, axis=1) for item, found in items.items()}
         for at_hot, (_, chosen), acc_ref in zip(hot, wants, acc_refs):
             landed = lax.dot_general(
@@ -313,14 +329,9 @@
         one(0, 0)
 
 
-FACE_WANTS = ((0, ((0, 16, 0),)), (3, ((48, 64, 0),)))
-FIRST_WANTS = (
-    (0, ((0, NODES, 0), (0, 16, 1))),
-    (1, ((0, NODES, 0),)),
-    (2, ((0, NODES, 0),)),
-    (3, ((0, NODES, 0), (48, 64, 1))),
-)
-LATER_WANTS = tuple((q, ((0, NODES, 1),)) for q in range(4))
+FACE_WANTS = ((0, ((0, 16, 0), (0, 16, 1))), (3, ((48, 64, 0), (48, 64, 1))))
+FIRST_WANTS = ((0, ((0, NODES, 0), (0, NODES, 1))),) + tuple((q, ((0, NODES, 0),)) for q in range(1, 4))
+LATER_WANTS = tuple((q, ((0, NODES, 1),)) for q in range(1, 4))
 
 
 def sums(events, wants):
@@ -329,40 +340,41 @@
     ]
 
 
-def spread_source(events, acc_refs, out_ref):
+def spread_source(events, acc_refs, skip, out_ref):
     for event in range(events):
         for k in range(SUB):
             cut = slice(k % 2 * LANE, (k % 2 + 1) * LANE)
-            out_ref[pl.ds(event * FIELD + k, NODES, stride=SUB), :] = acc_refs[k // 2][event * NODES : (event + 1) * NODES, cut]
+            first = event * NODES + (skip if k < 2 else 0)
+            rows = slice(first, first + NODES)
+            out_ref[pl.ds(event * FIELD + k, NODES, stride=SUB), :] = acc_refs[k // 2][rows, cut]
         assemble(out_ref, event * FIELD)
-
-
-def spread_faces(events, low_ref, high_ref, skip, out_ref):
-    out_ref[...] = jnp.zeros_like(out_ref)
-    for event in range(events):
-        rows = slice(skip + event * 16, skip + (event + 1) * 16)
-        for j in range(2):
-            cut = slice(j * LANE, (j + 1) * LANE)
-            out_ref[pl.ds(event * 16 * SUB + j, 16, stride=SUB), :] = low_ref[rows, cut]
-            out_ref[pl.ds(event * 16 * SUB + SUB - 2 + j, 16, stride=SUB), :] = high_ref[rows, cut]
-        assemble_layers(out_ref, event * 16 * SUB, 1)
 
 
 def land_faces_kernel(events, got_ref, faces_hbm, near_ref, far_ref, faces_ref, source_ref, low_ref, high_ref, sem):
     copy = pltpu.make_async_copy(faces_hbm, faces_ref, sem)
     copy.start()
     land(got_ref, events, FACE_WANTS, (low_ref, high_ref))
-    spread_faces(events, low_ref, high_ref, 0, source_ref)
+    source_ref[...] = jnp.zeros_like(source_ref)
+    for each in range(STEPS * events):
+        rows = slice(each * 16, (each + 1) * 16)
+        for j in range(2):
+            cut = slice(j * LANE, (j + 1) * LANE)
+            source_ref[pl.ds(each * 16 * SUB + j, 16, stride=SUB), :] = low_ref[rows, cut]
+            source_ref[pl.ds(each * 16 * SUB + SUB - 2 + j, 16, stride=SUB), :] = high_ref[rows, cut]
+        assemble_layers(source_ref, each * 16 * SUB, 1)
     copy.wait()
     even = is_even()
     fields = 2 * events + 1
-    for field in range(fields):
+    for field in range(fields + events):
         for b in range(4):
-            low = at(faces_ref, field * FACE, b)[...]
-            high = at(faces_ref, (fields + field) * FACE, b)[...]
+            if field < fields:
+                low = at(faces_ref, field * FACE, b)[...]
+                high = at(faces_ref, (fields + field) * FACE, b)[...]
             if events <= field < 2 * events:
                 source_low, source_high = face_tiles(source_ref, (field - events) * 16 * SUB, b, 0, 0)
                 low, high = low - source_low, high - source_high
+            if field >= fields:
+                low, high = face_tiles(source_ref, (events + field - fields) * 16 * SUB, b, 0, 0)
             at(near_ref, field * FACE, b)[...] = jnp.where(even, high, low)
             at(far_ref, field * FACE, b)[...] = jnp.where(even, low, high)
 
@@ -377,7 +389,7 @@
 
 
 def land_first_kernel(
-    events, got_ref, state_hbm, now_hbm, state_ref, now_ref, later_ref, source_ref, acc0, acc1, acc2, acc3, sems
+    events, got_ref, state_hbm, now_hbm, state_ref, now_ref, acc0, source_ref, acc1, acc2, acc3, sems
 ):
     copies = [
         pltpu.make_async_copy(state_hbm, state_ref, sems.at[0]),
@@ -386,8 +398,7 @@
     for copy in copies:
         copy.start()
     land(got_ref, events, FIRST_WANTS, (acc0, acc1, acc2, acc3))
-    spread_source(events, (acc0, acc1, acc2, acc3), source_ref)
-    spread_faces(events, acc0, acc3, events * NODES, later_ref)
+    spread_source(events, (acc0, acc1, acc2, acc3), 0, source_ref)
     for copy in copies:
         copy.wait()
     rows, _ = state_rows(events)
@@ -398,7 +409,7 @@
 
 
 def land_later_kernel(
-    events, got_ref, new_ref, fwd_hbm, adj_hbm, source_ref, out_ref, acc0, acc1, acc2, acc3, sems
+    events, got_ref, new_ref, acc0, fwd_hbm, adj_hbm, source_ref, out_ref, acc1, acc2, acc3, sems
 ):
     copies = []
     for event in range(events):
@@ -406,8 +417,8 @@
             gather_back(new_ref, field * FIELD, out_ref, field)
             copies.append(pltpu.make_async_copy(out_ref.at[field], out_hbm.at[event], sems.at[field]))
             copies[-1].start()
-    land(got_ref, events, LATER_WANTS, (acc0, acc1, acc2, acc3))
-    spread_source(events, (acc0, acc1, acc2, acc3), source_ref)
+    land(got_ref, events, LATER_WANTS, (acc1, acc2, acc3))
+    spread_source(events, (acc0, acc1, acc2, acc3), events * NODES, source_ref)
     for copy in copies:
         copy.wait()
 
@@ -454,13 +465,16 @@
 
 
 def second_kernel(
-    events, share, position_ref, state_ref, now_ref, later_ref, near_rim_ref, far_rim_ref,
-    new_ref, base_ref, factor_ref, next_ref, parts_ref, near_ref, far_ref, kern_ref,
+    events, share, position_ref, state_ref, now_ref, near_rim_ref, far_rim_ref,
+    new_ref, base_ref, factor_ref, next_ref, parts_ref, near_ref, far_ref, later_ref, kern_ref,
 ):
     rows, _ = state_rows(events)
     stiff_ref = state_ref.at[pl.ds(rows["stiff"], FIELD), :]
     kern_ref[...] = state_ref[pl.ds(rows["kern"], FIELD), :]
     mass = 2 * events
+    for side, rim_ref in enumerate((near_rim_ref, far_rim_ref)):
+        for row in range(0, events * FACE, SUB):
+            later_ref[side, row : row + SUB, :] = rim_ref[(mass + 1) * FACE + row : (mass + 1) * FACE + row + SUB, :]
     even = is_even()
     for n in range(NODES):
         at(factor_ref, 0, n)[...] = STEP_SQUARE / with_rim(
@@ -478,15 +492,11 @@
         stiffness([(new_ref, u), (new_ref, v)], [(next_ref, u), (next_ref, v)], stiff_ref, kern_ref)
         assemble(next_ref, u)
         assemble(next_ref, v)
-        for b in range(4):
-            low, high = face_tiles(next_ref, u, b, 0, 48)
-            at(near_ref, event * FACE, b)[...] = jnp.where(even, high, low)
-            at(far_ref, event * FACE, b)[...] = jnp.where(even, low, high)
-            low, high = face_tiles(next_ref, v, b, 0, 48)
-            source_low, source_high = face_tiles(later_ref, event * 16 * SUB, b, 0, 0)
-            low, high = low - source_low, high - source_high
-            at(near_ref, (events + event) * FACE, b)[...] = jnp.where(even, high, low)
-            at(far_ref, (events + event) * FACE, b)[...] = jnp.where(even, low, high)
+        for field in (u, v):
+            for b in range(4):
+                low, high = face_tiles(next_ref, field, b, 0, 48)
+                at(near_ref, field // NODES * 4, b)[...] = jnp.where(even, high, low)
+                at(far_ref, field // NODES * 4, b)[...] = jnp.where(even, low, high)
         return 0
 
     lax.fori_loop(0, events, one, 0)
@@ -500,7 +510,7 @@
             parts_ref[j, :, k * LANE : (k + 1) * LANE] = kern_ref[pl.ds(owner * tiles + k, NODES, stride=SUB), :]
 
 
-def last_kernel(events, share, base_ref, factor_ref, next_ref, source_ref, near_rim_ref, far_rim_ref, *rest):
+def last_kernel(events, share, base_ref, factor_ref, next_ref, source_ref, later_ref, near_rim_ref, far_rim_ref, *rest):
     fwd_hbm, adj_hbm, kernel_ref, done_ref, out_ref, sems = rest[share:]
     copies = []
     for event in range(events):
@@ -508,7 +518,8 @@
             for n in range(NODES):
                 force = with_rim(at(next_ref, field * FIELD, n)[...], n, near_rim_ref, far_rim_ref, field * FACE)
                 if field >= events:
-                    force = force - at(source_ref, event * FIELD, n)[...]
+                    source = at(source_ref, event * FIELD, n)[...]
+                    force = force - with_rim(source, n, later_ref.at[0], later_ref.at[1], event * FACE)
                 at(done_ref, 0, n)[...] = at(base_ref, field * FIELD, n)[...] - at(factor_ref, 0, n)[...] * force
             gather_back(done_ref, 0, out_ref, field)
             copies.append(pltpu.make_async_copy(out_ref.at[field], out_hbm.at[event], sems.at[field]))
@@ -580,11 +591,12 @@
     share = lax.axis_size("event")
     f32 = jnp.float32
     rows = -(-(NODES + events * STEPS + 1) // SUB) * SUB
+    packed = 2 * (NODES + events * STEPS + 1)
     blocks = stations // LANE
 
     send, token = call(
         place_kernel,
-        [(slabs, rows, CAP), near_core((SUB, LANE))],
+        [(slabs * packed, LANE), near_core((SUB, LANE))],
         [
             ((blocks, LANE), jnp.int32),
             ((blocks, LANE), jnp.int32),
@@ -603,7 +615,8 @@
             station_owner.reshape(blocks, LANE), receiver_local.reshape(blocks, LANE), station_weights, adj_records
         )
     )
-    got = lax.all_to_all(send, "space", split_axis=0, concat_axis=0, tiled=True)
+    send = send.reshape(slabs, packed // 2, 2, LANE)
+    got = lax.all_to_all(send, "space", split_axis=0, concat_axis=0, tiled=True).reshape(slabs * packed, LANE)
 
     fields = 2 * events + 1
     state, now, faces = call(
@@ -618,23 +631,23 @@
     )(*far_off(fwd_now, fwd_prev, adj_now, adj_prev, shear_mod, density.reshape(SUB, LANE)), *kept(token))
     near, far = call(
         functools.partial(land_faces_kernel, events),
-        [(fields * FACE, LANE), (fields * FACE, LANE)],
-        [((2 * fields * FACE, LANE), f32), ((events * 16 * SUB, LANE), f32)]
+        [((fields + events) * FACE, LANE)] * 2,
+        [((2 * fields * FACE, LANE), f32), ((STEPS * events * 16 * SUB, LANE), f32)]
         + sums(events, FACE_WANTS)
         + [pltpu.SemaphoreType.DMA(())],
         count=2,
         outside=1,
     )(got, *far_off(faces))
     near_rim, far_rim = beside(near, far)
-    state, now, later = call(
+    state, now, quarter = call(
         functools.partial(land_first_kernel, events),
-        [near_core(state.shape), near_core(now.shape), near_core((events * 16 * SUB, LANE))],
-        [((events * FIELD, LANE), f32)] + sums(events, FIRST_WANTS) + [pltpu.SemaphoreType.DMA((2,))],
+        [near_core(state.shape), near_core(now.shape), near_core((STEPS * events * NODES, CAP))],
+        [((events * FIELD, LANE), f32)] + sums(events, FIRST_WANTS[1:]) + [pltpu.SemaphoreType.DMA((2,))],
         count=3,
         outside=2,
         limit=40,
     )(got, *far_off(state, now))
-    new, base, factor, after, parts, near, far = call(
+    new, base, factor, after, parts, near, far, later = call(
         functools.partial(second_kernel, events, share),
         [
             near_core((2 * events * FIELD, LANE)),
@@ -644,11 +657,12 @@
             (share, NODES, elements // share),
             (2 * events * FACE, LANE),
             (2 * events * FACE, LANE),
+            near_core((2, events * FACE, LANE)),
         ],
         [((FIELD, LANE), f32)],
         smem=1,
-        count=6,
-    )(lax.axis_index("event").reshape(1).astype(jnp.int32), *kept(state, now, later), near_rim, far_rim)
+        count=5,
+    )(lax.axis_index("event").reshape(1).astype(jnp.int32), *kept(state, now), near_rim, far_rim)
     near_rim, far_rim = beside(near, far)
     pieces = [parts[0:1]] + [
         lax.ppermute(parts[j : j + 1], "event", [(i, (i + j) % share) for i in range(share)]) for j in range(1, share)
@@ -659,17 +673,17 @@
         [((2 * events, NODES, elements), f32)]
         + sums(events, LATER_WANTS)
         + [pltpu.SemaphoreType.DMA((2 * events,))],
-        count=2,
+        count=3,
         limit=40,
         written=2,
-    )(got, *kept(new))
+    )(got, *kept(new, quarter))
     fwd_last, adj_last, kernel = call(
         functools.partial(last_kernel, events, share),
         [fwd_now.shape, adj_now.shape, (NODES, elements // share)],
         [((FIELD, LANE), f32), ((2 * events, NODES, elements), f32), pltpu.SemaphoreType.DMA((2 * events,))],
-        count=6 + share,
+        count=7 + share,
         written=2,
-    )(*kept(base, factor, after, source), near_rim, far_rim, *pieces)
+    )(*kept(base, factor, after, source, later), near_rim, far_rim, *pieces)
     return fwd_last, fwd_before, adj_last, adj_before, kernel
 
 

time: 61.6 us -> 60.7 us (0.985)
  waiting for transfers between devices: 21.8 us -> 20.8 us
    all_to_all x1, waiting for transfers between devices: 21.5 us -> 20.5 us  [shards(): lax.all_to_all(send, 'space', split_axis=0, concat_axis=0, tiled=True)]
where the time goes in v4:
time: 60.7 us; the launch traced here: 60.4 us
  Pallas kernels  23.1 us (38%)
  waiting for transfers between devices  20.8 us (34%)
  starting transfers between devices  15.7 us (26%)
  between operations  0.73 us (1%)
    all_to_all x1, waiting for transfers between devices, shards(): lax.all_to_all(send, 'space', split_axis=0, concat_axis=0, tiled=True)  20.5 us
    ppermute x2, starting transfers between devices, beside(): from_far = lax.ppermute(far, 'space', inner)  7.55 us
    all_to_all x1, starting transfers between devices, shards(): lax.all_to_all(send, 'space', split_axis=0, concat_axis=0, tiled=True)  6.57 us
    pallas_call x1, Pallas kernels, shards(): call(functools.partial(first_kernel, events), [off_core((state_rows(event...  6.24 us
    pallas_call x1, Pallas kernels, shards(): call(place_kernel, [(slabs * packed, LANE), near_core((SUB, LANE))], [((b...  5.28 us
    pallas_call x1, Pallas kernels, shards(): call(functools.partial(land_first_kernel, events), [near_core(state.shape...  3.23 us
    pallas_call x1, Pallas kernels, shards(): call(functools.partial(land_later_kernel, events), [fwd_now.shape, adj_no...  3.06 us
    pallas_call x1, Pallas kernels, shards(): call(functools.partial(second_kernel, events, share), [near_core((2 * eve...  1.82 us
  transfers between devices with their start and end apart: 6, of which 2 were waited for; matrix products, arithmetic and copies ran while one was open for 0% of the time, Pallas kernels for 21%

profile of v4, /device:TPU:13, one launch (start us, length us, event | category | flops | bytes accessed | tf_op | source)
XLA Modules:
  0.0 60.4 jit_solution(4175369838569989271)
XLA Ops:
  0.6 5.3 %shard_map.137 = (f32[2208,128]{1,0:T(8,128)}, f32[8,128]{1,0:T(8,128)S(1)}) custom-call(s32[16,128]{1,0:T(8,128)} %bitcast.9, s32[16,128]{1,0:T(8,128)} %bitcast.10, f32[64,2048]{1,0:T(8,128)} %weights_hbm.1, f32[2,2,2048]{2,1,0:T(2,128)} %records_hbm.1), custom_call_target="tpu_custom_call" | custom-call | flops 2000000 | bytes 2000000 | tf_op jit(solution)/shard_map/pallas_call | solution.py:597
  5.9 6.6 %all-to-all-start = ((f32[16,69,2,128]{3,2,1,0:T(2,128)}), f32[16,69,2,128]{3,2,1,0:T(2,128)S(1)}, u32[]{:S(2)}, u32[]{:S(2)}) async-start(f32[16,69,2,128]{3,2,1,0:T(2,128)} %bitcast.3), calls=%async_computation | async-start | bytes 2260992 | tf_op jit(solution)/shard_map/all_to_all | solution.py:619
  12.5 6.2 %shard_map.138 = (f32[5632,128]{1,0:T(8,128)}, f32[2048,128]{1,0:T(8,128)}, f32[320,128]{1,0:T(8,128)}) custom-call(f32[2,64,1024]{2,1,0:T(8,128)} %fwd_ref.1, f32[2,64,1024]{2,1,0:T(8,128)} %fwd_prev_ref.1, f32[2,64,1024]{2,1,0:T(8,128)} %adj_ref.1, f32[2,64,1024]{2,1,0:T(8,128)} %adj_prev_ref.1, f32[64,1024]{1,0:T(8,128)} %shear_ref.1, f32[8,128]{1,0:T(8,128)} %bitcast.11, ...), custom_call_target="tpu_custom_call" | custom-call | flops 2000000 | bytes 2000000 | tf_op jit(solution)/shard_map/pallas_call | solution.py:622
  18.7 20.5 %all-to-all-done = f32[16,69,2,128]{3,2,1,0:T(2,128)S(1)} async-done(((f32[16,69,2,128]{3,2,1,0:T(2,128)}), f32[16,69,2,128]{3,2,1,0:T(2,128)S(1)}, u32[]{:S(2)}, u32[]{:S(2)}) %all-to-all-start) | async-done | bytes 1130528 | tf_op jit(solution)/shard_map/all_to_all | solution.py:619
  39.2 1.7 %shard_map.140 = (f32[224,128]{1,0:T(8,128)S(1)}, f32[224,128]{1,0:T(8,128)S(1)}) custom-call(f32[2208,128]{1,0:T(8,128)S(1)} %bitcast.6, f32[320,128]{1,0:T(8,128)} %get-tuple-element.35.faces_hbm), custom_call_target="tpu_custom_call" | custom-call | flops 2000000 | bytes 2000000 | tf_op jit(solution)/shard_map/pallas_call | solution.py:632
  40.9 0.3 collective-permute-start
  41.2 3.4 %collective-permute-start.1 = (f32[224,128]{1,0:T(8,128)S(1)}, f32[224,128]{1,0:T(8,128)S(1)}, u32[]{:S(2)}, u32[]{:S(2)}) collective-permute-start(f32[224,128]{1,0:T(8,128)S(1)} %get-tuple-element.37), channel_id=1, source_target_pairs={{2,4},{4,2},{6,8},{8,6},{10,12},{12,10},{14,16},{16,14},{18,20},{2... | collective-permute-start | bytes 344072 | tf_op jit(solution)/shard_map/ppermute | solution.py:570
  44.6 3.2 %shard_map.139 = (f32[5632,128]{1,0:T(8,128)S(1)}, f32[2048,128]{1,0:T(8,128)S(1)}, f32[256,256]{1,0:T(8,128)S(1)}) custom-call(f32[2208,128]{1,0:T(8,128)S(1)} %bitcast.7, f32[5632,128]{1,0:T(8,128)} %get-tuple-element.31.state_hbm, f32[2048,128]{1,0:T(8,128)} %get-tuple-element.32.now_hbm), custom_call_target="tpu_custom_call" | custom-call | flops 2000000 | bytes 2000000 | tf_op jit(solution)/shard_map/pallas_call | solution.py:642
  47.8 0.0 collective-permute-done.near_rim_ref
  47.8 0.4 collective-permute-done.1.far_rim_ref
  48.2 1.8 %shard_map.141 = (f32[2048,128]{1,0:T(8,128)S(1)}, f32[2048,128]{1,0:T(8,128)S(1)}, f32[512,128]{1,0:T(8,128)S(1)}, f32[2048,128]{1,0:T(8,128)S(1)}, f32[2,64,51...) custom-call(s32[1]{0:T(128)} %bitcast.position_ref, ...), custom_call_target="tpu_custom_call" | custom-call | flops 2000000 | bytes 2000000 | tf_op jit(solution)/shard_map/pallas_call | solution.py:650
  50.1 1.3 %collective-permute-start.4 = (f32[1,64,512]{2,1,0:T(8,128)S(1)}, f32[1,64,512]{2,1,0:T(8,128)S(1)}, u32[]{:S(2)}, u32[]{:S(2)}) collective-permute-start(f32[1,64,512]{2,1,0:T(8,128)S(1)} %get-tuple-element.53), channel_id=1, source_target_pairs={{0,1},{1,0},{2,3},{3,2},{4,5},{5,4},{6,7},{7,6},{8,9},{9,8},{10,11... | collective-permute-start | bytes 393224 | tf_op jit(solution)/shard_map/ppermute | solution.py:668
  51.3 0.0 collective-permute-start.2
  51.3 4.2 %collective-permute-start.3 = (f32[128,128]{1,0:T(8,128)S(1)}, f32[128,128]{1,0:T(8,128)S(1)}, u32[]{:S(2)}, u32[]{:S(2)}) collective-permute-start(f32[128,128]{1,0:T(8,128)S(1)} %get-tuple-element.46), channel_id=1, source_target_pairs={{2,4},{4,2},{6,8},{8,6},{10,12},{12,10},{14,16},{16,14},{18,20},{2... | collective-permute-start | bytes 196616 | tf_op jit(solution)/shard_map/ppermute | solution.py:570
  55.5 3.1 %shard_map.142 = (f32[2,64,1024]{2,1,0:T(8,128)}, f32[2,64,1024]{2,1,0:T(8,128)}, f32[1024,128]{1,0:T(8,128)S(1)}) custom-call(f32[2208,128]{1,0:T(8,128)S(1)} %bitcast.8, f32[2048,128]{1,0:T(8,128)S(1)} %get-tuple-element.41.new_ref, f32[256,256]{1,0:T(8,128)S(1)} %get-tuple-element.42.acc0), custom_call_target="tpu_custom_call" | custom-call | flops 2000000 | bytes 2000000 | tf_op jit(solution)/shard_map/pallas_call | solution.py:670
  58.6 0.0 collective-permute-done.2.near_rim_ref
  58.6 0.0 collective-permute-done.3.far_rim_ref
  58.6 0.0 collective-permute-done.4.rest_1_
  58.6 1.8 %shard_map.143 = (f32[2,64,1024]{2,1,0:T(8,128)}, f32[2,64,1024]{2,1,0:T(8,128)}, f32[64,512]{1,0:T(8,128)}) custom-call(f32[2048,128]{1,0:T(8,128)S(1)} %get-tuple-element.38.base_ref, f32[512,128]{1,0:T(8,128)S(1)} %get-tuple-element.39.factor_ref, f32[2048,128]{1,0:T(8,128)S(1)} %get-tuple-element.40.next_ref, ...), custom_call_target="tpu_custom_call" | custom-call | flops 2000000 | bytes 2000000 | tf_op jit(solution)/shard_map/pallas_call | solution.py:680
  (1 shorter events, 0.0 us)
Async XLA Ops:
  5.9 33.3 %all-to-all-start = ((f32[16,69,2,128]{3,2,1,0:T(2,128)}), f32[16,69,2,128]{3,2,1,0:T(2,128)S(1)}, u32[]{:S(2)}, u32[]{:S(2)}) async-start(f32[16,69,2,128]{3,2,1,0:T(2,128)} %bitcast.3), calls=%async_computation | async-start | bytes 2260992 | tf_op jit(solution)/shard_map/all_to_all | solution.py:619
  40.9 6.9 %collective-permute-start = (f32[224,128]{1,0:T(8,128)S(1)}, f32[224,128]{1,0:T(8,128)S(1)}, u32[]{:S(2)}, u32[]{:S(2)}) collective-permute-start(f32[224,128]{1,0:T(8,128)S(1)} %get-tuple-element.36), channel_id=1, source_target_pairs={{0,2},{2,0},{4,6},{6,4},{8,10},{10,8},{12,14},{14,12},{16,18},{18,... | collective-permute-start | bytes 344072 | tf_op jit(solution)/shard_map/ppermute | solution.py:571
  41.2 7.0 %collective-permute-start.1 = (f32[224,128]{1,0:T(8,128)S(1)}, f32[224,128]{1,0:T(8,128)S(1)}, u32[]{:S(2)}, u32[]{:S(2)}) collective-permute-start(f32[224,128]{1,0:T(8,128)S(1)} %get-tuple-element.37), channel_id=1, source_target_pairs={{2,4},{4,2},{6,8},{8,6},{10,12},{12,10},{14,16},{16,14},{18,20},{2... | collective-permute-start | bytes 344072 | tf_op jit(solution)/shard_map/ppermute | solution.py:570
  50.1 8.6 %collective-permute-start.4 = (f32[1,64,512]{2,1,0:T(8,128)S(1)}, f32[1,64,512]{2,1,0:T(8,128)S(1)}, u32[]{:S(2)}, u32[]{:S(2)}) collective-permute-start(f32[1,64,512]{2,1,0:T(8,128)S(1)} %get-tuple-element.53), channel_id=1, source_target_pairs={{0,1},{1,0},{2,3},{3,2},{4,5},{5,4},{6,7},{7,6},{8,9},{9,8},{10,11... | collective-permute-start | bytes 393224 | tf_op jit(solution)/shard_map/ppermute | solution.py:668
  51.3 7.3 %collective-permute-start.2 = (f32[128,128]{1,0:T(8,128)S(1)}, f32[128,128]{1,0:T(8,128)S(1)}, u32[]{:S(2)}, u32[]{:S(2)}) collective-permute-start(f32[128,128]{1,0:T(8,128)S(1)} %get-tuple-element.45), channel_id=1, source_target_pairs={{0,2},{2,0},{4,6},{6,4},{8,10},{10,8},{12,14},{14,12},{16,18},{18,... | collective-permute-start | bytes 196616 | tf_op jit(solution)/shard_map/ppermute | solution.py:571
  51.3 7.3 %collective-permute-start.3 = (f32[128,128]{1,0:T(8,128)S(1)}, f32[128,128]{1,0:T(8,128)S(1)}, u32[]{:S(2)}, u32[]{:S(2)}) collective-permute-start(f32[128,128]{1,0:T(8,128)S(1)} %get-tuple-element.46), channel_id=1, source_target_pairs={{2,4},{4,2},{6,8},{8,6},{10,12},{12,10},{14,16},{16,14},{18,20},{2... | collective-permute-start | bytes 196616 | tf_op jit(solution)/shard_map/ppermute | solution.py:570

commit v5 on v4

--- a/solution.py
+++ b/solution.py
@@ -166,8 +166,8 @@
 
 
 def place_kernel(
-    owner_hbm, local_hbm, weights_hbm, records_hbm, out_ref, token_ref,
-    owner_ref, local_ref, weights_ref, records_ref, spot_ref, data_ref, sorted_ref, sems,
+    owner_hbm, local_hbm, weights_hbm, records_hbm, out_hbm, token_ref,
+    owner_ref, local_ref, weights_ref, records_ref, spot_ref, data_ref, sorted_ref, out_ref, sems, out_sems,
 ):
     copies = [
         pltpu.make_async_copy(src, dst, sems.at[i])
@@ -234,6 +234,8 @@
     lane = lax.broadcasted_iota(jnp.int32, (SUB, LANE), 1)
     sorted_ref[:, stations:] = jnp.zeros((rows, 3 * LANE), jnp.float32)
 
+    leaving = []
+
     def cut_block(slab):
         begin, size = begins[slab], sizes[slab]
         shift = lax.rem(begin, LANE)
@@ -251,6 +253,10 @@
                 else:
                     piece = jnp.where(lane + j * LANE < size, piece, 0.0)
                     out_ref[pl.ds(slab * packed + 2 * NODES + j * few, few), :] = piece[:few]
+        if slab % 4 == 3:
+            part = pl.ds((slab - 3) * packed, 4 * packed)
+            leaving.append(pltpu.make_async_copy(out_ref.at[part], out_hbm.at[part], out_sems.at[slab // 4]))
+            leaving[-1].start()
 
     for chunk in range(chunks):
         spots = spot_ref[...] - float(chunk * CAP)
@@ -269,6 +275,8 @@
         cut_block(chunk)
     for slab in range(chunks, slabs):
         cut_block(slab)
+    for copy in leaving:
+        copy.wait()
 
 
 def split(full):
@@ -465,7 +473,7 @@
 
 
 def second_kernel(
-    events, share, position_ref, state_ref, now_ref, near_rim_ref, far_rim_ref,
+    events, share, position_ref, state_ref, now_ref, far_rim_ref, near_rim_ref,
     new_ref, base_ref, factor_ref, next_ref, parts_ref, near_ref, far_ref, later_ref, kern_ref,
 ):
     rows, _ = state_rows(events)
@@ -510,9 +518,14 @@
             parts_ref[j, :, k * LANE : (k + 1) * LANE] = kern_ref[pl.ds(owner * tiles + k, NODES, stride=SUB), :]
 
 
-def last_kernel(events, share, base_ref, factor_ref, next_ref, source_ref, later_ref, near_rim_ref, far_rim_ref, *rest):
-    fwd_hbm, adj_hbm, kernel_ref, done_ref, out_ref, sems = rest[share:]
-    copies = []
+def last_kernel(events, share, base_ref, factor_ref, next_ref, source_ref, later_ref, *rest):
+    far_rim_ref, near_rim_ref, fwd_hbm, adj_hbm, kernel_hbm, done_ref, out_ref, kernel_ref, sems = rest[share:]
+    total = rest[0][0]
+    for part in rest[1:share]:
+        total = total + part[0]
+    kernel_ref[...] = total
+    copies = [pltpu.make_async_copy(kernel_ref, kernel_hbm, sems.at[2 * events])]
+    copies[0].start()
     for event in range(events):
         for field, out_hbm in ((event, fwd_hbm), (events + event, adj_hbm)):
             for n in range(NODES):
@@ -524,10 +537,6 @@
             gather_back(done_ref, 0, out_ref, field)
             copies.append(pltpu.make_async_copy(out_ref.at[field], out_hbm.at[event], sems.at[field]))
             copies[-1].start()
-    total = rest[0][0]
-    for part in rest[1:share]:
-        total = total + part[0]
-    kernel_ref[...] = total
     for copy in copies:
         copy.wait()
 
@@ -605,8 +614,11 @@
             ((blocks, LANE), f32),
             ((2 * rows, stations), jnp.bfloat16),
             ((rows, stations + 3 * LANE), f32),
+            ((slabs * packed, LANE), f32),
             pltpu.SemaphoreType.DMA((4,)),
+            pltpu.SemaphoreType.DMA((slabs // 4,)),
         ],
+        written=1,
         count=4,
         outside=4,
         limit=48,
@@ -662,7 +674,7 @@
         [((FIELD, LANE), f32)],
         smem=1,
         count=5,
-    )(lax.axis_index("event").reshape(1).astype(jnp.int32), *kept(state, now), near_rim, far_rim)
+    )(lax.axis_index("event").reshape(1).astype(jnp.int32), *kept(state, now), far_rim, near_rim)
     near_rim, far_rim = beside(near, far)
     pieces = [parts[0:1]] + [
         lax.ppermute(parts[j : j + 1], "event", [(i, (i + j) % share) for i in range(share)]) for j in range(1, share)
@@ -680,10 +692,15 @@
     fwd_last, adj_last, kernel = call(
         functools.partial(last_kernel, events, share),
         [fwd_now.shape, adj_now.shape, (NODES, elements // share)],
-        [((FIELD, LANE), f32), ((2 * events, NODES, elements), f32), pltpu.SemaphoreType.DMA((2 * events,))],
+        [
+            ((FIELD, LANE), f32),
+            ((2 * events, NODES, elements), f32),
+            ((NODES, elements // share), f32),
+            pltpu.SemaphoreType.DMA((2 * events + 1,)),
+        ],
         count=7 + share,
-        written=2,
-    )(*kept(base, factor, after, source, later), near_rim, far_rim, *pieces)
+        written=3,
+    )(*kept(base, factor, after, source, later), *pieces, far_rim, near_rim)
     return fwd_last, fwd_before, adj_last, adj_before, kernel
 
 

time: 60.7 us -> 59.5 us (0.980)
  Pallas kernels: 23.1 us -> 22.3 us
    pallas_call x1, Pallas kernels: 1.78 us -> 1.14 us  [shards(): call(functools.partial(last_kernel, events, share), [fwd_now.shape, adj_n...]
where the time goes in v5:
time: 59.5 us; the launch traced here: 59.1 us
  Pallas kernels  22.3 us (37%)
  waiting for transfers between devices  20.6 us (35%)
  starting transfers between devices  15.5 us (26%)
  between operations  0.74 us (1%)
    all_to_all x1, waiting for transfers between devices, shards(): lax.all_to_all(send, 'space', split_axis=0, concat_axis=0, tiled=True)  20.5 us
    ppermute x2, starting transfers between devices, beside(): from_far = lax.ppermute(far, 'space', inner)  7.52 us
    all_to_all x1, starting transfers between devices, shards(): lax.all_to_all(send, 'space', split_axis=0, concat_axis=0, tiled=True)  6.57 us
    pallas_call x1, Pallas kernels, shards(): call(functools.partial(first_kernel, events), [off_core((state_rows(event...  6.24 us
    pallas_call x1, Pallas kernels, shards(): call(place_kernel, [(slabs * packed, LANE), near_core((SUB, LANE))], [((b...  5.07 us
    pallas_call x1, Pallas kernels, shards(): call(functools.partial(land_first_kernel, events), [near_core(state.shape...  3.23 us
    pallas_call x1, Pallas kernels, shards(): call(functools.partial(land_later_kernel, events), [fwd_now.shape, adj_no...  3.06 us
    pallas_call x1, Pallas kernels, shards(): call(functools.partial(second_kernel, events, share), [near_core((2 * eve...  1.82 us
  transfers between devices with their start and end apart: 6, of which 2 were waited for; matrix products, arithmetic and copies ran while one was open for 0% of the time, Pallas kernels for 21%

profile of v5, /device:TPU:13, one launch (start us, length us, event | category | flops | bytes accessed | tf_op | source)
XLA Modules:
  0.0 59.1 jit_solution(6066319828513409825)
XLA Ops:
  0.6 5.1 %shard_map.137 = (f32[2208,128]{1,0:T(8,128)}, f32[8,128]{1,0:T(8,128)S(1)}) custom-call(s32[16,128]{1,0:T(8,128)} %bitcast.9, s32[16,128]{1,0:T(8,128)} %bitcast.10, f32[64,2048]{1,0:T(8,128)} %weights_hbm.1, f32[2,2,2048]{2,1,0:T(2,128)} %records_hbm.1), custom_call_target="tpu_custom_call" | custom-call | flops 2000000 | bytes 2000000 | tf_op jit(solution)/shard_map/pallas_call | solution.py:606
  5.7 6.6 %all-to-all-start = ((f32[16,69,2,128]{3,2,1,0:T(2,128)}), f32[16,69,2,128]{3,2,1,0:T(2,128)S(1)}, u32[]{:S(2)}, u32[]{:S(2)}) async-start(f32[16,69,2,128]{3,2,1,0:T(2,128)} %bitcast.3), calls=%async_computation | async-start | bytes 2260992 | tf_op jit(solution)/shard_map/all_to_all | solution.py:631
  12.3 6.2 %shard_map.138 = (f32[5632,128]{1,0:T(8,128)}, f32[2048,128]{1,0:T(8,128)}, f32[320,128]{1,0:T(8,128)}) custom-call(f32[2,64,1024]{2,1,0:T(8,128)} %fwd_ref.1, f32[2,64,1024]{2,1,0:T(8,128)} %fwd_prev_ref.1, f32[2,64,1024]{2,1,0:T(8,128)} %adj_ref.1, f32[2,64,1024]{2,1,0:T(8,128)} %adj_prev_ref.1, f32[64,1024]{1,0:T(8,128)} %shear_ref.1, f32[8,128]{1,0:T(8,128)} %bitcast.11, ...), custom_call_target="tpu_custom_call" | custom-call | flops 2000000 | bytes 2000000 | tf_op jit(solution)/shard_map/pallas_call | solution.py:634
  18.5 20.5 %all-to-all-done = f32[16,69,2,128]{3,2,1,0:T(2,128)S(1)} async-done(((f32[16,69,2,128]{3,2,1,0:T(2,128)}), f32[16,69,2,128]{3,2,1,0:T(2,128)S(1)}, u32[]{:S(2)}, u32[]{:S(2)}) %all-to-all-start) | async-done | bytes 1130528 | tf_op jit(solution)/shard_map/all_to_all | solution.py:631
  39.0 1.7 %shard_map.140 = (f32[224,128]{1,0:T(8,128)S(1)}, f32[224,128]{1,0:T(8,128)S(1)}) custom-call(f32[2208,128]{1,0:T(8,128)S(1)} %bitcast.6, f32[320,128]{1,0:T(8,128)} %get-tuple-element.35.faces_hbm), custom_call_target="tpu_custom_call" | custom-call | flops 2000000 | bytes 2000000 | tf_op jit(solution)/shard_map/pallas_call | solution.py:644
  40.7 3.6 %collective-permute-start = (f32[224,128]{1,0:T(8,128)S(1)}, f32[224,128]{1,0:T(8,128)S(1)}, u32[]{:S(2)}, u32[]{:S(2)}) collective-permute-start(f32[224,128]{1,0:T(8,128)S(1)} %get-tuple-element.36), channel_id=1, source_target_pairs={{2,4},{4,2},{6,8},{8,6},{10,12},{12,10},{14,16},{16,14},{18,20},{2... | collective-permute-start | bytes 344072 | tf_op jit(solution)/shard_map/ppermute | solution.py:579
  44.3 0.1 collective-permute-start.1
  44.4 3.2 %shard_map.139 = (f32[5632,128]{1,0:T(8,128)S(1)}, f32[2048,128]{1,0:T(8,128)S(1)}, f32[256,256]{1,0:T(8,128)S(1)}) custom-call(f32[2208,128]{1,0:T(8,128)S(1)} %bitcast.7, f32[5632,128]{1,0:T(8,128)} %get-tuple-element.31.state_hbm, f32[2048,128]{1,0:T(8,128)} %get-tuple-element.32.now_hbm), custom_call_target="tpu_custom_call" | custom-call | flops 2000000 | bytes 2000000 | tf_op jit(solution)/shard_map/pallas_call | solution.py:654
  47.6 0.1 collective-permute-done.far_rim_ref
  47.7 0.0 collective-permute-done.1.near_rim_ref
  47.7 1.8 %shard_map.141 = (f32[2048,128]{1,0:T(8,128)S(1)}, f32[2048,128]{1,0:T(8,128)S(1)}, f32[512,128]{1,0:T(8,128)S(1)}, f32[2048,128]{1,0:T(8,128)S(1)}, f32[2,64,51...) custom-call(s32[1]{0:T(128)} %bitcast.position_ref, ...), custom_call_target="tpu_custom_call" | custom-call | flops 2000000 | bytes 2000000 | tf_op jit(solution)/shard_map/pallas_call | solution.py:662
  49.6 1.3 %collective-permute-start.2 = (f32[1,64,512]{2,1,0:T(8,128)S(1)}, f32[1,64,512]{2,1,0:T(8,128)S(1)}, u32[]{:S(2)}, u32[]{:S(2)}) collective-permute-start(f32[1,64,512]{2,1,0:T(8,128)S(1)} %get-tuple-element.53), channel_id=1, source_target_pairs={{0,1},{1,0},{2,3},{3,2},{4,5},{5,4},{6,7},{7,6},{8,9},{9,8},{10,11... | collective-permute-start | bytes 393224 | tf_op jit(solution)/shard_map/ppermute | solution.py:680
  50.9 3.9 %collective-permute-start.3 = (f32[128,128]{1,0:T(8,128)S(1)}, f32[128,128]{1,0:T(8,128)S(1)}, u32[]{:S(2)}, u32[]{:S(2)}) collective-permute-start(f32[128,128]{1,0:T(8,128)S(1)} %get-tuple-element.46), channel_id=1, source_target_pairs={{2,4},{4,2},{6,8},{8,6},{10,12},{12,10},{14,16},{16,14},{18,20},{2... | collective-permute-start | bytes 196616 | tf_op jit(solution)/shard_map/ppermute | solution.py:579
  54.8 0.1 collective-permute-start.4
  54.9 3.1 %shard_map.142 = (f32[2,64,1024]{2,1,0:T(8,128)}, f32[2,64,1024]{2,1,0:T(8,128)}, f32[1024,128]{1,0:T(8,128)S(1)}) custom-call(f32[2208,128]{1,0:T(8,128)S(1)} %bitcast.8, f32[2048,128]{1,0:T(8,128)S(1)} %get-tuple-element.41.new_ref, f32[256,256]{1,0:T(8,128)S(1)} %get-tuple-element.42.acc0), custom_call_target="tpu_custom_call" | custom-call | flops 2000000 | bytes 2000000 | tf_op jit(solution)/shard_map/pallas_call | solution.py:682
  58.0 0.0 collective-permute-done.3.rest_2_
  58.0 0.0 collective-permute-done.4.rest_3_
  58.0 0.0 collective-permute-done.2.rest_1_
  58.0 1.1 %shard_map.143 = (f32[2,64,1024]{2,1,0:T(8,128)}, f32[2,64,1024]{2,1,0:T(8,128)}, f32[64,512]{1,0:T(8,128)}) custom-call(f32[2048,128]{1,0:T(8,128)S(1)} %get-tuple-element.38.base_ref, f32[512,128]{1,0:T(8,128)S(1)} %get-tuple-element.39.factor_ref, f32[2048,128]{1,0:T(8,128)S(1)} %get-tuple-element.40.next_ref, ...), custom_call_target="tpu_custom_call" | custom-call | flops 2000000 | bytes 2000000 | tf_op jit(solution)/shard_map/pallas_call | solution.py:692
  (1 shorter events, 0.0 us)
Async XLA Ops:
  5.7 33.3 %all-to-all-start = ((f32[16,69,2,128]{3,2,1,0:T(2,128)}), f32[16,69,2,128]{3,2,1,0:T(2,128)S(1)}, u32[]{:S(2)}, u32[]{:S(2)}) async-start(f32[16,69,2,128]{3,2,1,0:T(2,128)} %bitcast.3), calls=%async_computation | async-start | bytes 2260992 | tf_op jit(solution)/shard_map/all_to_all | solution.py:631
  40.7 7.0 %collective-permute-start = (f32[224,128]{1,0:T(8,128)S(1)}, f32[224,128]{1,0:T(8,128)S(1)}, u32[]{:S(2)}, u32[]{:S(2)}) collective-permute-start(f32[224,128]{1,0:T(8,128)S(1)} %get-tuple-element.36), channel_id=1, source_target_pairs={{2,4},{4,2},{6,8},{8,6},{10,12},{12,10},{14,16},{16,14},{18,20},{2... | collective-permute-start | bytes 344072 | tf_op jit(solution)/shard_map/ppermute | solution.py:579
  44.3 3.4 %collective-permute-start.1 = (f32[224,128]{1,0:T(8,128)S(1)}, f32[224,128]{1,0:T(8,128)S(1)}, u32[]{:S(2)}, u32[]{:S(2)}) collective-permute-start(f32[224,128]{1,0:T(8,128)S(1)} %get-tuple-element.37), channel_id=1, source_target_pairs={{0,2},{2,0},{4,6},{6,4},{8,10},{10,8},{12,14},{14,12},{16,18},{18,... | collective-permute-start | bytes 344072 | tf_op jit(solution)/shard_map/ppermute | solution.py:580
  49.6 8.4 %collective-permute-start.2 = (f32[1,64,512]{2,1,0:T(8,128)S(1)}, f32[1,64,512]{2,1,0:T(8,128)S(1)}, u32[]{:S(2)}, u32[]{:S(2)}) collective-permute-start(f32[1,64,512]{2,1,0:T(8,128)S(1)} %get-tuple-element.53), channel_id=1, source_target_pairs={{0,1},{1,0},{2,3},{3,2},{4,5},{5,4},{6,7},{7,6},{8,9},{9,8},{10,11... | collective-permute-start | bytes 393224 | tf_op jit(solution)/shard_map/ppermute | solution.py:680
  50.9 7.1 %collective-permute-start.3 = (f32[128,128]{1,0:T(8,128)S(1)}, f32[128,128]{1,0:T(8,128)S(1)}, u32[]{:S(2)}, u32[]{:S(2)}) collective-permute-start(f32[128,128]{1,0:T(8,128)S(1)} %get-tuple-element.46), channel_id=1, source_target_pairs={{2,4},{4,2},{6,8},{8,6},{10,12},{12,10},{14,16},{16,14},{18,20},{2... | collective-permute-start | bytes 196616 | tf_op jit(solution)/shard_map/ppermute | solution.py:579
  54.8 3.2 %collective-permute-start.4 = (f32[128,128]{1,0:T(8,128)S(1)}, f32[128,128]{1,0:T(8,128)S(1)}, u32[]{:S(2)}, u32[]{:S(2)}) collective-permute-start(f32[128,128]{1,0:T(8,128)S(1)} %get-tuple-element.47), channel_id=1, source_target_pairs={{0,2},{2,0},{4,6},{6,4},{8,10},{10,8},{12,14},{14,12},{16,18},{18,... | collective-permute-start | bytes 196616 | tf_op jit(solution)/shard_map/ppermute | solution.py:580

commit v6 on v5

--- a/solution.py
+++ b/solution.py
@@ -166,8 +166,8 @@
 
 
 def place_kernel(
-    owner_hbm, local_hbm, weights_hbm, records_hbm, out_hbm, token_ref,
-    owner_ref, local_ref, weights_ref, records_ref, spot_ref, data_ref, sorted_ref, out_ref, sems, out_sems,
+    owner_hbm, local_hbm, weights_hbm, records_hbm, out_ref, token_ref,
+    owner_ref, local_ref, weights_ref, records_ref, spot_ref, data_ref, sorted_ref, sems,
 ):
     copies = [
         pltpu.make_async_copy(src, dst, sems.at[i])
@@ -234,29 +234,22 @@
     lane = lax.broadcasted_iota(jnp.int32, (SUB, LANE), 1)
     sorted_ref[:, stations:] = jnp.zeros((rows, 3 * LANE), jnp.float32)
 
-    leaving = []
-
     def cut_block(slab):
         begin, size = begins[slab], sizes[slab]
         shift = lax.rem(begin, LANE)
         base = begin - shift
-        turn = lax.rem(LANE - shift, LANE)
-        kept_lanes = lane >= shift
+        late = lane >= shift
+        slots = (jnp.where(late, lane - shift, lane + 2 * LANE - shift), lane + LANE - shift)
         for first in range(0, rows, SUB):
             tiles = [
                 sorted_ref[first : first + SUB, pl.ds(pl.multiple_of(base + j * LANE, LANE), LANE)] for j in range(3)
             ]
-            for j in range(2):
-                piece = pltpu.roll(jnp.where(kept_lanes, tiles[j], tiles[j + 1]), turn, 1)
+            for j, piece in enumerate((jnp.where(late, tiles[0], tiles[2]), tiles[1])):
                 if first < NODES:
                     out_ref[pl.ds(slab * packed + j * NODES + first, SUB), :] = piece
                 else:
-                    piece = jnp.where(lane + j * LANE < size, piece, 0.0)
+                    piece = jnp.where(slots[j] < size, piece, 0.0)
                     out_ref[pl.ds(slab * packed + 2 * NODES + j * few, few), :] = piece[:few]
-        if slab % 4 == 3:
-            part = pl.ds((slab - 3) * packed, 4 * packed)
-            leaving.append(pltpu.make_async_copy(out_ref.at[part], out_hbm.at[part], out_sems.at[slab // 4]))
-            leaving[-1].start()
 
     for chunk in range(chunks):
         spots = spot_ref[...] - float(chunk * CAP)
@@ -275,8 +268,6 @@
         cut_block(chunk)
     for slab in range(chunks, slabs):
         cut_block(slab)
-    for copy in leaving:
-        copy.wait()
 
 
 def split(full):
@@ -605,7 +596,7 @@
 
     send, token = call(
         place_kernel,
-        [(slabs * packed, LANE), near_core((SUB, LANE))],
+        [near_core((slabs * packed, LANE)), near_core((SUB, LANE))],
         [
             ((blocks, LANE), jnp.int32),
             ((blocks, LANE), jnp.int32),
@@ -614,11 +605,8 @@
             ((blocks, LANE), f32),
             ((2 * rows, stations), jnp.bfloat16),
             ((rows, stations + 3 * LANE), f32),
-            ((slabs * packed, LANE), f32),
             pltpu.SemaphoreType.DMA((4,)),
-            pltpu.SemaphoreType.DMA((slabs // 4,)),
         ],
-        written=1,
         count=4,
         outside=4,
         limit=48,

time: 59.5 us -> 59.6 us (level)
  no operation moved by 1% of the time
where the time goes in v6:
time: 59.6 us; the launch traced here: 59.1 us
  Pallas kernels  22.3 us (37%)
  waiting for transfers between devices  20.6 us (35%)
  starting transfers between devices  15.5 us (26%)
  between operations  0.74 us (1%)
    all_to_all x1, waiting for transfers between devices, shards(): lax.all_to_all(send, 'space', split_axis=0, concat_axis=0, tiled=True)  20.5 us
    ppermute x2, starting transfers between devices, beside(): from_far = lax.ppermute(far, 'space', inner)  7.51 us
    all_to_all x1, starting transfers between devices, shards(): lax.all_to_all(send, 'space', split_axis=0, concat_axis=0, tiled=True)  6.57 us
    pallas_call x1, Pallas kernels, shards(): call(functools.partial(first_kernel, events), [off_core((state_rows(event...  6.24 us
    pallas_call x1, Pallas kernels, shards(): call(place_kernel, [near_core((slabs * packed, LANE)), near_core((SUB, LA...  5.09 us
    pallas_call x1, Pallas kernels, shards(): call(functools.partial(land_first_kernel, events), [near_core(state.shape...  3.22 us
    pallas_call x1, Pallas kernels, shards(): call(functools.partial(land_later_kernel, events), [fwd_now.shape, adj_no...  3.06 us
    pallas_call x1, Pallas kernels, shards(): call(functools.partial(second_kernel, events, share), [near_core((2 * eve...  1.82 us
  transfers between devices with their start and end apart: 6, of which 2 were waited for; matrix products, arithmetic and copies ran while one was open for 0% of the time, Pallas kernels for 21%

profile of v6, /device:TPU:13, one launch (start us, length us, event | category | flops | bytes accessed | tf_op | source)
XLA Modules:
  0.0 59.1 jit_solution(14412978569453950048)
XLA Ops:
  0.6 5.1 %shard_map.137 = (f32[2208,128]{1,0:T(8,128)}, f32[8,128]{1,0:T(8,128)S(1)}) custom-call(s32[16,128]{1,0:T(8,128)} %bitcast.9, s32[16,128]{1,0:T(8,128)} %bitcast.10, f32[64,2048]{1,0:T(8,128)} %weights_hbm.1, f32[2,2,2048]{2,1,0:T(2,128)} %records_hbm.1), custom_call_target="tpu_custom_call" | custom-call | flops 2000000 | bytes 2000000 | tf_op jit(solution)/shard_map/pallas_call | solution.py:597
  5.7 6.6 %all-to-all-start = ((f32[16,69,2,128]{3,2,1,0:T(2,128)}), f32[16,69,2,128]{3,2,1,0:T(2,128)S(1)}, u32[]{:S(2)}, u32[]{:S(2)}) async-start(f32[16,69,2,128]{3,2,1,0:T(2,128)} %bitcast.3), calls=%async_computation | async-start | bytes 2260992 | tf_op jit(solution)/shard_map/all_to_all | solution.py:619
  12.3 6.2 %shard_map.138 = (f32[5632,128]{1,0:T(8,128)}, f32[2048,128]{1,0:T(8,128)}, f32[320,128]{1,0:T(8,128)}) custom-call(f32[2,64,1024]{2,1,0:T(8,128)} %fwd_ref.1, f32[2,64,1024]{2,1,0:T(8,128)} %fwd_prev_ref.1, f32[2,64,1024]{2,1,0:T(8,128)} %adj_ref.1, f32[2,64,1024]{2,1,0:T(8,128)} %adj_prev_ref.1, f32[64,1024]{1,0:T(8,128)} %shear_ref.1, f32[8,128]{1,0:T(8,128)} %bitcast.11, ...), custom_call_target="tpu_custom_call" | custom-call | flops 2000000 | bytes 2000000 | tf_op jit(solution)/shard_map/pallas_call | solution.py:622
  18.5 20.5 %all-to-all-done = f32[16,69,2,128]{3,2,1,0:T(2,128)S(1)} async-done(((f32[16,69,2,128]{3,2,1,0:T(2,128)}), f32[16,69,2,128]{3,2,1,0:T(2,128)S(1)}, u32[]{:S(2)}, u32[]{:S(2)}) %all-to-all-start) | async-done | bytes 1130528 | tf_op jit(solution)/shard_map/all_to_all | solution.py:619
  39.0 1.7 %shard_map.140 = (f32[224,128]{1,0:T(8,128)S(1)}, f32[224,128]{1,0:T(8,128)S(1)}) custom-call(f32[2208,128]{1,0:T(8,128)S(1)} %bitcast.6, f32[320,128]{1,0:T(8,128)} %get-tuple-element.35.faces_hbm), custom_call_target="tpu_custom_call" | custom-call | flops 2000000 | bytes 2000000 | tf_op jit(solution)/shard_map/pallas_call | solution.py:632
  40.7 3.6 %collective-permute-start = (f32[224,128]{1,0:T(8,128)S(1)}, f32[224,128]{1,0:T(8,128)S(1)}, u32[]{:S(2)}, u32[]{:S(2)}) collective-permute-start(f32[224,128]{1,0:T(8,128)S(1)} %get-tuple-element.36), channel_id=1, source_target_pairs={{2,4},{4,2},{6,8},{8,6},{10,12},{12,10},{14,16},{16,14},{18,20},{2... | collective-permute-start | bytes 344072 | tf_op jit(solution)/shard_map/ppermute | solution.py:570
  44.3 0.1 collective-permute-start.1
  44.4 3.2 %shard_map.139 = (f32[5632,128]{1,0:T(8,128)S(1)}, f32[2048,128]{1,0:T(8,128)S(1)}, f32[256,256]{1,0:T(8,128)S(1)}) custom-call(f32[2208,128]{1,0:T(8,128)S(1)} %bitcast.7, f32[5632,128]{1,0:T(8,128)} %get-tuple-element.31.state_hbm, f32[2048,128]{1,0:T(8,128)} %get-tuple-element.32.now_hbm), custom_call_target="tpu_custom_call" | custom-call | flops 2000000 | bytes 2000000 | tf_op jit(solution)/shard_map/pallas_call | solution.py:642
  47.6 0.1 collective-permute-done.far_rim_ref
  47.7 0.0 collective-permute-done.1.near_rim_ref
  47.8 1.8 %shard_map.141 = (f32[2048,128]{1,0:T(8,128)S(1)}, f32[2048,128]{1,0:T(8,128)S(1)}, f32[512,128]{1,0:T(8,128)S(1)}, f32[2048,128]{1,0:T(8,128)S(1)}, f32[2,64,51...) custom-call(s32[1]{0:T(128)} %bitcast.position_ref, ...), custom_call_target="tpu_custom_call" | custom-call | flops 2000000 | bytes 2000000 | tf_op jit(solution)/shard_map/pallas_call | solution.py:650
  49.6 1.3 %collective-permute-start.2 = (f32[1,64,512]{2,1,0:T(8,128)S(1)}, f32[1,64,512]{2,1,0:T(8,128)S(1)}, u32[]{:S(2)}, u32[]{:S(2)}) collective-permute-start(f32[1,64,512]{2,1,0:T(8,128)S(1)} %get-tuple-element.53), channel_id=1, source_target_pairs={{0,1},{1,0},{2,3},{3,2},{4,5},{5,4},{6,7},{7,6},{8,9},{9,8},{10,11... | collective-permute-start | bytes 393224 | tf_op jit(solution)/shard_map/ppermute | solution.py:668
  50.9 3.9 %collective-permute-start.3 = (f32[128,128]{1,0:T(8,128)S(1)}, f32[128,128]{1,0:T(8,128)S(1)}, u32[]{:S(2)}, u32[]{:S(2)}) collective-permute-start(f32[128,128]{1,0:T(8,128)S(1)} %get-tuple-element.46), channel_id=1, source_target_pairs={{2,4},{4,2},{6,8},{8,6},{10,12},{12,10},{14,16},{16,14},{18,20},{2... | collective-permute-start | bytes 196616 | tf_op jit(solution)/shard_map/ppermute | solution.py:570
  54.8 0.1 collective-permute-start.4
  54.9 3.1 %shard_map.142 = (f32[2,64,1024]{2,1,0:T(8,128)}, f32[2,64,1024]{2,1,0:T(8,128)}, f32[1024,128]{1,0:T(8,128)S(1)}) custom-call(f32[2208,128]{1,0:T(8,128)S(1)} %bitcast.8, f32[2048,128]{1,0:T(8,128)S(1)} %get-tuple-element.41.new_ref, f32[256,256]{1,0:T(8,128)S(1)} %get-tuple-element.42.acc0), custom_call_target="tpu_custom_call" | custom-call | flops 2000000 | bytes 2000000 | tf_op jit(solution)/shard_map/pallas_call | solution.py:670
  58.0 0.0 collective-permute-done.3.rest_2_
  58.0 0.0 collective-permute-done.4.rest_3_
  58.0 0.0 collective-permute-done.2.rest_1_
  58.0 1.1 %shard_map.143 = (f32[2,64,1024]{2,1,0:T(8,128)}, f32[2,64,1024]{2,1,0:T(8,128)}, f32[64,512]{1,0:T(8,128)}) custom-call(f32[2048,128]{1,0:T(8,128)S(1)} %get-tuple-element.38.base_ref, f32[512,128]{1,0:T(8,128)S(1)} %get-tuple-element.39.factor_ref, f32[2048,128]{1,0:T(8,128)S(1)} %get-tuple-element.40.next_ref, ...), custom_call_target="tpu_custom_call" | custom-call | flops 2000000 | bytes 2000000 | tf_op jit(solution)/shard_map/pallas_call | solution.py:680
  (1 shorter events, 0.0 us)
Async XLA Ops:
  5.7 33.3 %all-to-all-start = ((f32[16,69,2,128]{3,2,1,0:T(2,128)}), f32[16,69,2,128]{3,2,1,0:T(2,128)S(1)}, u32[]{:S(2)}, u32[]{:S(2)}) async-start(f32[16,69,2,128]{3,2,1,0:T(2,128)} %bitcast.3), calls=%async_computation | async-start | bytes 2260992 | tf_op jit(solution)/shard_map/all_to_all | solution.py:619
  40.7 7.0 %collective-permute-start = (f32[224,128]{1,0:T(8,128)S(1)}, f32[224,128]{1,0:T(8,128)S(1)}, u32[]{:S(2)}, u32[]{:S(2)}) collective-permute-start(f32[224,128]{1,0:T(8,128)S(1)} %get-tuple-element.36), channel_id=1, source_target_pairs={{2,4},{4,2},{6,8},{8,6},{10,12},{12,10},{14,16},{16,14},{18,20},{2... | collective-permute-start | bytes 344072 | tf_op jit(solution)/shard_map/ppermute | solution.py:570
  44.3 3.4 %collective-permute-start.1 = (f32[224,128]{1,0:T(8,128)S(1)}, f32[224,128]{1,0:T(8,128)S(1)}, u32[]{:S(2)}, u32[]{:S(2)}) collective-permute-start(f32[224,128]{1,0:T(8,128)S(1)} %get-tuple-element.37), channel_id=1, source_target_pairs={{0,2},{2,0},{4,6},{6,4},{8,10},{10,8},{12,14},{14,12},{16,18},{18,... | collective-permute-start | bytes 344072 | tf_op jit(solution)/shard_map/ppermute | solution.py:571
  49.6 8.4 %collective-permute-start.2 = (f32[1,64,512]{2,1,0:T(8,128)S(1)}, f32[1,64,512]{2,1,0:T(8,128)S(1)}, u32[]{:S(2)}, u32[]{:S(2)}) collective-permute-start(f32[1,64,512]{2,1,0:T(8,128)S(1)} %get-tuple-element.53), channel_id=1, source_target_pairs={{0,1},{1,0},{2,3},{3,2},{4,5},{5,4},{6,7},{7,6},{8,9},{9,8},{10,11... | collective-permute-start | bytes 393224 | tf_op jit(solution)/shard_map/ppermute | solution.py:668
  50.9 7.1 %collective-permute-start.3 = (f32[128,128]{1,0:T(8,128)S(1)}, f32[128,128]{1,0:T(8,128)S(1)}, u32[]{:S(2)}, u32[]{:S(2)}) collective-permute-start(f32[128,128]{1,0:T(8,128)S(1)} %get-tuple-element.46), channel_id=1, source_target_pairs={{2,4},{4,2},{6,8},{8,6},{10,12},{12,10},{14,16},{16,14},{18,20},{2... | collective-permute-start | bytes 196616 | tf_op jit(solution)/shard_map/ppermute | solution.py:570
  54.8 3.2 %collective-permute-start.4 = (f32[128,128]{1,0:T(8,128)S(1)}, f32[128,128]{1,0:T(8,128)S(1)}, u32[]{:S(2)}, u32[]{:S(2)}) collective-permute-start(f32[128,128]{1,0:T(8,128)S(1)} %get-tuple-element.47), channel_id=1, source_target_pairs={{0,2},{2,0},{4,6},{6,4},{8,10},{10,8},{12,14},{14,12},{16,18},{18,... | collective-permute-start | bytes 196616 | tf_op jit(solution)/shard_map/ppermute | solution.py:571

commit v7 on v6

--- a/solution.py
+++ b/solution.py
@@ -518,14 +518,14 @@
     copies = [pltpu.make_async_copy(kernel_ref, kernel_hbm, sems.at[2 * events])]
     copies[0].start()
     for event in range(events):
-        for field, out_hbm in ((event, fwd_hbm), (events + event, adj_hbm)):
+        for field, out_hbm in ((events + event, adj_hbm), (event, fwd_hbm)):
             for n in range(NODES):
                 force = with_rim(at(next_ref, field * FIELD, n)[...], n, near_rim_ref, far_rim_ref, field * FACE)
                 if field >= events:
                     source = at(source_ref, event * FIELD, n)[...]
                     force = force - with_rim(source, n, later_ref.at[0], later_ref.at[1], event * FACE)
-                at(done_ref, 0, n)[...] = at(base_ref, field * FIELD, n)[...] - at(factor_ref, 0, n)[...] * force
-            gather_back(done_ref, 0, out_ref, field)
+                at(done_ref, field * FIELD, n)[...] = at(base_ref, field * FIELD, n)[...] - at(factor_ref, 0, n)[...] * force
+            gather_back(done_ref, field * FIELD, out_ref, field)
             copies.append(pltpu.make_async_copy(out_ref.at[field], out_hbm.at[event], sems.at[field]))
             copies[-1].start()
     for copy in copies:
@@ -681,7 +681,7 @@
         functools.partial(last_kernel, events, share),
         [fwd_now.shape, adj_now.shape, (NODES, elements // share)],
         [
-            ((FIELD, LANE), f32),
+            ((2 * events * FIELD, LANE), f32),
             ((2 * events, NODES, elements), f32),
             ((NODES, elements // share), f32),
             pltpu.SemaphoreType.DMA((2 * events + 1,)),

time: 59.6 us -> 59.6 us (level)
  no operation moved by 1% of the time
where the time goes in v7:
time: 59.6 us; the launch traced here: 59.2 us
  Pallas kernels  22.3 us (37%)
  waiting for transfers between devices  20.6 us (35%)
  starting transfers between devices  15.5 us (26%)
  between operations  0.74 us (1%)
    all_to_all x1, waiting for transfers between devices, shards(): lax.all_to_all(send, 'space', split_axis=0, concat_axis=0, tiled=True)  20.5 us
    ppermute x2, starting transfers between devices, beside(): from_far = lax.ppermute(far, 'space', inner)  7.52 us
    all_to_all x1, starting transfers between devices, shards(): lax.all_to_all(send, 'space', split_axis=0, concat_axis=0, tiled=True)  6.57 us
    pallas_call x1, Pallas kernels, shards(): call(functools.partial(first_kernel, events), [off_core((state_rows(event...  6.24 us
    pallas_call x1, Pallas kernels, shards(): call(place_kernel, [near_core((slabs * packed, LANE)), near_core((SUB, LA...  5.09 us
    pallas_call x1, Pallas kernels, shards(): call(functools.partial(land_first_kernel, events), [near_core(state.shape...  3.23 us
    pallas_call x1, Pallas kernels, shards(): call(functools.partial(land_later_kernel, events), [fwd_now.shape, adj_no...  3.06 us
    pallas_call x1, Pallas kernels, shards(): call(functools.partial(second_kernel, events, share), [near_core((2 * eve...  1.82 us
  transfers between devices with their start and end apart: 6, of which 2 were waited for; matrix products, arithmetic and copies ran while one was open for 0% of the time, Pallas kernels for 21%

profile of v7, /device:TPU:13, one launch (start us, length us, event | category | flops | bytes accessed | tf_op | source)
XLA Modules:
  0.0 59.2 jit_solution(6392776527394780144)
XLA Ops:
  0.6 5.1 %shard_map.137 = (f32[2208,128]{1,0:T(8,128)}, f32[8,128]{1,0:T(8,128)S(1)}) custom-call(s32[16,128]{1,0:T(8,128)} %bitcast.9, s32[16,128]{1,0:T(8,128)} %bitcast.10, f32[64,2048]{1,0:T(8,128)} %weights_hbm.1, f32[2,2,2048]{2,1,0:T(2,128)} %records_hbm.1), custom_call_target="tpu_custom_call" | custom-call | flops 2000000 | bytes 2000000 | tf_op jit(solution)/shard_map/pallas_call | solution.py:597
  5.7 6.6 %all-to-all-start = ((f32[16,69,2,128]{3,2,1,0:T(2,128)}), f32[16,69,2,128]{3,2,1,0:T(2,128)S(1)}, u32[]{:S(2)}, u32[]{:S(2)}) async-start(f32[16,69,2,128]{3,2,1,0:T(2,128)} %bitcast.3), calls=%async_computation | async-start | bytes 2260992 | tf_op jit(solution)/shard_map/all_to_all | solution.py:619
  12.3 6.2 %shard_map.138 = (f32[5632,128]{1,0:T(8,128)}, f32[2048,128]{1,0:T(8,128)}, f32[320,128]{1,0:T(8,128)}) custom-call(f32[2,64,1024]{2,1,0:T(8,128)} %fwd_ref.1, f32[2,64,1024]{2,1,0:T(8,128)} %fwd_prev_ref.1, f32[2,64,1024]{2,1,0:T(8,128)} %adj_ref.1, f32[2,64,1024]{2,1,0:T(8,128)} %adj_prev_ref.1, f32[64,1024]{1,0:T(8,128)} %shear_ref.1, f32[8,128]{1,0:T(8,128)} %bitcast.11, ...), custom_call_target="tpu_custom_call" | custom-call | flops 2000000 | bytes 2000000 | tf_op jit(solution)/shard_map/pallas_call | solution.py:622
  18.5 20.5 %all-to-all-done = f32[16,69,2,128]{3,2,1,0:T(2,128)S(1)} async-done(((f32[16,69,2,128]{3,2,1,0:T(2,128)}), f32[16,69,2,128]{3,2,1,0:T(2,128)S(1)}, u32[]{:S(2)}, u32[]{:S(2)}) %all-to-all-start) | async-done | bytes 1130528 | tf_op jit(solution)/shard_map/all_to_all | solution.py:619
  39.0 1.7 %shard_map.140 = (f32[224,128]{1,0:T(8,128)S(1)}, f32[224,128]{1,0:T(8,128)S(1)}) custom-call(f32[2208,128]{1,0:T(8,128)S(1)} %bitcast.6, f32[320,128]{1,0:T(8,128)} %get-tuple-element.35.faces_hbm), custom_call_target="tpu_custom_call" | custom-call | flops 2000000 | bytes 2000000 | tf_op jit(solution)/shard_map/pallas_call | solution.py:632
  40.7 3.6 %collective-permute-start = (f32[224,128]{1,0:T(8,128)S(1)}, f32[224,128]{1,0:T(8,128)S(1)}, u32[]{:S(2)}, u32[]{:S(2)}) collective-permute-start(f32[224,128]{1,0:T(8,128)S(1)} %get-tuple-element.36), channel_id=1, source_target_pairs={{2,4},{4,2},{6,8},{8,6},{10,12},{12,10},{14,16},{16,14},{18,20},{2... | collective-permute-start | bytes 344072 | tf_op jit(solution)/shard_map/ppermute | solution.py:570
  44.3 0.1 collective-permute-start.1
  44.4 3.2 %shard_map.139 = (f32[5632,128]{1,0:T(8,128)S(1)}, f32[2048,128]{1,0:T(8,128)S(1)}, f32[256,256]{1,0:T(8,128)S(1)}) custom-call(f32[2208,128]{1,0:T(8,128)S(1)} %bitcast.7, f32[5632,128]{1,0:T(8,128)} %get-tuple-element.31.state_hbm, f32[2048,128]{1,0:T(8,128)} %get-tuple-element.32.now_hbm), custom_call_target="tpu_custom_call" | custom-call | flops 2000000 | bytes 2000000 | tf_op jit(solution)/shard_map/pallas_call | solution.py:642
  47.6 0.1 collective-permute-done.far_rim_ref
  47.7 0.0 collective-permute-done.1.near_rim_ref
  47.8 1.8 %shard_map.141 = (f32[2048,128]{1,0:T(8,128)S(1)}, f32[2048,128]{1,0:T(8,128)S(1)}, f32[512,128]{1,0:T(8,128)S(1)}, f32[2048,128]{1,0:T(8,128)S(1)}, f32[2,64,51...) custom-call(s32[1]{0:T(128)} %bitcast.position_ref, ...), custom_call_target="tpu_custom_call" | custom-call | flops 2000000 | bytes 2000000 | tf_op jit(solution)/shard_map/pallas_call | solution.py:650
  49.6 1.3 %collective-permute-start.2 = (f32[1,64,512]{2,1,0:T(8,128)S(1)}, f32[1,64,512]{2,1,0:T(8,128)S(1)}, u32[]{:S(2)}, u32[]{:S(2)}) collective-permute-start(f32[1,64,512]{2,1,0:T(8,128)S(1)} %get-tuple-element.53), channel_id=1, source_target_pairs={{0,1},{1,0},{2,3},{3,2},{4,5},{5,4},{6,7},{7,6},{8,9},{9,8},{10,11... | collective-permute-start | bytes 393224 | tf_op jit(solution)/shard_map/ppermute | solution.py:668
  50.9 3.9 %collective-permute-start.3 = (f32[128,128]{1,0:T(8,128)S(1)}, f32[128,128]{1,0:T(8,128)S(1)}, u32[]{:S(2)}, u32[]{:S(2)}) collective-permute-start(f32[128,128]{1,0:T(8,128)S(1)} %get-tuple-element.46), channel_id=1, source_target_pairs={{2,4},{4,2},{6,8},{8,6},{10,12},{12,10},{14,16},{16,14},{18,20},{2... | collective-permute-start | bytes 196616 | tf_op jit(solution)/shard_map/ppermute | solution.py:570
  54.8 0.1 collective-permute-start.4
  54.9 3.1 %shard_map.142 = (f32[2,64,1024]{2,1,0:T(8,128)}, f32[2,64,1024]{2,1,0:T(8,128)}, f32[1024,128]{1,0:T(8,128)S(1)}) custom-call(f32[2208,128]{1,0:T(8,128)S(1)} %bitcast.8, f32[2048,128]{1,0:T(8,128)S(1)} %get-tuple-element.41.new_ref, f32[256,256]{1,0:T(8,128)S(1)} %get-tuple-element.42.acc0), custom_call_target="tpu_custom_call" | custom-call | flops 2000000 | bytes 2000000 | tf_op jit(solution)/shard_map/pallas_call | solution.py:670
  58.0 0.0 collective-permute-done.3.rest_2_
  58.0 0.0 collective-permute-done.4.rest_3_
  58.0 0.0 collective-permute-done.2.rest_1_
  58.0 1.1 %shard_map.143 = (f32[2,64,1024]{2,1,0:T(8,128)}, f32[2,64,1024]{2,1,0:T(8,128)}, f32[64,512]{1,0:T(8,128)}) custom-call(f32[2048,128]{1,0:T(8,128)S(1)} %get-tuple-element.38.base_ref, f32[512,128]{1,0:T(8,128)S(1)} %get-tuple-element.39.factor_ref, f32[2048,128]{1,0:T(8,128)S(1)} %get-tuple-element.40.next_ref, ...), custom_call_target="tpu_custom_call" | custom-call | flops 2000000 | bytes 2000000 | tf_op jit(solution)/shard_map/pallas_call | solution.py:680
  (1 shorter events, 0.0 us)
Async XLA Ops:
  5.7 33.3 %all-to-all-start = ((f32[16,69,2,128]{3,2,1,0:T(2,128)}), f32[16,69,2,128]{3,2,1,0:T(2,128)S(1)}, u32[]{:S(2)}, u32[]{:S(2)}) async-start(f32[16,69,2,128]{3,2,1,0:T(2,128)} %bitcast.3), calls=%async_computation | async-start | bytes 2260992 | tf_op jit(solution)/shard_map/all_to_all | solution.py:619
  40.7 7.0 %collective-permute-start = (f32[224,128]{1,0:T(8,128)S(1)}, f32[224,128]{1,0:T(8,128)S(1)}, u32[]{:S(2)}, u32[]{:S(2)}) collective-permute-start(f32[224,128]{1,0:T(8,128)S(1)} %get-tuple-element.36), channel_id=1, source_target_pairs={{2,4},{4,2},{6,8},{8,6},{10,12},{12,10},{14,16},{16,14},{18,20},{2... | collective-permute-start | bytes 344072 | tf_op jit(solution)/shard_map/ppermute | solution.py:570
  44.3 3.4 %collective-permute-start.1 = (f32[224,128]{1,0:T(8,128)S(1)}, f32[224,128]{1,0:T(8,128)S(1)}, u32[]{:S(2)}, u32[]{:S(2)}) collective-permute-start(f32[224,128]{1,0:T(8,128)S(1)} %get-tuple-element.37), channel_id=1, source_target_pairs={{0,2},{2,0},{4,6},{6,4},{8,10},{10,8},{12,14},{14,12},{16,18},{18,... | collective-permute-start | bytes 344072 | tf_op jit(solution)/shard_map/ppermute | solution.py:571
  49.6 8.4 %collective-permute-start.2 = (f32[1,64,512]{2,1,0:T(8,128)S(1)}, f32[1,64,512]{2,1,0:T(8,128)S(1)}, u32[]{:S(2)}, u32[]{:S(2)}) collective-permute-start(f32[1,64,512]{2,1,0:T(8,128)S(1)} %get-tuple-element.53), channel_id=1, source_target_pairs={{0,1},{1,0},{2,3},{3,2},{4,5},{5,4},{6,7},{7,6},{8,9},{9,8},{10,11... | collective-permute-start | bytes 393224 | tf_op jit(solution)/shard_map/ppermute | solution.py:668
  50.9 7.1 %collective-permute-start.3 = (f32[128,128]{1,0:T(8,128)S(1)}, f32[128,128]{1,0:T(8,128)S(1)}, u32[]{:S(2)}, u32[]{:S(2)}) collective-permute-start(f32[128,128]{1,0:T(8,128)S(1)} %get-tuple-element.46), channel_id=1, source_target_pairs={{2,4},{4,2},{6,8},{8,6},{10,12},{12,10},{14,16},{16,14},{18,20},{2... | collective-permute-start | bytes 196616 | tf_op jit(solution)/shard_map/ppermute | solution.py:570
  54.8 3.2 %collective-permute-start.4 = (f32[128,128]{1,0:T(8,128)S(1)}, f32[128,128]{1,0:T(8,128)S(1)}, u32[]{:S(2)}, u32[]{:S(2)}) collective-permute-start(f32[128,128]{1,0:T(8,128)S(1)} %get-tuple-element.47), channel_id=1, source_target_pairs={{0,2},{2,0},{4,6},{6,4},{8,10},{10,8},{12,14},{14,12},{16,18},{18,... | collective-permute-start | bytes 196616 | tf_op jit(solution)/shard_map/ppermute | solution.py:571
